TPU v7x, 32 devices: a whole 2x2x4 slice. The times are simulated.
32 devices in a mesh: tensor: 2 (over y), request: 16 (over z, x, core).
Axes of the slice: x: 2, y: 2, z: 4, core: 2. Of those that a mesh axis runs over, the one named last changes fastest.
Arguments:
- queries: bfloat16 [32, 16, 16384], P('request', None, 'tensor'), may hold values from -120 to 120
- cache_keys: bfloat16 [32, 256, 1024], P('request', None, 'tensor'), may hold values from -6 to 6
- cache_values: bfloat16 [32, 256, 1024], P('request', None, 'tensor'), may hold values from -6 to 6
- tree_keys: bfloat16 [32, 16, 1024], P('request', None, 'tensor'), may hold values from -6 to 6
- tree_values: bfloat16 [32, 16, 1024], P('request', None, 'tensor'), may hold values from -6 to 6
- cache_len: int32 [32], P('request'), may hold values from 64 to 256, as said below
- tree_parent: int32 [32, 16], P('request'), may hold values from 0 to 14, as said below
- residual: bfloat16 [32, 16, 16384], P('tensor', None, 'request'), may hold values from -6 to 6
- low_feats: bfloat16 [32, 16, 16384], P('tensor', None, 'request'), may hold values from -6 to 6
- mid_feats: bfloat16 [32, 16, 16384], P('tensor', None, 'request'), may hold values from -6 to 6
- out_proj: bfloat16 [16384, 16384], P('tensor', 'request'), may hold values from -1.25 to 1.25
- last_node: int32 [32], replicated, may hold values from 0 to 15
- draft_gain: float32 [16384], P('tensor'), may hold values from 0.1 to 1.9
- draft_join: bfloat16 [3, 16384, 16384], P(None, 'request', 'tensor'), may hold values from -0.24356964 to 0.24356964
Outputs:
- hidden: bfloat16 [32, 16, 16384], P('tensor', None, 'request')
- draft_features: bfloat16 [32, 16384], P('request', 'tensor')
Inputs may be any that keep to these rules, and one draw needn't show every extreme that they name: `cache_len`: every request has between 64 and 256 filled cache positions, and some request has exactly 256. tree_parent[b, 0] = 0 and tree_parent[b, i] < i for i >= 1.
All inputs are finite; a program needn't handle non-finite values.
Results may differ from a plain program's by a relative error of at most 0.0075.
Values may be sent and summed in bfloat16 or wider, within the bound.
No kernel may reach another device: no remote copies, remote signals or barrier semaphores. Data moves between devices by JAX's collectives and lax.ppermute only.
A program may use at most 128 MiB of HBM per device.

v0:
```python
import jax
import jax.numpy as jnp
from jax import lax
from jax.sharding import PartitionSpec as P

D = 16384
HEADS = 128
KV_HEADS = 8
HEAD = 128
TREE = 16


def ancestors(parents):
    nodes = jnp.arange(TREE, dtype=jnp.int32)
    step_matrix = (parents[:, None] == nodes[None, :]).astype(jnp.float32)
    reach = jnp.eye(TREE, dtype=jnp.float32)
    walker = reach
    for hop in range(TREE - 1):
        walker = jnp.dot(walker, step_matrix, precision=lax.Precision.HIGHEST)
        reach = jnp.maximum(reach, walker)
    return (reach > 0.5).astype(jnp.int32)


def verify_request(inputs):
    query_rows, keys_cache, values_cache, keys_tree, values_tree, length, parents = inputs
    kv_count = keys_cache.shape[-1] // HEAD
    group = HEADS // KV_HEADS
    factor = HEAD ** (-0.5)
    cache_rows = keys_cache.shape[0]
    query_heads = query_rows.reshape(TREE, kv_count, group, HEAD)
    cache_k = keys_cache.reshape(cache_rows, kv_count, HEAD)
    cache_v = values_cache.reshape(cache_rows, kv_count, HEAD)
    tree_k = keys_tree.reshape(TREE, kv_count, HEAD)
    tree_v = values_tree.reshape(TREE, kv_count, HEAD)
    score_cache = (
        jnp.einsum("tgqd,pgd->gqtp", query_heads, cache_k, preferred_element_type=jnp.float32)
        * factor
    )
    live = jnp.arange(cache_rows, dtype=jnp.int32) < length
    score_cache = jnp.where(live, score_cache, -1e30)
    score_tree = (
        jnp.einsum("tgqd,jgd->gqtj", query_heads, tree_k, preferred_element_type=jnp.float32)
        * factor
    )
    score_tree = jnp.where(ancestors(parents) == 1, score_tree, -1e30)
    top = jnp.maximum(jnp.max(score_cache, axis=-1), jnp.max(score_tree, axis=-1))
    exp_cache = jnp.exp(score_cache - top[..., None])
    exp_tree = jnp.exp(score_tree - top[..., None])
    total = jnp.sum(exp_cache, axis=-1) + jnp.sum(exp_tree, axis=-1)
    weight_cache = (exp_cache / total[..., None]).astype(jnp.bfloat16)
    weight_tree = (exp_tree / total[..., None]).astype(jnp.bfloat16)
    mixed = jnp.einsum("gqtp,pgd->tgqd", weight_cache, cache_v, preferred_element_type=jnp.float32)
    mixed = mixed + jnp.einsum(
        "gqtj,jgd->tgqd", weight_tree, tree_v, preferred_element_type=jnp.float32
    )
    return mixed.reshape(TREE, kv_count * group * HEAD).astype(jnp.bfloat16)


def body(
    queries,
    cache_keys,
    cache_values,
    tree_keys,
    tree_values,
    cache_len,
    tree_parent,
    residual,
    low_feats,
    mid_feats,
    out_proj,
    last_node,
    draft_gain,
    draft_join,
):
    heads_out = lax.map(
        verify_request,
        (queries, cache_keys, cache_values, tree_keys, tree_values, cache_len, tree_parent),
    )
    flat_rows = heads_out.reshape(-1, heads_out.shape[-1])
    partial_value = jnp.dot(
        lax.all_gather(flat_rows, "request", axis=0, tiled=True),
        out_proj,
        preferred_element_type=jnp.float32,
    )
    summed = lax.psum_scatter(partial_value, "tensor", scatter_dimension=0, tiled=True)
    local_req = residual.shape[0]
    columns = residual.shape[2]
    hidden = (residual.reshape(-1, columns).astype(jnp.float32) + summed).astype(jnp.bfloat16)
    hidden = hidden.reshape(residual.shape)
    all_req = last_node.shape[0]
    first_req = lax.axis_index("tensor") * local_req
    chosen_all = last_node[:, None] == jnp.arange(TREE, dtype=jnp.int32)[None, :]
    own_chosen = lax.dynamic_slice_in_dim(chosen_all, first_req, local_req, 0)

    def pick(rows):
        return jnp.sum(
            jnp.where(own_chosen[:, :, None], rows.astype(jnp.float32), 0.0), axis=1
        ).astype(jnp.bfloat16)

    low_rows, mid_rows, top_rows = (
        lax.all_gather(pick(low_feats), "tensor", axis=0, tiled=True),
        lax.all_gather(pick(mid_feats), "tensor", axis=0, tiled=True),
        lax.all_gather(pick(hidden), "tensor", axis=0, tiled=True),
    )
    stacked = jnp.stack((low_rows, mid_rows, top_rows), axis=1)
    joined_part = jnp.einsum("bsk,skn->bn", stacked, draft_join, preferred_element_type=jnp.float32)
    own_count = all_req // lax.axis_size("request")
    joined_total = lax.psum(joined_part, "request")
    joined = lax.dynamic_slice_in_dim(
        joined_total, lax.axis_index("request") * own_count, own_count, 0
    )
    squares = lax.psum(jnp.sum(joined * joined, axis=1), "tensor")
    row_scale = lax.rsqrt(squares / D + 1e-05)
    features = (joined * row_scale[:, None] * draft_gain[None, :]).astype(jnp.bfloat16)
    return (hidden, features)


def solution(mesh):
    return jax.shard_map(
        body,
        mesh=mesh,
        in_specs=(
            P("request", None, "tensor"),
            P("request", None, "tensor"),
            P("request", None, "tensor"),
            P("request", None, "tensor"),
            P("request", None, "tensor"),
            P("request"),
            P("request", None),
            P("tensor", None, "request"),
            P("tensor", None, "request"),
            P("tensor", None, "request"),
            P("tensor", "request"),
            P(),
            P("tensor"),
            P(None, "request", "tensor"),
        ),
        out_specs=(P("tensor", None, "request"), P("request", "tensor")),
        check_vma=False,
    )
```

profile of v0, /device:TPU:0, one launch (start us, length us, event | category | flops | bytes accessed | tf_op | source)
XLA Modules:
  0.0 300.3 jit_solution(8554122083734844641)
XLA Ops:
  7.2 23.9 %while.10 = (s32[]{:T(128)}, bf16[2,16,8192]{2,1,0:T(8,128)(2,1)S(1)}, bf16[2,256,512]{2,1,0:T(8,128)(2,1)}, s32[2]{0:T(128)}, bf16[2,256,512]{2,1,0:T(8,128)(2,...) while((s32[]{:T(128)}, ...), condition=%wide.region_5.6_spmd, body=%wide.region_0.5_spmd.sunk | while | flops 145800448 | bytes 11873489 | solution.py:75
  7.2 1.1 constant_dynamic-slice_fusion.7
  8.6 1.0 dynamic-slice_bitcast_fusion.2
  9.6 1.2 dynamic_slice.53
  10.9 0.6 iota_compare_fusion.53
  11.9 0.7 constant_dynamic-slice_fusion.8
  12.6 0.7 fusion.138
  16.3 0.8 fusion.154
  17.1 0.4 fusion.155
  19.2 1.1 constant_dynamic-slice_fusion.7
  20.6 1.0 dynamic-slice_bitcast_fusion.2
  21.6 1.2 dynamic_slice.53
  22.8 0.6 iota_compare_fusion.53
  23.5 0.4 fusion.137
  23.9 0.7 constant_dynamic-slice_fusion.8
  24.6 0.7 fusion.138
  28.3 0.8 fusion.154
  29.1 0.4 fusion.155
  31.2 0.8 copy-done.3
  32.1 77.6 %all-gather.2.cloned.1.call-done = bf16[512,8192]{1,0:T(8,128)(2,1)} async-done(((bf16[32,8192]{1,0:T(8,128)(2,1)}), bf16[512,8192]{1,0:T(8,128)(2,1)}) %all-gather.2.cloned.1.call-update) | async-done | bytes 8388624 | tf_op jit(solution)/shard_map/all_gather | solution.py:81
  109.7 15.8 %fusion.56 = f32[512,1024]{1,0:T(8,128)} fusion(bf16[512,8192]{1,0:T(8,128)(2,1)} %all-gather.2.cloned.1.call-done, bf16[8192,1024]{1,0:T(8,128)(2,1)} %param.26), kind=kOutput, calls=%fused_computation.83 | convolution fusion | flops 8589934592 | bytes 27262976 | tf_op jit(solution)/shard_map/dot_general | solution.py:80
  125.8 30.0 %reduce-scatter.2.cloned.1.call-done = f32[256,1024]{1,0:T(8,128)} async-done(((f32[512,1024]{1,0:T(8,128)}), f32[256,1024]{1,0:T(8,128)}) %reduce-scatter.2.cloned.1.call-update) | async-done | bytes 1048592 | tf_op jit(solution)/shard_map/reduce_scatter | solution.py:85
  155.8 1.4 fusion.47
  157.2 0.8 select_reduce_fusion.2
  158.1 4.6 %all_gather.15 = bf16[32,1024]{1,0:T(8,128)(2,1)S(1)} all-gather(bf16[16,1024]{1,0:T(8,128)(2,1)S(1)} %get-tuple-element.61), channel_id=1, replica_groups=mesh['tensor'=2,'request'=16] {'tensor'}, dimensions={0}, use_global_device_ids=true | all-gather | bytes 98304 | tf_op jit(solution)/shard_map/all_gather | solution.py:103
  162.6 4.6 %all_gather.14 = bf16[32,1024]{1,0:T(8,128)(2,1)S(1)} all-gather(bf16[16,1024]{1,0:T(8,128)(2,1)S(1)} %get-tuple-element.60), channel_id=1, replica_groups=mesh['tensor'=2,'request'=16] {'tensor'}, dimensions={0}, use_global_device_ids=true | all-gather | bytes 98304 | tf_op jit(solution)/shard_map/all_gather | solution.py:102
  167.2 4.6 %all_gather.13 = bf16[32,1024]{1,0:T(8,128)(2,1)S(1)} all-gather(bf16[16,1024]{1,0:T(8,128)(2,1)S(1)} %get-tuple-element.59), channel_id=1, replica_groups=mesh['tensor'=2,'request'=16] {'tensor'}, dimensions={0}, use_global_device_ids=true | all-gather | bytes 98304 | tf_op jit(solution)/shard_map/all_gather | solution.py:101
  171.8 20.8 %convolution_bitcast_fusion = f32[32,8192]{1,0:T(8,128)} fusion(bf16[3,1024,8192]{2,1,0:T(8,128)(2,1)} %param.29, bf16[32,1,1024]{2,0,1:T(8,128)(2,1)S(1)} %bitcast.121, bf16[32,1,1024]{2,0,1:T(8,128)(2,1)S(1)} %bitcast.122, bf16[32,1,1024]{2,0,1:T(8,128)(2,1)S(1)} %bitcast.123), kind=kOutput, calls=%fused_computation.65 | convolution fusion | flops 1610809344 | bytes 51576832 | tf_op jit(solution)/shard_map/bsk,skn->bn/dot_general | solution.py:106
  192.6 93.4 %all-reduce.2.cloned.1.call-done = f32[32,8192]{1,0:T(8,128)} async-done(((f32[32,8192]{1,0:T(8,128)}), f32[32,8192]{1,0:T(8,128)}) %all-reduce.2.cloned.1.call-update) | async-done | bytes 1048592 | tf_op jit(solution)/shard_map/psum | solution.py:108
  286.0 1.1 multiply_reduce_fusion
  287.1 4.9 %psum.15 = f32[2]{0:T(128)S(1)} all-reduce(f32[2]{0:T(128)S(1)} %multiply_reduce_fusion), channel_id=1, replica_groups=mesh['tensor'=2,'request'=16] {'tensor'}, use_global_device_ids=true, to_apply=%region_12.13 | all-reduce | flops 2 | bytes 16 | tf_op jit(solution)/shard_map/psum | solution.py:112
  292.1 1.7 multiply_convert_fusion
  (86 shorter events, 10.6 us)
Async XLA Ops:
  7.2 102.6 %all-gather.2.cloned.1.call-start = ((), (), s32[]{:S(2)}) async-start(), calls=%async_computation.1 | async-start | bytes 8912896 | tf_op jit(solution)/shard_map/all_gather | solution.py:81
  31.2 0.8 copy-start.3
  32.0 93.6 %copy-start.6 = (s32[32]{0:T(128)S(1)}, s32[32]{0:T(128)}, u32[]{:S(2)}) copy-start(s32[32]{0:T(128)} %param.27) | copy-start | bytes 388
  32.0 123.8 %copy-start.4 = (bf16[16,16,1024]{2,1,0:T(8,128)(2,1)S(1)}, bf16[16,16,1024]{2,1,0:T(8,128)(2,1)}, u32[]{:S(2)}) copy-start(bf16[16,16,1024]{2,1,0:T(8,128)(2,1)} %param.23) | copy-start | bytes 1572868
  32.0 125.2 %copy-start.1 = (bf16[16,16,1024]{2,1,0:T(8,128)(2,1)S(1)}, bf16[16,16,1024]{2,1,0:T(8,128)(2,1)}, u32[]{:S(2)}) copy-start(bf16[16,16,1024]{2,1,0:T(8,128)(2,1)} %param.24) | copy-start | bytes 1572868
  32.0 125.2 %copy-start.2 = (bf16[16,16,1024]{2,1,0:T(8,128)(2,1)S(1)}, bf16[16,16,1024]{2,1,0:T(8,128)(2,1)}, u32[]{:S(2)}) copy-start(bf16[16,16,1024]{2,1,0:T(8,128)(2,1)} %param.25) | copy-start | bytes 1572868
  32.0 123.8 %reduce-scatter.2.cloned.1.call-start = ((), (), s32[]{:S(2)}) async-start(), calls=%async_computation.2 | async-start | bytes 3145728 | tf_op jit(solution)/shard_map/reduce_scatter | solution.py:85
  125.6 160.4 %all-reduce.2.cloned.1.call-start = ((), (), s32[]{:S(2)}) async-start(), calls=%async_computation.3 | async-start | bytes 2097152 | tf_op jit(solution)/shard_map/psum | solution.py:108
  157.2 35.4 %copy-start = (bf16[256,1024]{1,0:T(8,128)(2,1)}, bf16[256,1024]{1,0:T(8,128)(2,1)S(1)}, u32[]{:S(2)}) copy-start(bf16[256,1024]{1,0:T(8,128)(2,1)S(1)} %fusion.47) | copy-start | bytes 1572868
  171.8 120.2 %copy-start.5 = (f32[8192]{0:T(1024)S(1)}, f32[8192]{0:T(1024)}, u32[]{:S(2)}) copy-start(f32[8192]{0:T(1024)} %param.28) | copy-start | bytes 98308
Sparse Core Ops, SparseCore 0:
  32.1 77.5 all-gather.1
  125.7 30.0 reduce-scatter.1
  192.7 93.1 all-reduce.1
where the time goes:
time: 301 us; the launch traced here: 300 us
  waiting for transfers between devices  201 us (67%)
  matrix products  45.8 us (15%)
  blocking collectives  18.7 us (6%)
  between operations  13.9 us (5%)
  local copies, waits for them, and re-layouts  12 us (4%)
  other arithmetic  8.41 us (3%)
    psum x1, waiting for transfers between devices, body(): joined_total = lax.psum(joined_part, 'request')  93.4 us
    all_gather x1, waiting for transfers between devices, body(): lax.all_gather(flat_rows, 'request', axis=0, tiled=True)  77.6 us
    reduce_scatter x1, waiting for transfers between devices, body(): lax.psum_scatter(partial_value, 'tensor', scatter_dimension=0, tiled=True)  30 us
    dot_general x1, matrix products, body(): jnp.einsum('bsk,skn->bn', stacked, draft_join, preferred_element_type=jnp...  20.8 us
    dot_general x1, matrix products, body(): jnp.dot(lax.all_gather(flat_rows, 'request', axis=0, tiled=True), out_pro...  15.8 us
    dynamic_slice x10, local copies, waits for them, and re-layouts, body(): lax.map(verify_request, (queries, cache_keys, cache_values, tree_keys, tr...  6.65 us
  transfers between devices with their start and end apart: 3, of which 3 were waited for; matrix products, arithmetic and copies ran while one was open for 0% of the time, Pallas kernels for 0%

commit v1 on v0

v1 whole, which is shorter than its diff:
```python
import functools

import jax
import jax.numpy as jnp
from jax import lax
from jax.experimental import pallas as pl
from jax.experimental.pallas import tpu as pltpu
from jax.sharding import PartitionSpec as P

D = 16384
HEADS = 128
KV_HEADS = 8
HEAD = 128
TREE = 16
GROUP = HEADS // KV_HEADS
FACTOR = HEAD ** (-0.5)
LIMIT = 44 * 1024 * 1024
BF = jnp.bfloat16
F32 = jnp.float32


def params(grid_dims=1):
    return pltpu.CompilerParams(
        vmem_limit_bytes=LIMIT, dimension_semantics=("arbitrary",) * grid_dims
    )


def attention_kernel(len_ref, last_ref, parent_ref, q_ref, ck_ref, cv_ref, tk_ref, tv_ref, o_ref, pick_ref, vis_ref):
    g, b = pl.program_id(0), pl.program_id(1)

    @pl.when(g == 0)
    def _():
        cols = lax.broadcasted_iota(jnp.int32, (TREE, TREE), 1)
        rows = lax.broadcasted_iota(jnp.int32, (TREE, TREE), 0)
        reach = jnp.where((parent_ref[0] == cols) | (rows == cols), 1.0, 0.0).astype(F32)
        for _ in range(4):
            half = reach.astype(BF)
            reach = jnp.minimum(jnp.dot(half, half, preferred_element_type=F32), 1.0)
        vis_ref[b] = reach

    q = q_ref[0]
    stacked = jnp.concatenate([q[:, h * HEAD : (h + 1) * HEAD] for h in range(GROUP)], axis=0)
    dims = (((1,), (1,)), ((), ()))
    s_cache = lax.dot_general(stacked, ck_ref[0], dims, preferred_element_type=F32) * FACTOR
    s_tree = lax.dot_general(stacked, tk_ref[0], dims, preferred_element_type=F32) * FACTOR
    live = lax.broadcasted_iota(jnp.int32, (1, s_cache.shape[1]), 1) < len_ref[b]
    s_cache = jnp.where(live, s_cache, -1e30)
    seen = jnp.concatenate([vis_ref[b]] * GROUP, axis=0) > 0.5
    s_tree = jnp.where(seen, s_tree, -1e30)
    top = jnp.maximum(
        jnp.max(s_cache, axis=1, keepdims=True), jnp.max(s_tree, axis=1, keepdims=True)
    )
    e_cache = jnp.exp(s_cache - top)
    e_tree = jnp.exp(s_tree - top)
    total = jnp.sum(e_cache, axis=1, keepdims=True) + jnp.sum(e_tree, axis=1, keepdims=True)
    inverse = 1.0 / total
    w_cache = (e_cache * inverse).astype(BF)
    w_tree = (e_tree * inverse).astype(BF)
    mixed = jnp.dot(w_cache, cv_ref[0], preferred_element_type=F32)
    mixed = mixed + jnp.dot(w_tree, tv_ref[0], preferred_element_type=F32)
    chosen = lax.broadcasted_iota(jnp.int32, (TREE, 1), 0) == last_ref[b]
    picks = []
    for h in range(GROUP):
        block = mixed[h * TREE : (h + 1) * TREE]
        o_ref[0, :, h * HEAD : (h + 1) * HEAD] = block.astype(BF)
        picks.append(jnp.sum(jnp.where(chosen, block, 0.0), axis=0, keepdims=True))
    row = jnp.concatenate(picks, axis=1)
    which = lax.broadcasted_iota(jnp.int32, pick_ref.shape, 0) == b
    pick_ref[...] = jnp.where(which, row, pick_ref[...].astype(F32)).astype(BF)


def attention(queries, ck, cv, tk, tv, lengths, parents, last):
    count, _, width = queries.shape
    cache = ck.shape[1]
    groups = ck.shape[2] // HEAD
    lanes = GROUP * HEAD
    smem = pl.BlockSpec(memory_space=pltpu.SMEM)
    wide = pl.BlockSpec((1, TREE, lanes), lambda g, b: (b, 0, g))
    long = pl.BlockSpec((1, cache, HEAD), lambda g, b: (b, 0, g))
    short = pl.BlockSpec((1, TREE, HEAD), lambda g, b: (b, 0, g))
    return pl.pallas_call(
        attention_kernel,
        grid=(groups, count),
        in_specs=[smem, smem, pl.BlockSpec((1, TREE, 1), lambda g, b: (b, 0, 0)), wide, long, long, short, short],
        out_specs=[wide, pl.BlockSpec((count, lanes), lambda g, b: (0, g))],
        out_shape=[
            jax.ShapeDtypeStruct(queries.shape, BF),
            jax.ShapeDtypeStruct((count, width), BF),
        ],
        scratch_shapes=[pltpu.VMEM((count, TREE, TREE), F32)],
        compiler_params=params(2),
        name="attention",
    )(lengths, last, parents[:, :, None], queries, ck, cv, tk, tv)


def pick_kernel(row_ref, low_ref, mid_ref, res_ref, feats_ref, res_out_ref):
    rows = low_ref.shape[0]
    count = row_ref.shape[0]
    hot = row_ref[...] == lax.broadcasted_iota(jnp.int32, (count, rows), 1)
    hot = jnp.where(hot, 1.0, 0.0).astype(BF)
    feats_ref[:count] = jnp.dot(hot, low_ref[...], preferred_element_type=F32).astype(BF)
    feats_ref[count:] = jnp.dot(hot, mid_ref[...], preferred_element_type=F32).astype(BF)
    res_out_ref[...] = jnp.dot(hot, res_ref[...], preferred_element_type=F32)


def pick(row_ids, low, mid, res):
    count, columns = row_ids.shape[0], low.shape[1]
    return pl.pallas_call(
        pick_kernel,
        out_shape=[
            jax.ShapeDtypeStruct((2 * count, columns), BF),
            jax.ShapeDtypeStruct((count, columns), F32),
        ],
        compiler_params=params(0),
        name="pick",
    )(row_ids, low, mid, res)


def project(name, blocks, weights, extras, finish, outs, step=1024):
    rows = sum(x.shape[0] for x in blocks)
    depth, columns = weights.shape
    steps = depth // step
    n = len(blocks)
    m = len(extras)

    def kernel(*refs):
        xs, w, more = refs[:n], refs[n], refs[n + 1 : n + 1 + m]
        results, total = refs[n + 1 + m : -1], refs[-1]
        k = pl.program_id(0)
        x = jnp.concatenate([r[...] for r in xs], axis=0)
        part = jnp.dot(x, w[...], preferred_element_type=F32)

        @pl.when(k == 0)
        def _():
            total[...] = part

        @pl.when(k > 0)
        def _():
            total[...] += part

        @pl.when(k == steps - 1)
        def _():
            finish(total, more, results)

    extra_specs, extra_args = [], []
    for extra in extras:
        array, spec = extra
        extra_args.append(array)
        extra_specs.append(spec)
    return pl.pallas_call(
        kernel,
        grid=(steps,),
        in_specs=[pl.BlockSpec((x.shape[0], step), lambda k: (0, k)) for x in blocks]
        + [pl.BlockSpec((step, columns), lambda k: (k, 0))]
        + extra_specs,
        out_specs=[pl.BlockSpec(o.shape, lambda k: (0, 0)) for o in outs],
        out_shape=outs,
        scratch_shapes=[pltpu.VMEM((rows, columns), F32)],
        compiler_params=params(1),
        cost_estimate=pl.CostEstimate(
            flops=2 * rows * depth * columns,
            bytes_accessed=2 * depth * columns + 2 * rows * depth,
            transcendentals=0,
        ),
        name=name,
    )(*blocks, weights, *extra_args)


def whole(array):
    return (array, pl.BlockSpec(array.shape, lambda k: (0,) * array.ndim))


def scalars(array):
    return (array, pl.BlockSpec(memory_space=pltpu.SMEM))


def join_features(own, other, join, step=512):
    count = own.shape[0] // 2
    depth, columns = join.shape[1:]

    def kernel(a_ref, b_ref, w_ref, o_ref):
        x = a_ref[...] + b_ref[...]
        o_ref[...] = jnp.dot(x[:count], w_ref[0], preferred_element_type=F32) + jnp.dot(
            x[count:], w_ref[1], preferred_element_type=F32
        )

    return pl.pallas_call(
        kernel,
        grid=(columns // step,),
        in_specs=[
            pl.BlockSpec(own.shape, lambda n: (0, 0)),
            pl.BlockSpec(own.shape, lambda n: (0, 0)),
            pl.BlockSpec((2, depth, step), lambda n: (0, 0, n)),
        ],
        out_specs=pl.BlockSpec((count, step), lambda n: (0, n)),
        out_shape=jax.ShapeDtypeStruct((count, columns), F32),
        compiler_params=params(1),
        cost_estimate=pl.CostEstimate(
            flops=4 * count * depth * columns,
            bytes_accessed=4 * depth * columns,
            transcendentals=0,
        ),
        name="join_features",
    )(own, other, join)


def join_hidden(own, other, before, join, step=1024):
    count = own.shape[0]
    depth, columns = join.shape[1:]
    half = count // 2

    def kernel(a_ref, b_ref, before_ref, w_ref, keep_ref, send_ref):
        x = (a_ref[...] + b_ref[...]).astype(BF)
        y = jnp.dot(x, w_ref[0], preferred_element_type=F32) + before_ref[...]
        keep_ref[...] = y[:half]
        send_ref[...] = y[half:].astype(BF)

    return pl.pallas_call(
        kernel,
        grid=(columns // step,),
        in_specs=[
            pl.BlockSpec(own.shape, lambda n: (0, 0)),
            pl.BlockSpec(own.shape, lambda n: (0, 0)),
            pl.BlockSpec((count, step), lambda n: (0, n)),
            pl.BlockSpec((1, depth, step), lambda n: (2, 0, n)),
        ],
        out_specs=[
            pl.BlockSpec((half, step), lambda n: (0, n)),
            pl.BlockSpec((half, step), lambda n: (0, n)),
        ],
        out_shape=[
            jax.ShapeDtypeStruct((half, columns), F32),
            jax.ShapeDtypeStruct((half, columns), BF),
        ],
        compiler_params=params(1),
        cost_estimate=pl.CostEstimate(
            flops=2 * count * depth * columns,
            bytes_accessed=2 * depth * columns + 6 * count * columns,
            transcendentals=0,
        ),
        name="join_hidden",
    )(own, other, before, join)


def finish_hidden(places, keep_b, got_b, keep_c, got_c, residual, rows):
    columns = residual.shape[1]
    n_b, n_c = keep_b.shape[0] // rows, keep_c.shape[0] // rows

    def kernel(place_ref, kb, gb, kc, gc, res, out):
        i = pl.program_id(0)

        @pl.when(i < n_b)
        def _():
            out[...] = (res[...].astype(F32) + (kb[...] + gb[...].astype(F32))).astype(BF)

        @pl.when(i >= n_b)
        def _():
            out[...] = (res[...].astype(F32) + (kc[...] + gc[...].astype(F32))).astype(BF)

    block = (rows, columns)
    early = lambda i, p: (jnp.minimum(i, n_b - 1), 0)
    late = lambda i, p: (jnp.maximum(i - n_b, 0), 0)
    moved = lambda i, p: (p[i], 0)
    return pl.pallas_call(
        kernel,
        grid_spec=pltpu.PrefetchScalarGridSpec(
            num_scalar_prefetch=1,
            grid=(n_b + n_c,),
            in_specs=[
                pl.BlockSpec(block, early),
                pl.BlockSpec(block, early),
                pl.BlockSpec(block, late),
                pl.BlockSpec(block, late),
                pl.BlockSpec(block, moved),
            ],
            out_specs=pl.BlockSpec(block, moved),
        ),
        out_shape=jax.ShapeDtypeStruct(residual.shape, BF),
        compiler_params=params(1),
        name="finish_hidden",
    )(places, keep_b, got_b, keep_c, got_c, residual)


CHIPS = 8


def chip_of(position):
    return (position, 0) if position < 4 else (7 - position, 1)


def device_of(position, core):
    z, x = chip_of(position % CHIPS)
    return (z * 2 + x) * 2 + core


def ring_body(
    queries,
    cache_keys,
    cache_values,
    tree_keys,
    tree_values,
    cache_len,
    tree_parent,
    residual,
    low_feats,
    mid_feats,
    out_proj,
    last_node,
    draft_gain,
    draft_join,
):
    request = lax.axis_index("request")
    side = lax.axis_index("tensor")
    size = lax.axis_size("request")
    own_count = queries.shape[0]
    columns = residual.shape[2]
    all_req = last_node.shape[0]
    side_rows = residual.shape[0] * TREE
    block_rows = own_count * TREE

    forward = [(device_of(p, c), device_of(p + 1, c)) for p in range(CHIPS) for c in range(2)]
    backward = [(b, a) for a, b in forward]
    ahead = lambda v: lax.ppermute(v, "request", forward)
    back = lambda v: lax.ppermute(v, "request", backward)
    swap_core = lambda v: lax.ppermute(v, "request", [(r, r ^ 1) for r in range(size)])
    swap_x = lambda v: lax.ppermute(v, "request", [(r, r ^ 2) for r in range(size)])
    shift_z = lambda v, k: lax.ppermute(v, "request", [(r, (r + 4 * k) % size) for r in range(size)])
    swap_side = lambda v: lax.ppermute(v, "tensor", [(0, 1), (1, 0)])

    core, x, z = request % 2, (request // 2) % 2, request // 4
    position = jnp.where(x == 0, z, 7 - z)
    pairs = jnp.array([-1, 1, -2, 0], jnp.int32)
    first = (position + pairs + CHIPS) % CHIPS
    first_side = ((first + 2) // 4) % 2
    flags = (first_side == side).astype(jnp.int32)
    kept = jnp.where(flags == 1, first, (first + 4) % CHIPS)
    kept_chip = jnp.where(kept < 4, kept * 2, (7 - kept) * 2 + 1)
    kept_device = kept_chip[:, None] * 2 + jnp.stack([core, 1 - core])[None, :]
    places = (kept_device - side * (size // 2)).reshape(-1).astype(jnp.int32)

    order = jnp.arange(all_req, dtype=jnp.int32)
    rel_core, rel_x, rel_z, within = order // 16, (order // 8) % 2, (order // 2) % 4, order % 2
    of_z, of_x, of_core = (z - rel_z + 4) % 4, (x + rel_x) % 2, (core + rel_core) % 2
    req = ((of_z * 2 + of_x) * 2 + of_core) * own_count + within
    last_rel = jnp.sum(jnp.where(req[:, None] == order[None, :], last_node[None, :], 0), axis=1)
    row_ids = (req * TREE + last_rel - side * side_rows)[:, None]
    own_last = lax.dynamic_slice_in_dim(last_node, request * own_count, own_count, 0)

    feats, res_rows = pick(
        row_ids,
        low_feats.reshape(-1, columns),
        mid_feats.reshape(-1, columns),
        residual.reshape(-1, columns),
    )
    feats_other = swap_side(feats)

    heads, picked = attention(
        queries, cache_keys, cache_values, tree_keys, tree_values, cache_len, tree_parent, own_last
    )
    h = heads.reshape(block_rows, -1)

    by_z = jnp.concatenate([picked] + [shift_z(picked, k) for k in range(1, 4)], axis=0)
    by_x = jnp.concatenate([by_z, swap_x(by_z)], axis=0)

    f1, b1 = ahead(h), back(h)
    hs = swap_core(h)
    picked_other = swap_core(by_x)

    joined_feats = join_features(feats, feats_other, draft_join)

    f2, b2 = ahead(f1), back(b1)
    f1s, b1s = swap_core(f1), swap_core(b1)

    def finish_a(total, more, results):
        results[0][...] = total[: 6 * block_rows]
        results[1][...] = total[6 * block_rows :] + more[0][...]

    part_a, part_picked = project(
        "project_a",
        [h, hs, f1, f1s, b1, b1s, by_x, picked_other],
        out_proj,
        [whole(res_rows)],
        finish_a,
        [
            jax.ShapeDtypeStruct((6 * block_rows, columns), F32),
            jax.ShapeDtypeStruct((all_req, columns), F32),
        ],
    )
    part_other = swap_side(part_picked)

    f3, b3 = ahead(f2), back(b2)
    f2s, b2s = swap_core(f2), swap_core(b2)

    keep16, send16 = join_hidden(part_picked, part_other, joined_feats, draft_join)
    got16 = swap_core(send16)

    f4, b4 = ahead(f3[:TREE]), back(b3[TREE:])
    f3s, b3s = swap_core(f3), swap_core(b3)

    two = 2 * block_rows

    def finish_b(total, more, results):
        flag, before = more
        keep, send = results
        early = [before[two : 2 * two], before[2 * two : 3 * two]]
        late = [total[i * two : (i + 1) * two] for i in range(4)]
        for i, (u, v) in enumerate([(early[0], late[3]), (early[1], late[2]), (late[0], late[1])]):
            mine = flag[i] == 1
            keep[i * two : (i + 1) * two] = jnp.where(mine, u, v)
            send[i * two : (i + 1) * two] = jnp.where(mine, v, u).astype(BF)

    keep_b, send_b = project(
        "project_b",
        [f2, f2s, b2, b2s, f3, f3s, b3, b3s],
        out_proj,
        [scalars(flags), whole(part_a)],
        finish_b,
        [
            jax.ShapeDtypeStruct((3 * two, columns), F32),
            jax.ShapeDtypeStruct((3 * two, columns), BF),
        ],
    )
    got_b = swap_side(send_b)

    f4s, b4s = swap_core(f4), swap_core(b4)

    def finish_c(total, more, results):
        flag, before = more
        keep, send = results
        mine = flag[3] == 1
        u, v = before[...], total[...]
        keep[...] = jnp.where(mine, u, v)
        send[...] = jnp.where(mine, v, u).astype(BF)

    keep_c, send_c = project(
        "project_c",
        [f4, b4, f4s, b4s],
        out_proj,
        [scalars(flags), (part_a, pl.BlockSpec((two, columns), lambda k: (0, 0)))],
        finish_c,
        [
            jax.ShapeDtypeStruct((two, columns), F32),
            jax.ShapeDtypeStruct((two, columns), BF),
        ],
    )
    got_c = swap_side(send_c)

    hidden = finish_hidden(
        places, keep_b, got_b, keep_c, got_c, residual.reshape(-1, columns), block_rows
    ).reshape(residual.shape)

    sum16 = keep16 + got16.astype(F32)
    sum8 = sum16[:8] + swap_x(sum16[8:].astype(BF)).astype(F32)
    joined = sum8[:own_count]
    for k in range(1, 4):
        send = sum8[k * own_count : (k + 1) * own_count].astype(BF)
        joined = joined + shift_z(send, 4 - k).astype(F32)
    squares = jnp.sum(joined * joined, axis=1, keepdims=True)
    squares = squares + swap_side(squares)
    row_scale = lax.rsqrt(squares / D + 1e-05)
    features = (joined * row_scale * draft_gain[None, :]).astype(BF)
    return (hidden, features)


def any_body(
    queries,
    cache_keys,
    cache_values,
    tree_keys,
    tree_values,
    cache_len,
    tree_parent,
    residual,
    low_feats,
    mid_feats,
    out_proj,
    last_node,
    draft_gain,
    draft_join,
):
    own_count = queries.shape[0]
    first_own = lax.axis_index("request") * own_count
    own_last = lax.dynamic_slice_in_dim(last_node, first_own, own_count, 0)
    heads, _ = attention(
        queries, cache_keys, cache_values, tree_keys, tree_values, cache_len, tree_parent, own_last
    )
    flat_rows = heads.reshape(-1, heads.shape[-1])
    partial_value = jnp.dot(
        lax.all_gather(flat_rows, "request", axis=0, tiled=True),
        out_proj,
        preferred_element_type=F32,
    )
    summed = lax.psum_scatter(partial_value, "tensor", scatter_dimension=0, tiled=True)
    local_req = residual.shape[0]
    columns = residual.shape[2]
    hidden = (residual.reshape(-1, columns).astype(F32) + summed).astype(BF)
    hidden = hidden.reshape(residual.shape)
    first_req = lax.axis_index("tensor") * local_req
    chosen_all = last_node[:, None] == jnp.arange(TREE, dtype=jnp.int32)[None, :]
    own_chosen = lax.dynamic_slice_in_dim(chosen_all, first_req, local_req, 0)

    def choose(rows):
        return jnp.sum(jnp.where(own_chosen[:, :, None], rows.astype(F32), 0.0), axis=1).astype(BF)

    rows = jnp.stack((choose(low_feats), choose(mid_feats), choose(hidden)), axis=1)
    stacked = lax.all_gather(rows, "tensor", axis=0, tiled=True)
    joined_part = jnp.einsum("bsk,skn->bn", stacked, draft_join, preferred_element_type=F32)
    joined = lax.psum_scatter(joined_part, "request", scatter_dimension=0, tiled=True)
    squares = lax.psum(jnp.sum(joined * joined, axis=1), "tensor")
    row_scale = lax.rsqrt(squares / D + 1e-05)
    features = (joined * row_scale[:, None] * draft_gain[None, :]).astype(BF)
    return (hidden, features)


def solution(mesh):
    small = mesh.shape["tensor"] == 2 and mesh.shape["request"] == 2 * CHIPS
    return jax.shard_map(
        ring_body if small else any_body,
        mesh=mesh,
        in_specs=(
            P("request", None, "tensor"),
            P("request", None, "tensor"),
            P("request", None, "tensor"),
            P("request", None, "tensor"),
            P("request", None, "tensor"),
            P("request"),
            P("request", None),
            P("tensor", None, "request"),
            P("tensor", None, "request"),
            P("tensor", None, "request"),
            P("tensor", "request"),
            P(),
            P("tensor"),
            P(None, "request", "tensor"),
        ),
        out_specs=(P("tensor", None, "request"), P("request", "tensor")),
        check_vma=False,
    )
```

time: 301 us -> 169 us (0.56)
  waiting for transfers between devices: 201 us -> 47.4 us
  Pallas kernels: 0 us -> 71.9 us
  matrix products: 45.8 us -> 0 us
  starting transfers between devices: 0.12 us -> 27.1 us
  blocking collectives: 18.7 us -> 0 us
  between operations: 13.9 us -> 0.83 us
    psum x1 -> x0, waiting for transfers between devices: 93.4 us -> none  [body(): joined_total = lax.psum(joined_part, 'request')]
    all_gather x1 -> x0, waiting for transfers between devices: 77.6 us -> none  [body(): lax.all_gather(flat_rows, 'request', axis=0, tiled=True)]
    pallas_call x0 -> x8, Pallas kernels: none -> 71.9 us  [the longest x3 32.5 us: project(): pl.pallas_call(kernel, grid=(steps,), in_specs=[pl.BlockSpec((x.shape[0],...]
    ppermute x0 -> x32, waiting for transfers between devices: none -> 47.4 us  [the longest x4 15.2 us: ring_body(): back = lambda v: lax.ppermute(v, 'request', backward)]
    dot_general x40 -> x0, matrix products: 45.8 us -> none  [the longest x1 20.8 us: body(): jnp.einsum('bsk,skn->bn', stacked, draft_join, preferred_element_type=jnp...]
    reduce_scatter x1 -> x0, waiting for transfers between devices: 30 us -> none  [body(): lax.psum_scatter(partial_value, 'tensor', scatter_dimension=0, tiled=True)]
    ppermute x0 -> x32, starting transfers between devices: none -> 27.1 us  [the longest x6 7.99 us: ring_body(): lax.ppermute(v, 'request', [(r, (r + 4 * k) % size) for r in range(size)])]
    all_gather x3 -> x0, blocking collectives: 13.7 us -> none  [the longest x1 4.59 us: body(): lax.all_gather(pick(hidden), 'tensor', axis=0, tiled=True)]
  transfers between devices with their start and end apart: 3 -> 32, of which waited for: 3 -> 8; matrix products, arithmetic and copies ran while one was open for 0% -> 5% of each run, Pallas kernels for 0% -> 36%
where the time goes in v1:
time: 169 us; the launch traced here: 168 us
  Pallas kernels  71.9 us (43%)
  waiting for transfers between devices  47.4 us (28%)
  starting transfers between devices  27.1 us (16%)
  local copies, waits for them, and re-layouts  15 us (9%)
  other arithmetic  5.79 us (3%)
    pallas_call x3, Pallas kernels, project(): pl.pallas_call(kernel, grid=(steps,), in_specs=[pl.BlockSpec((x.shape[0],...  32.5 us
    pallas_call x1, Pallas kernels, join_features(): pl.pallas_call(kernel, grid=(columns // step,), in_specs=[pl.BlockSpec(ow...  18.3 us
    ppermute x4, waiting for transfers between devices, ring_body(): back = lambda v: lax.ppermute(v, 'request', backward)  15.2 us
    unnamed x30, local copies, waits for them, and re-layouts  11.7 us
    ppermute x5, waiting for transfers between devices, ring_body(): swap_side = lambda v: lax.ppermute(v, 'tensor', [(0, 1), (1, 0)])  10.9 us
    ppermute x6, waiting for transfers between devices, ring_body(): lax.ppermute(v, 'request', [(r, (r + 4 * k) % size) for r in range(size)])  10.9 us
    pallas_call x1, Pallas kernels, join_hidden(): pl.pallas_call(kernel, grid=(columns // step,), in_specs=[pl.BlockSpec(ow...  10.1 us
    ppermute x2, waiting for transfers between devices, ring_body(): lax.ppermute(v, 'request', [(r, r ^ 2) for r in range(size)])  7.99 us
  transfers between devices with their start and end apart: 32, of which 8 were waited for; matrix products, arithmetic and copies ran while one was open for 5% of the time, Pallas kernels for 36%

profile of v1, /device:TPU:0, one launch (start us, length us, event | category | flops | bytes accessed | tf_op | source)
XLA Modules:
  0.0 168.0 jit_solution(16999270859663613835)
XLA Ops:
  2.1 1.0 copy-done.7
  3.2 1.0 copy-done.8
  7.4 7.4 %attention.1 = (bf16[2,16,8192]{2,1,0:T(8,128)(2,1)S(1)}, bf16[2,8192]{1,0:T(2,128)(2,1)S(1)}) custom-call(s32[2]{0:T(128)S(1)} %copy-done.12, s32[2]{0:T(128)S(1)} %dynamic_slice.3.last_ref, s32[2,16,1]{2,1,0:T(8,128)S(1)} %copy.23.parent_ref, bf16[2,16,8192]{2,1,0:T(8,128)(2,1)S(1)} %copy-done.7, bf16[2,256,512]{2,1,0:T(8,128)(2,1)S(1)} %copy-done.8, ...), custom_call_target="tpu_custom_call" | custom-call | tf_op jit(solution)/shard_map/attention/pallas_call | solution.py:81
  14.8 3.1 %collective-permute-start = (bf16[32,8192]{1,0:T(8,128)(2,1)S(1)}, bf16[32,8192]{1,0:T(8,128)(2,1)S(1)}, u32[]{:S(2)}, u32[]{:S(2)}) collective-permute-start(bf16[32,8192]{1,0:T(8,128)(2,1)S(1)} %bitcast.17), channel_id=1, source_target_pairs={{0,4},{1,5},{4,8},{5,9},{8,12},{9,13},{12,14},{13,15},{14,10},{15,... | collective-permute-start | bytes 1572872 | tf_op jit(solution)/shard_map/ppermute | solution.py:323
  17.9 2.0 %collective-permute-start.13 = (bf16[2,8192]{1,0:T(2,128)(2,1)S(1)}, bf16[2,8192]{1,0:T(2,128)(2,1)S(1)}, u32[]{:S(2)}, u32[]{:S(2)}) collective-permute-start(bf16[2,8192]{1,0:T(2,128)(2,1)S(1)} %get-tuple-element.15), channel_id=1, source_target_pairs={{0,4},{1,5},{2,6},{3,7},{4,8},{5,9},{6,10},{7,11},{8,12},{9,13},{1... | collective-permute-start | bytes 98312 | tf_op jit(solution)/shard_map/ppermute | solution.py:327
  19.9 2.6 %collective-permute-start.14 = (bf16[2,8192]{1,0:T(2,128)(2,1)S(1)}, bf16[2,8192]{1,0:T(2,128)(2,1)S(1)}, u32[]{:S(2)}, u32[]{:S(2)}) collective-permute-start(bf16[2,8192]{1,0:T(2,128)(2,1)S(1)} %get-tuple-element.15), channel_id=1, source_target_pairs={{0,8},{1,9},{2,10},{3,11},{4,12},{5,13},{6,14},{7,15},{8,0},{9,1},... | collective-permute-start | bytes 98312 | tf_op jit(solution)/shard_map/ppermute | solution.py:327
  22.5 1.3 collective-permute-start.15
  23.9 10.9 %collective-permute-done.13 = bf16[2,8192]{1,0:T(2,128)(2,1)S(1)} collective-permute-done((bf16[2,8192]{1,0:T(2,128)(2,1)S(1)}, bf16[2,8192]{1,0:T(2,128)(2,1)S(1)}, u32[]{:S(2)}, u32[]{:S(2)}) %collective-permute-start.13) | collective-permute-done | bytes 32800 | tf_op jit(solution)/shard_map/ppermute | solution.py:327
  35.8 5.6 %collective-permute-done.16 = bf16[8,8192]{1,0:T(8,128)(2,1)S(1)} collective-permute-done((bf16[8,8192]{1,0:T(8,128)(2,1)S(1)}, bf16[8,8192]{1,0:T(8,128)(2,1)S(1)}, u32[]{:S(2)}, u32[]{:S(2)}) %collective-permute-start.16) | collective-permute-done | bytes 131104 | tf_op jit(solution)/shard_map/ppermute | solution.py:326
  46.2 1.6 collective-permute-start.25
  49.6 10.9 %project_a.1 = (f32[192,1024]{1,0:T(8,128)S(1)}, f32[32,1024]{1,0:T(8,128)S(1)}) custom-call(bf16[32,8192]{1,0:T(8,128)(2,1)S(1)} %bitcast.20, bf16[32,8192]{1,0:T(8,128)(2,1)S(1)} %copy-done.5, bf16[32,8192]{1,0:T(8,128)(2,1)S(1)} %collective-permute-done.refs_2_, bf16[32,8192]{1,0:T(8,128)(2,1)} %collective-permute-done.11.refs_3_, ...), custom_call_target="tpu_custom_call" | custom-call | flops 3758096384 | bytes 20447232 | tf_op jit(solution)/shard_map/project_a/pallas_call | solution.py:150
  61.2 18.3 %join_features.1.before_ref = f32[32,8192]{1,0:T(8,128)S(1)} custom-call(bf16[64,1024]{1,0:T(8,128)(2,1)S(1)} %get-tuple-element.23.a_ref, bf16[64,1024]{1,0:T(8,128)(2,1)S(1)} %collective-permute-done.25.b_ref, bf16[3,1024,8192]{2,1,0:T(8,128)(2,1)} %w_ref.3), custom_call_target="tpu_custom_call" | custom-call | flops 1073741824 | bytes 33554432 | tf_op jit(solution)/shard_map/join_features/pallas_call | solution.py:187
  79.5 10.1 %join_hidden.1 = (f32[16,8192]{1,0:T(8,128)S(1)}, bf16[16,8192]{1,0:T(8,128)(2,1)}) custom-call(f32[32,1024]{1,0:T(8,128)S(1)} %get-tuple-element.22.a_ref, f32[32,1024]{1,0:T(8,128)S(1)} %collective-permute-done.24.b_ref, f32[32,8192]{1,0:T(8,128)S(1)} %join_features.1.before_ref, bf16[3,1024,8192]{2,1,0:T(8,128)(2,1)} %w_ref.3), custom_call_target="tpu_custom_call" | custom-call | flops 536870912 | bytes 18350080 | tf_op jit(solution)/shard_map/join_hidden/pallas_call | solution.py:218
  90.4 2.0 %collective-permute-start.4 = (bf16[32,8192]{1,0:T(8,128)(2,1)S(1)}, bf16[32,8192]{1,0:T(8,128)(2,1)S(1)}, u32[]{:S(2)}, u32[]{:S(2)}) collective-permute-start(bf16[32,8192]{1,0:T(8,128)(2,1)S(1)} %collective-permute-done.3.refs_4_), channel_id=1, source_target_pairs={{4,0},{5,1},{8,4},{9,5},{12,8},{13,9},{14,12},{15,13},{10,14},{11,... | collective-permute-start | bytes 1572872 | tf_op jit(solution)/shard_map/ppermute | solution.py:324
  92.4 1.2 convert_add_fusion
  93.6 2.1 %collective-permute-start.27 = (bf16[8,8192]{1,0:T(8,128)(2,1)S(1)}, bf16[8,8192]{1,0:T(8,128)(2,1)S(1)}, u32[]{:S(2)}, u32[]{:S(2)}) collective-permute-start(bf16[8,8192]{1,0:T(8,128)(2,1)S(1)} %slice.51), channel_id=1, source_target_pairs={{0,2},{1,3},{2,0},{3,1},{4,6},{5,7},{6,4},{7,5},{8,10},{9,11},{10,... | collective-permute-start | bytes 393224 | tf_op jit(solution)/shard_map/ppermute | solution.py:326
  95.7 9.0 %collective-permute-done.4.refs_2_ = bf16[32,8192]{1,0:T(8,128)(2,1)S(1)} collective-permute-done((bf16[32,8192]{1,0:T(8,128)(2,1)S(1)}, bf16[32,8192]{1,0:T(8,128)(2,1)S(1)}, u32[]{:S(2)}, u32[]{:S(2)}) %collective-permute-start.4) | collective-permute-done | bytes 524320 | tf_op jit(solution)/shard_map/ppermute | solution.py:324
  104.7 2.4 %collective-permute-start.8 = (bf16[32,8192]{1,0:T(8,128)(2,1)S(1)}, bf16[32,8192]{1,0:T(8,128)(2,1)S(1)}, u32[]{:S(2)}, u32[]{:S(2)}) collective-permute-start(bf16[32,8192]{1,0:T(8,128)(2,1)S(1)} %collective-permute-done.4.refs_2_), channel_id=1, source_target_pairs={{4,0},{5,1},{8,4},{9,5},{12,8},{13,9},{14,12},{15,13},{10,14},{11,... | collective-permute-start | bytes 1572872 | tf_op jit(solution)/shard_map/ppermute | solution.py:324
  107.2 2.4 %collective-permute-done.27 = bf16[8,8192]{1,0:T(8,128)(2,1)S(1)} collective-permute-done((bf16[8,8192]{1,0:T(8,128)(2,1)S(1)}, bf16[8,8192]{1,0:T(8,128)(2,1)S(1)}, u32[]{:S(2)}, u32[]{:S(2)}) %collective-permute-start.27) | collective-permute-done | bytes 131104 | tf_op jit(solution)/shard_map/ppermute | solution.py:326
  111.2 1.8 %collective-permute-start.30 = (bf16[2,8192]{1,0:T(2,128)(2,1)S(1)}, bf16[2,8192]{1,0:T(2,128)(2,1)S(1)}, u32[]{:S(2)}, u32[]{:S(2)}) collective-permute-start(bf16[2,8192]{1,0:T(2,128)(2,1)S(1)} %get-tuple-element.33), channel_id=1, source_target_pairs={{0,4},{1,5},{2,6},{3,7},{4,8},{5,9},{6,10},{7,11},{8,12},{9,13},{1... | collective-permute-start | bytes 98312 | tf_op jit(solution)/shard_map/ppermute | solution.py:327
  113.1 6.2 %collective-permute-done.8.refs_6_ = bf16[32,8192]{1,0:T(8,128)(2,1)S(1)} collective-permute-done((bf16[32,8192]{1,0:T(8,128)(2,1)S(1)}, bf16[32,8192]{1,0:T(8,128)(2,1)S(1)}, u32[]{:S(2)}, u32[]{:S(2)}) %collective-permute-start.8) | collective-permute-done | bytes 524320 | tf_op jit(solution)/shard_map/ppermute | solution.py:324
  120.0 1.5 collective-permute-start.20
  122.8 1.2 multiply_reduce_fusion
  124.0 1.6 collective-permute-start.31
  125.6 2.0 %collective-permute-done.31 = f32[2,1]{0,1:T(1,128)S(1)} collective-permute-done((f32[2,1]{0,1:T(1,128)S(1)}, f32[2,1]{0,1:T(1,128)S(1)}, u32[]{:S(2)}, u32[]{:S(2)}) %collective-permute-start.31) | collective-permute-done | bytes 40 | tf_op jit(solution)/shard_map/ppermute | solution.py:328
  128.3 2.2 %collective-permute-done.22.refs_3_ = bf16[16,8192]{1,0:T(8,128)(2,1)} collective-permute-done((bf16[16,8192]{1,0:T(8,128)(2,1)}, bf16[16,8192]{1,0:T(8,128)(2,1)}, u32[]{:S(2)}, u32[]{:S(2)}) %collective-permute-start.22) | collective-permute-done | bytes 262176 | tf_op jit(solution)/shard_map/ppermute | solution.py:325
  130.6 10.0 %project_c.1 = (f32[64,1024]{1,0:T(8,128)S(1)}, bf16[64,1024]{1,0:T(8,128)(2,1)S(1)}) custom-call(bf16[16,8192]{1,0:T(8,128)(2,1)} %collective-permute-done.19.refs_0_, bf16[16,8192]{1,0:T(8,128)(2,1)} %collective-permute-done.20.refs_1_, bf16[16,8192]{1,0:T(8,128)(2,1)} %collective-permute-done.21.refs_2_, ...), custom_call_target="tpu_custom_call" | custom-call | flops 1073741824 | bytes 17825792 | tf_op jit(solution)/shard_map/project_c/pallas_call | solution.py:150
  140.6 1.6 collective-permute-start.23
  142.2 11.6 %project_b.1 = (f32[192,1024]{1,0:T(8,128)S(1)}, bf16[192,1024]{1,0:T(8,128)(2,1)S(1)}) custom-call(bf16[32,8192]{1,0:T(8,128)(2,1)S(1)} %collective-permute-done.1.refs_0_, bf16[32,8192]{1,0:T(8,128)(2,1)} %collective-permute-done.2.refs_1_, bf16[32,8192]{1,0:T(8,128)(2,1)S(1)} %collective-permute-done.4.refs_2_, ...), custom_call_target="tpu_custom_call" | custom-call | flops 4294967296 | bytes 20971520 | tf_op jit(solution)/shard_map/project_b/pallas_call | solution.py:150
  154.3 1.5 multiply_convert_fusion
  155.8 8.9 %collective-permute-done.18.gb = bf16[192,1024]{1,0:T(8,128)(2,1)S(1)} collective-permute-done((bf16[192,1024]{1,0:T(8,128)(2,1)S(1)}, bf16[192,1024]{1,0:T(8,128)(2,1)S(1)}, u32[]{:S(2)}, u32[]{:S(2)}) %collective-permute-start.18) | collective-permute-done | bytes 393248 | tf_op jit(solution)/shard_map/ppermute | solution.py:328
  164.7 3.3 %finish_hidden.1 = bf16[256,1024]{1,0:T(8,128)(2,1)} custom-call(s32[8]{0:T(128)S(1)} %sub.91.place_ref, f32[192,1024]{1,0:T(8,128)S(1)} %get-tuple-element.18.kb, bf16[192,1024]{1,0:T(8,128)(2,1)S(1)} %collective-permute-done.18.gb, f32[64,1024]{1,0:T(8,128)S(1)} %get-tuple-element.20.kc, bf16[64,1024]{1,0:T(8,128)(2,1)S(1)} %collective-permute-done.23.gc, ...), custom_call_target="tpu_custom_call" | custom-call | tf_op jit(solution)/shard_map/finish_hidden/pallas_call | solution.py:264
  (91 shorter events, 18.9 us)
Async XLA Ops:
  14.8 19.9 %collective-permute-start = (bf16[32,8192]{1,0:T(8,128)(2,1)S(1)}, bf16[32,8192]{1,0:T(8,128)(2,1)S(1)}, u32[]{:S(2)}, u32[]{:S(2)}) collective-permute-start(bf16[32,8192]{1,0:T(8,128)(2,1)S(1)} %bitcast.17), channel_id=1, source_target_pairs={{0,4},{1,5},{4,8},{5,9},{8,12},{9,13},{12,14},{13,15},{14,10},{15,... | collective-permute-start | bytes 1572872 | tf_op jit(solution)/shard_map/ppermute | solution.py:323
  17.9 17.4 %collective-permute-start.3 = (bf16[32,8192]{1,0:T(8,128)(2,1)S(1)}, bf16[32,8192]{1,0:T(8,128)(2,1)S(1)}, u32[]{:S(2)}, u32[]{:S(2)}) collective-permute-start(bf16[32,8192]{1,0:T(8,128)(2,1)S(1)} %bitcast.18), channel_id=1, source_target_pairs={{4,0},{5,1},{8,4},{9,5},{12,8},{13,9},{14,12},{15,13},{10,14},{11,... | collective-permute-start | bytes 1572872 | tf_op jit(solution)/shard_map/ppermute | solution.py:324
  17.9 16.9 %collective-permute-start.13 = (bf16[2,8192]{1,0:T(2,128)(2,1)S(1)}, bf16[2,8192]{1,0:T(2,128)(2,1)S(1)}, u32[]{:S(2)}, u32[]{:S(2)}) collective-permute-start(bf16[2,8192]{1,0:T(2,128)(2,1)S(1)} %get-tuple-element.15), channel_id=1, source_target_pairs={{0,4},{1,5},{2,6},{3,7},{4,8},{5,9},{6,10},{7,11},{8,12},{9,13},{1... | collective-permute-start | bytes 98312 | tf_op jit(solution)/shard_map/ppermute | solution.py:327
  19.9 15.4 %collective-permute-start.14 = (bf16[2,8192]{1,0:T(2,128)(2,1)S(1)}, bf16[2,8192]{1,0:T(2,128)(2,1)S(1)}, u32[]{:S(2)}, u32[]{:S(2)}) collective-permute-start(bf16[2,8192]{1,0:T(2,128)(2,1)S(1)} %get-tuple-element.15), channel_id=1, source_target_pairs={{0,8},{1,9},{2,10},{3,11},{4,12},{5,13},{6,14},{7,15},{8,0},{9,1},... | collective-permute-start | bytes 98312 | tf_op jit(solution)/shard_map/ppermute | solution.py:327
  22.5 12.8 %collective-permute-start.15 = (bf16[2,8192]{1,0:T(2,128)(2,1)S(1)}, bf16[2,8192]{1,0:T(2,128)(2,1)S(1)}, u32[]{:S(2)}, u32[]{:S(2)}) collective-permute-start(bf16[2,8192]{1,0:T(2,128)(2,1)S(1)} %get-tuple-element.15), channel_id=1, source_target_pairs={{0,12},{1,13},{2,14},{3,15},{4,0},{5,1},{6,2},{7,3},{8,4},{9,5},{1... | collective-permute-start | bytes 98312 | tf_op jit(solution)/shard_map/ppermute | solution.py:327
  34.7 13.0 %collective-permute-start.10 = (bf16[32,8192]{1,0:T(8,128)(2,1)S(1)}, bf16[32,8192]{1,0:T(8,128)(2,1)S(1)}, u32[]{:S(2)}, u32[]{:S(2)}) collective-permute-start(bf16[32,8192]{1,0:T(8,128)(2,1)S(1)} %bitcast.19), channel_id=1, source_target_pairs={{0,1},{1,0},{2,3},{3,2},{4,5},{5,4},{6,7},{7,6},{8,9},{9,8},{10,11... | collective-permute-start | bytes 1572872 | tf_op jit(solution)/shard_map/ppermute | solution.py:325
  34.8 13.8 %collective-permute-start.11 = (bf16[32,8192]{1,0:T(8,128)(2,1)S(1)}, bf16[32,8192]{1,0:T(8,128)(2,1)}, u32[]{:S(2)}, u32[]{:S(2)}) collective-permute-start(bf16[32,8192]{1,0:T(8,128)(2,1)S(1)} %collective-permute-done.refs_2_), channel_id=1, source_target_pairs={{0,1},{1,0},{2,3},{3,2},{4,5},{5,4},{6,7},{7,6},{8,9},{9,8},{10,11... | collective-permute-start | bytes 1572872 | tf_op jit(solution)/shard_map/ppermute | solution.py:325
  35.3 13.3 %collective-permute-start.12 = (bf16[32,8192]{1,0:T(8,128)(2,1)S(1)}, bf16[32,8192]{1,0:T(8,128)(2,1)}, u32[]{:S(2)}, u32[]{:S(2)}) collective-permute-start(bf16[32,8192]{1,0:T(8,128)(2,1)S(1)} %collective-permute-done.3.refs_4_), channel_id=1, source_target_pairs={{0,1},{1,0},{2,3},{3,2},{4,5},{5,4},{6,7},{7,6},{8,9},{9,8},{10,11... | collective-permute-start | bytes 1572872 | tf_op jit(solution)/shard_map/ppermute | solution.py:325
  35.5 5.9 %collective-permute-start.16 = (bf16[8,8192]{1,0:T(8,128)(2,1)S(1)}, bf16[8,8192]{1,0:T(8,128)(2,1)S(1)}, u32[]{:S(2)}, u32[]{:S(2)}) collective-permute-start(bf16[8,8192]{1,0:T(8,128)(2,1)S(1)} %pad_maximum_fusion), channel_id=1, source_target_pairs={{0,2},{1,3},{2,0},{3,1},{4,6},{5,7},{6,4},{7,5},{8,10},{9,11},{10,... | collective-permute-start | bytes 393224 | tf_op jit(solution)/shard_map/ppermute | solution.py:326
  41.6 6.2 %collective-permute-start.17 = (bf16[16,8192]{1,0:T(8,128)(2,1)S(1)}, bf16[16,8192]{1,0:T(8,128)(2,1)S(1)}, u32[]{:S(2)}, u32[]{:S(2)}) collective-permute-start(bf16[16,8192]{1,0:T(8,128)(2,1)S(1)} %concatenate.8.refs_6_), channel_id=1, source_target_pairs={{0,1},{1,0},{2,3},{3,2},{4,5},{5,4},{6,7},{7,6},{8,9},{9,8},{10,11... | collective-permute-start | bytes 786440 | tf_op jit(solution)/shard_map/ppermute | solution.py:325
  46.2 15.0 %collective-permute-start.25 = (bf16[64,1024]{1,0:T(8,128)(2,1)S(1)}, bf16[64,1024]{1,0:T(8,128)(2,1)S(1)}, u32[]{:S(2)}, u32[]{:S(2)}) collective-permute-start(bf16[64,1024]{1,0:T(8,128)(2,1)S(1)} %get-tuple-element.23.a_ref), channel_id=1, source_target_pairs={{0,16},{16,0},{1,17},{17,1},{2,18},{18,2},{3,19},{19,3},{4,20},{20... | collective-permute-start | bytes 393224 | tf_op jit(solution)/shard_map/ppermute | solution.py:328
  47.8 44.6 %collective-permute-start.1 = (bf16[32,8192]{1,0:T(8,128)(2,1)S(1)}, bf16[32,8192]{1,0:T(8,128)(2,1)S(1)}, u32[]{:S(2)}, u32[]{:S(2)}) collective-permute-start(bf16[32,8192]{1,0:T(8,128)(2,1)S(1)} %collective-permute-done.refs_2_), channel_id=1, source_target_pairs={{0,4},{1,5},{4,8},{5,9},{8,12},{9,13},{12,14},{13,15},{14,10},{15,... | collective-permute-start | bytes 1572872 | tf_op jit(solution)/shard_map/ppermute | solution.py:323
  60.6 18.9 %collective-permute-start.24 = (f32[32,1024]{1,0:T(8,128)S(1)}, f32[32,1024]{1,0:T(8,128)S(1)}, u32[]{:S(2)}, u32[]{:S(2)}) collective-permute-start(f32[32,1024]{1,0:T(8,128)S(1)} %get-tuple-element.22.a_ref), channel_id=1, source_target_pairs={{0,16},{16,0},{1,17},{17,1},{2,18},{18,2},{3,19},{19,3},{4,20},{20... | collective-permute-start | bytes 393224 | tf_op jit(solution)/shard_map/ppermute | solution.py:328
  90.4 2.0 %collective-permute-start.26 = (bf16[16,8192]{1,0:T(8,128)(2,1)}, bf16[16,8192]{1,0:T(8,128)(2,1)}, u32[]{:S(2)}, u32[]{:S(2)}) collective-permute-start(bf16[16,8192]{1,0:T(8,128)(2,1)} %get-tuple-element.25), channel_id=1, source_target_pairs={{0,1},{1,0},{2,3},{3,2},{4,5},{5,4},{6,7},{7,6},{8,9},{9,8},{10,11... | collective-permute-start | bytes 786440 | tf_op jit(solution)/shard_map/ppermute | solution.py:325
  90.4 14.3 %collective-permute-start.4 = (bf16[32,8192]{1,0:T(8,128)(2,1)S(1)}, bf16[32,8192]{1,0:T(8,128)(2,1)S(1)}, u32[]{:S(2)}, u32[]{:S(2)}) collective-permute-start(bf16[32,8192]{1,0:T(8,128)(2,1)S(1)} %collective-permute-done.3.refs_4_), channel_id=1, source_target_pairs={{4,0},{5,1},{8,4},{9,5},{12,8},{13,9},{14,12},{15,13},{10,14},{11,... | collective-permute-start | bytes 1572872 | tf_op jit(solution)/shard_map/ppermute | solution.py:324
  92.4 14.8 %collective-permute-start.6 = (bf16[32,8192]{1,0:T(8,128)(2,1)S(1)}, bf16[32,8192]{1,0:T(8,128)(2,1)S(1)}, u32[]{:S(2)}, u32[]{:S(2)}) collective-permute-start(bf16[32,8192]{1,0:T(8,128)(2,1)S(1)} %collective-permute-done.1.refs_0_), channel_id=1, source_target_pairs={{0,4},{1,5},{4,8},{5,9},{8,12},{9,13},{12,14},{13,15},{14,10},{15,... | collective-permute-start | bytes 1572872 | tf_op jit(solution)/shard_map/ppermute | solution.py:323
  93.6 16.0 %collective-permute-start.27 = (bf16[8,8192]{1,0:T(8,128)(2,1)S(1)}, bf16[8,8192]{1,0:T(8,128)(2,1)S(1)}, u32[]{:S(2)}, u32[]{:S(2)}) collective-permute-start(bf16[8,8192]{1,0:T(8,128)(2,1)S(1)} %slice.51), channel_id=1, source_target_pairs={{0,2},{1,3},{2,0},{3,1},{4,6},{5,7},{6,4},{7,5},{8,10},{9,11},{10,... | collective-permute-start | bytes 393224 | tf_op jit(solution)/shard_map/ppermute | solution.py:326
  104.7 14.5 %collective-permute-start.8 = (bf16[32,8192]{1,0:T(8,128)(2,1)S(1)}, bf16[32,8192]{1,0:T(8,128)(2,1)S(1)}, u32[]{:S(2)}, u32[]{:S(2)}) collective-permute-start(bf16[32,8192]{1,0:T(8,128)(2,1)S(1)} %collective-permute-done.4.refs_2_), channel_id=1, source_target_pairs={{4,0},{5,1},{8,4},{9,5},{12,8},{13,9},{14,12},{15,13},{10,14},{11,... | collective-permute-start | bytes 1572872 | tf_op jit(solution)/shard_map/ppermute | solution.py:324
  107.2 14.3 %collective-permute-start.19 = (bf16[16,8192]{1,0:T(8,128)(2,1)S(1)}, bf16[16,8192]{1,0:T(8,128)(2,1)}, u32[]{:S(2)}, u32[]{:S(2)}) collective-permute-start(bf16[16,8192]{1,0:T(8,128)(2,1)S(1)} %slice.36), channel_id=1, source_target_pairs={{0,4},{1,5},{4,8},{5,9},{8,12},{9,13},{12,14},{13,15},{14,10},{15,... | collective-permute-start | bytes 786440 | tf_op jit(solution)/shard_map/ppermute | solution.py:323
  111.0 10.5 %collective-permute-start.28 = (bf16[2,8192]{1,0:T(2,128)(2,1)}, bf16[2,8192]{1,0:T(2,128)(2,1)S(1)}, u32[]{:S(2)}, u32[]{:S(2)}) collective-permute-start(bf16[2,8192]{1,0:T(2,128)(2,1)} %get-tuple-element.32), channel_id=1, source_target_pairs={{0,12},{1,13},{2,14},{3,15},{4,0},{5,1},{6,2},{7,3},{8,4},{9,5},{1... | collective-permute-start | bytes 98312 | tf_op jit(solution)/shard_map/ppermute | solution.py:327
  111.2 10.9 %collective-permute-start.29 = (bf16[2,8192]{1,0:T(2,128)(2,1)}, bf16[2,8192]{1,0:T(2,128)(2,1)S(1)}, u32[]{:S(2)}, u32[]{:S(2)}) collective-permute-start(bf16[2,8192]{1,0:T(2,128)(2,1)} %get-tuple-element.34), channel_id=1, source_target_pairs={{0,8},{1,9},{2,10},{3,11},{4,12},{5,13},{6,14},{7,15},{8,0},{9,1},... | collective-permute-start | bytes 98312 | tf_op jit(solution)/shard_map/ppermute | solution.py:327
  111.2 10.9 %collective-permute-start.30 = (bf16[2,8192]{1,0:T(2,128)(2,1)S(1)}, bf16[2,8192]{1,0:T(2,128)(2,1)S(1)}, u32[]{:S(2)}, u32[]{:S(2)}) collective-permute-start(bf16[2,8192]{1,0:T(2,128)(2,1)S(1)} %get-tuple-element.33), channel_id=1, source_target_pairs={{0,4},{1,5},{2,6},{3,7},{4,8},{5,9},{6,10},{7,11},{8,12},{9,13},{1... | collective-permute-start | bytes 98312 | tf_op jit(solution)/shard_map/ppermute | solution.py:327
  120.0 7.6 %collective-permute-start.20 = (bf16[16,8192]{1,0:T(8,128)(2,1)}, bf16[16,8192]{1,0:T(8,128)(2,1)}, u32[]{:S(2)}, u32[]{:S(2)}) collective-permute-start(bf16[16,8192]{1,0:T(8,128)(2,1)} %slice.37), channel_id=1, source_target_pairs={{4,0},{5,1},{8,4},{9,5},{12,8},{13,9},{14,12},{15,13},{10,14},{11,... | collective-permute-start | bytes 786440 | tf_op jit(solution)/shard_map/ppermute | solution.py:324
  121.5 6.6 %collective-permute-start.21 = (bf16[16,8192]{1,0:T(8,128)(2,1)}, bf16[16,8192]{1,0:T(8,128)(2,1)}, u32[]{:S(2)}, u32[]{:S(2)}) collective-permute-start(bf16[16,8192]{1,0:T(8,128)(2,1)} %collective-permute-done.19.refs_0_), channel_id=1, source_target_pairs={{0,1},{1,0},{2,3},{3,2},{4,5},{5,4},{6,7},{7,6},{8,9},{9,8},{10,11... | collective-permute-start | bytes 786440 | tf_op jit(solution)/shard_map/ppermute | solution.py:325
  121.6 20.6 %collective-permute-start.2 = (bf16[32,8192]{1,0:T(8,128)(2,1)S(1)}, bf16[32,8192]{1,0:T(8,128)(2,1)}, u32[]{:S(2)}, u32[]{:S(2)}) collective-permute-start(bf16[32,8192]{1,0:T(8,128)(2,1)S(1)} %collective-permute-done.1.refs_0_), channel_id=1, source_target_pairs={{0,1},{1,0},{2,3},{3,2},{4,5},{5,4},{6,7},{7,6},{8,9},{9,8},{10,11... | collective-permute-start | bytes 1572872 | tf_op jit(solution)/shard_map/ppermute | solution.py:325
  122.1 20.1 %collective-permute-start.5 = (bf16[32,8192]{1,0:T(8,128)(2,1)S(1)}, bf16[32,8192]{1,0:T(8,128)(2,1)}, u32[]{:S(2)}, u32[]{:S(2)}) collective-permute-start(bf16[32,8192]{1,0:T(8,128)(2,1)S(1)} %collective-permute-done.4.refs_2_), channel_id=1, source_target_pairs={{0,1},{1,0},{2,3},{3,2},{4,5},{5,4},{6,7},{7,6},{8,9},{9,8},{10,11... | collective-permute-start | bytes 1572872 | tf_op jit(solution)/shard_map/ppermute | solution.py:325
  124.0 3.6 %collective-permute-start.31 = (f32[2,1]{0,1:T(1,128)S(1)}, f32[2,1]{0,1:T(1,128)S(1)}, u32[]{:S(2)}, u32[]{:S(2)}) collective-permute-start(f32[2,1]{0,1:T(1,128)S(1)} %bitcast.23), channel_id=1, source_target_pairs={{0,16},{16,0},{1,17},{17,1},{2,18},{18,2},{3,19},{19,3},{4,20},{20... | collective-permute-start | bytes 32 | tf_op jit(solution)/shard_map/ppermute | solution.py:328
  127.6 14.6 %collective-permute-start.7 = (bf16[32,8192]{1,0:T(8,128)(2,1)S(1)}, bf16[32,8192]{1,0:T(8,128)(2,1)}, u32[]{:S(2)}, u32[]{:S(2)}) collective-permute-start(bf16[32,8192]{1,0:T(8,128)(2,1)S(1)} %collective-permute-done.6.refs_4_), channel_id=1, source_target_pairs={{0,1},{1,0},{2,3},{3,2},{4,5},{5,4},{6,7},{7,6},{8,9},{9,8},{10,11... | collective-permute-start | bytes 1572872 | tf_op jit(solution)/shard_map/ppermute | solution.py:325
  127.6 14.6 %collective-permute-start.9 = (bf16[32,8192]{1,0:T(8,128)(2,1)S(1)}, bf16[32,8192]{1,0:T(8,128)(2,1)}, u32[]{:S(2)}, u32[]{:S(2)}) collective-permute-start(bf16[32,8192]{1,0:T(8,128)(2,1)S(1)} %collective-permute-done.8.refs_6_), channel_id=1, source_target_pairs={{0,1},{1,0},{2,3},{3,2},{4,5},{5,4},{6,7},{7,6},{8,9},{9,8},{10,11... | collective-permute-start | bytes 1572872 | tf_op jit(solution)/shard_map/ppermute | solution.py:325
  128.1 2.5 %collective-permute-start.22 = (bf16[16,8192]{1,0:T(8,128)(2,1)}, bf16[16,8192]{1,0:T(8,128)(2,1)}, u32[]{:S(2)}, u32[]{:S(2)}) collective-permute-start(bf16[16,8192]{1,0:T(8,128)(2,1)} %collective-permute-done.20.refs_1_), channel_id=1, source_target_pairs={{0,1},{1,0},{2,3},{3,2},{4,5},{5,4},{6,7},{7,6},{8,9},{9,8},{10,11... | collective-permute-start | bytes 786440 | tf_op jit(solution)/shard_map/ppermute | solution.py:325
  140.6 15.2 %collective-permute-start.23 = (bf16[64,1024]{1,0:T(8,128)(2,1)S(1)}, bf16[64,1024]{1,0:T(8,128)(2,1)S(1)}, u32[]{:S(2)}, u32[]{:S(2)}) collective-permute-start(bf16[64,1024]{1,0:T(8,128)(2,1)S(1)} %get-tuple-element.21), channel_id=1, source_target_pairs={{0,16},{16,0},{1,17},{17,1},{2,18},{18,2},{3,19},{19,3},{4,20},{20... | collective-permute-start | bytes 393224 | tf_op jit(solution)/shard_map/ppermute | solution.py:328
  153.8 10.9 %collective-permute-start.18 = (bf16[192,1024]{1,0:T(8,128)(2,1)S(1)}, bf16[192,1024]{1,0:T(8,128)(2,1)S(1)}, u32[]{:S(2)}, u32[]{:S(2)}) collective-permute-start(bf16[192,1024]{1,0:T(8,128)(2,1)S(1)} %get-tuple-element.19), channel_id=1, source_target_pairs={{0,16},{16,0},{1,17},{17,1},{2,18},{18,2},{3,19},{19,3},{4,20},{20... | collective-permute-start | bytes 1179656 | tf_op jit(solution)/shard_map/ppermute | solution.py:328
  (15 other events, 132.0 us)

commit v2 on v0

v2 whole, which is shorter than its diff:
```python
import jax
import jax.numpy as jnp
from jax import lax
from jax.experimental import pallas as pl
from jax.experimental.pallas import tpu as pltpu
from jax.sharding import PartitionSpec as P

D = 16384
HEADS = 128
KV_HEADS = 8
HEAD = 128
TREE = 16
GROUP = HEADS // KV_HEADS
FACTOR = HEAD ** (-0.5)
MIB = 1024 * 1024
ATTENTION_MIB = 58
EARLY = pl.CostEstimate(flops=1, bytes_accessed=1, transcendentals=0)
BF = jnp.bfloat16
F32 = jnp.float32


def small_params(limit=12):
    return pltpu.CompilerParams(vmem_limit_bytes=int(limit * MIB))


def stream_params():
    return pltpu.CompilerParams(
        vmem_limit_bytes=16 * MIB, dimension_semantics=("arbitrary",)
    )


CHIPS = 8


def chip_of(position):
    return (position, 0) if position < 4 else (7 - position, 1)


def device_of(position, core):
    z, x = chip_of(position % CHIPS)
    return (z * 2 + x) * 2 + core


def coordinates(request):
    core, x, z = request & 1, (request >> 1) & 1, request >> 2
    return core, x, z, jnp.where(x == 0, z, 7 - z)


PAIRS = ((-1, 3), (1, -3), (-2, 2), (0, 4))


def first_is_mine(pair, position, side):
    first = (position + PAIRS[pair][0] + CHIPS) & 7
    return first, (((first + 2) >> 2) & 1) == side


HBM = pl.BlockSpec(memory_space=pltpu.HBM)
VMEM = pl.BlockSpec(memory_space=pltpu.VMEM)
SMEM = pl.BlockSpec(memory_space=pltpu.SMEM)


def attention(queries, ck, cv, tk, tv, lengths, parents, last, picks=None):
    count, _, width = queries.shape
    cache = ck.shape[1]
    groups = ck.shape[2] // HEAD
    lanes = GROUP * HEAD
    sources = (parents, queries, ck, tk, cv, tv) + (picks or ())
    all_req = last.shape[0]

    def kernel(len_ref, last_ref, *refs):
        n = len(sources)
        here, refs = refs[:n], refs[n:]
        if picks:
            row_ref, o_ref, pick_ref, feats_ref, res_out_ref = refs[:5]
            refs = refs[5:]
        else:
            o_ref, pick_ref = refs[:2]
            refs = refs[2:]
        held, sem = refs[:n], refs[n]
        copies = [pltpu.make_async_copy(a, v, sem.at[i]) for i, (a, v) in enumerate(zip(here, held))]
        for c in copies:
            c.start()
        parent, q_ref, ck_ref, tk_ref, cv_ref, tv_ref = held[:6]
        first = lax.axis_index("request") * count
        copies[0].wait()
        up = lax.broadcasted_iota(jnp.int32, (TREE, TREE), 0)
        node = lax.broadcasted_iota(jnp.int32, (TREE, TREE), 1)
        spread = lax.broadcasted_iota(jnp.int32, (GROUP * TREE, TREE), 0) % TREE
        spread = spread == lax.broadcasted_iota(jnp.int32, (GROUP * TREE, TREE), 1)
        spread = jnp.where(spread, 1.0, 0.0).astype(BF)
        dims = (((1,), (1,)), ((), ()))
        seen = []
        for b in range(count):
            reach = jnp.where((parent[b : b + 1] == up) | (up == node), 1.0, 0.0).astype(BF)
            for _ in range(4):
                paths = jnp.dot(reach, reach, preferred_element_type=F32)
                reach = jnp.minimum(paths, 1.0).astype(BF)
            seen.append(lax.dot_general(spread, reach, dims, preferred_element_type=F32) > 0.5)
        for c in copies[1:6]:
            c.wait()
        for b in range(count):
            live = lax.broadcasted_iota(jnp.int32, (1, cache), 1) < len_ref[b]
            chosen = lax.broadcasted_iota(jnp.int32, (TREE, 1), 0) == last_ref[first + b]
            for g in range(groups):
                head = slice(g * HEAD, (g + 1) * HEAD)
                base = g * lanes
                q = jnp.concatenate(
                    [q_ref[b, :, base + h * HEAD : base + (h + 1) * HEAD] for h in range(GROUP)],
                    axis=0,
                )
                s_cache = lax.dot_general(q, ck_ref[b, :, head], dims, preferred_element_type=F32)
                s_tree = lax.dot_general(q, tk_ref[b, :, head], dims, preferred_element_type=F32)
                s_cache = jnp.where(live, s_cache * FACTOR, -1e30)
                s_tree = jnp.where(seen[b], s_tree * FACTOR, -1e30)
                top = jnp.maximum(
                    jnp.max(s_cache, axis=1, keepdims=True), jnp.max(s_tree, axis=1, keepdims=True)
                )
                e_cache = jnp.exp(s_cache - top)
                e_tree = jnp.exp(s_tree - top)
                total = jnp.sum(e_cache, axis=1, keepdims=True) + jnp.sum(
                    e_tree, axis=1, keepdims=True
                )
                inverse = 1.0 / total
                w_cache = (e_cache * inverse).astype(BF)
                w_tree = (e_tree * inverse).astype(BF)
                mixed = jnp.dot(w_cache, cv_ref[b, :, head], preferred_element_type=F32)
                mixed = mixed + jnp.dot(w_tree, tv_ref[b, :, head], preferred_element_type=F32)
                for h in range(GROUP):
                    block = mixed[h * TREE : (h + 1) * TREE]
                    where = slice(base + h * HEAD, base + (h + 1) * HEAD)
                    o_ref[b * TREE : (b + 1) * TREE, where] = block.astype(BF)
                    pick_ref[b : b + 1, where] = jnp.sum(
                        jnp.where(chosen, block, 0.0), axis=0, keepdims=True
                    ).astype(BF)

        if picks:
            side_rows = picks[0].shape[0]
            core, x, z, _ = coordinates(lax.axis_index("request"))
            order = lax.broadcasted_iota(jnp.int32, (all_req, all_req), 0)
            of_core, of_x = core ^ (order >> 4), x ^ ((order >> 3) & 1)
            of_z = z ^ ((order >> 1) & 3)
            req = ((of_z * 2 + of_x) * 2 + of_core) * count + (order & 1)
            named = req == lax.broadcasted_iota(jnp.int32, (all_req, all_req), 1)
            last_rel = jnp.sum(jnp.where(named, row_ref[...], 0), axis=1, keepdims=True)
            rows = req[:, :1] * TREE + last_rel - lax.axis_index("tensor") * side_rows
            hot = rows == lax.broadcasted_iota(jnp.int32, (all_req, side_rows), 1)
            hot = jnp.where(hot, 1.0, 0.0).astype(BF)
            for c in copies[6:9]:
                c.wait()
            for i in range(2):
                feats_ref[i * all_req : (i + 1) * all_req] = jnp.dot(
                    hot, held[6 + i][...], preferred_element_type=F32
                ).astype(BF)
            res_out_ref[...] = jnp.dot(hot, held[8][...], preferred_element_type=F32)

    arrays = [lengths, last, *sources]
    in_specs = [SMEM, SMEM] + [HBM] * len(sources)
    outs = [
        jax.ShapeDtypeStruct((count * TREE, width), BF),
        jax.ShapeDtypeStruct((count, width), BF),
    ]
    scratch = [pltpu.VMEM(a.shape, a.dtype) for a in sources]
    scratch.append(pltpu.SemaphoreType.DMA((len(sources),)))
    if picks:
        arrays.append(last[None, :])
        in_specs.append(VMEM)
        columns = picks[0].shape[1]
        outs += [
            jax.ShapeDtypeStruct((2 * all_req, columns), BF),
            jax.ShapeDtypeStruct((all_req, columns), F32),
        ]
    return pl.pallas_call(
        kernel,
        in_specs=in_specs,
        out_specs=[VMEM] * len(outs),
        out_shape=outs,
        scratch_shapes=scratch,
        compiler_params=small_params(ATTENTION_MIB),
        cost_estimate=EARLY,
        name="attention",
    )(*arrays)


def project(name, blocks, weights, extras, finish, outs, step=1024):
    rows = sum(x.shape[0] for x in blocks)
    depth, columns = weights.shape
    n = len(blocks)
    m = len(extras)

    def kernel(*refs):
        xs, w, more = refs[:n], refs[n], refs[n + 1 : n + 1 + m]
        results, total = refs[n + 1 + m : -1], refs[-1]
        for k in range(depth // step):
            part = slice(k * step, (k + 1) * step)
            x = jnp.concatenate([r[:, part] for r in xs], axis=0)
            term = jnp.dot(x, w[part], preferred_element_type=F32)
            if k == 0:
                total[...] = term
            else:
                total[...] += term
        finish(total, more, results)

    return pl.pallas_call(
        kernel,
        in_specs=[VMEM] * (n + 1 + m),
        out_specs=[VMEM] * len(outs),
        out_shape=outs,
        scratch_shapes=[pltpu.VMEM((rows, columns), F32)],
        compiler_params=small_params(),
        cost_estimate=EARLY,
        name=name,
    )(*blocks, weights, *extras)


def split_pairs(pairs, firsts, seconds, keep, send):
    position = coordinates(lax.axis_index("request"))[3]
    side = lax.axis_index("tensor")
    rows = keep.shape[0] // len(pairs)
    for i, pair in enumerate(pairs):
        mine = first_is_mine(pair, position, side)[1]
        u, v = firsts[i], seconds[i]
        keep[i * rows : (i + 1) * rows] = jnp.where(mine, u, v)
        send[i * rows : (i + 1) * rows] = jnp.where(mine, v, u).astype(BF)


def join_layer(name, layer, own, other, before, join, outs, finish, step=1024):
    depth, columns = join.shape[1:]
    steps = columns // (2 * step)

    def kernel(*refs):
        a_ref, b_ref, w0, w1 = refs[:4]
        x = (a_ref[...] + b_ref[...]).astype(BF)
        term = jnp.concatenate(
            [
                jnp.dot(x, w0[0], preferred_element_type=F32),
                jnp.dot(x, w1[0], preferred_element_type=F32),
            ],
            axis=1,
        )
        rest = refs[4:]
        if before is not None:
            term = term + rest[0][...]
            rest = rest[1:]
        finish(term, rest)

    rows = pl.BlockSpec((32, depth), lambda n: (0, 0))
    arrays = [own, other, join, join]
    specs = [
        rows,
        rows,
        pl.BlockSpec((1, depth, step), lambda n: (layer, 0, 2 * n)),
        pl.BlockSpec((1, depth, step), lambda n: (layer, 0, 2 * n + 1)),
    ]
    if before is not None:
        arrays.append(before)
        specs.append(pl.BlockSpec((32, 2 * step), lambda n: (0, n)))
    return pl.pallas_call(
        kernel,
        grid=(steps,),
        in_specs=specs,
        out_specs=[pl.BlockSpec((o.shape[0], 2 * step), lambda n: (0, n)) for o in outs],
        out_shape=outs,
        compiler_params=stream_params(),
        cost_estimate=EARLY,
        name=name,
    )(*arrays)


def project_and_join(name, blocks, weights, split, own, other, before, join, layer, step=1024):
    rows = sum(x.shape[0] for x in blocks)
    depth, columns = weights.shape
    count, joined = before.shape
    half = count // 2
    n = len(blocks)
    chunks = joined // step

    def kernel(*refs):
        xs, w, a_ref, b_ref, before_ref, j_hbm = refs[:n], *refs[n : n + 5]
        keep, send, keep_half, send_half, total, held, sem = refs[n + 5 :]
        copies = []
        for i in range(chunks):
            at = pl.ds(i * step, step)
            copies.append(
                pltpu.make_async_copy(j_hbm.at[layer, :, at], held.at[:, at], sem.at[i])
            )
            copies[-1].start()
        for k in range(depth // step):
            part = slice(k * step, (k + 1) * step)
            x = jnp.concatenate([r[:, part] for r in xs], axis=0)
            term = jnp.dot(x, w[part], preferred_element_type=F32)
            if k == 0:
                total[...] = term
            else:
                total[...] += term
        split(total, keep, send)
        x = (a_ref[...] + b_ref[...]).astype(BF)
        for i in range(chunks):
            part = slice(i * step, (i + 1) * step)
            copies[i].wait()
            term = jnp.dot(x, held[:, part], preferred_element_type=F32) + before_ref[:, part]
            keep_half[:, part] = term[:half]
            send_half[:, part] = term[half:].astype(BF)

    return pl.pallas_call(
        kernel,
        in_specs=[VMEM] * (n + 4) + [HBM],
        out_specs=[VMEM] * 4,
        out_shape=[
            jax.ShapeDtypeStruct((rows // 2, columns), F32),
            jax.ShapeDtypeStruct((rows // 2, columns), BF),
            jax.ShapeDtypeStruct((half, joined), F32),
            jax.ShapeDtypeStruct((half, joined), BF),
        ],
        scratch_shapes=[
            pltpu.VMEM((rows, columns), F32),
            pltpu.VMEM(join.shape[1:], BF),
            pltpu.SemaphoreType.DMA((chunks,)),
        ],
        compiler_params=small_params(22),
        cost_estimate=EARLY,
        name=name,
    )(*blocks, weights, own, other, before, join)


def finish_hidden(residual, kept, got):
    rows = 2 * TREE
    n = len(kept)
    pair_of = []
    for i, k in enumerate(kept):
        pair_of.append(k[1])
    arrays = [k[0] for k in kept] + list(got)

    def kernel(res, *refs):
        out = refs[-1]
        core, _, _, position = coordinates(lax.axis_index("request"))
        side = lax.axis_index("tensor")
        for i in range(n):
            keep, more = refs[i], refs[n + i]
            for j, pair in enumerate(pair_of[i]):
                first, mine = first_is_mine(pair, position, side)
                chip = jnp.where(mine, first, (first + 4) & 7)
                chip = jnp.where(chip < 4, chip * 2, (7 - chip) * 2 + 1)
                for c in range(2):
                    place = (chip * 2 + (core ^ c) - side * 8) * rows
                    place = pl.multiple_of(place, rows)
                    here = slice((2 * j + c) * rows, (2 * j + c + 1) * rows)
                    total = keep[here] + more[here].astype(F32)
                    out[pl.ds(place, rows)] = (res[pl.ds(place, rows)].astype(F32) + total).astype(BF)

    return pl.pallas_call(
        kernel,
        in_specs=[VMEM] * (1 + len(arrays)),
        out_specs=VMEM,
        out_shape=jax.ShapeDtypeStruct(residual.shape, BF),
        compiler_params=small_params(),
        cost_estimate=EARLY,
        name="finish_hidden",
    )(residual, *arrays)


def add_and_split(name, keep, got, pieces):
    rows, columns = keep.shape
    part = rows // pieces

    def kernel(k_ref, g_ref, stay_ref, *sends):
        total = k_ref[...] + g_ref[...].astype(F32)
        stay_ref[...] = total[:part]
        for i, s in enumerate(sends):
            s[...] = total[(i + 1) * part : (i + 2) * part].astype(BF)

    return pl.pallas_call(
        kernel,
        in_specs=[VMEM, VMEM],
        out_specs=[VMEM] * pieces,
        out_shape=[jax.ShapeDtypeStruct((part, columns), F32)]
        + [jax.ShapeDtypeStruct((part, columns), BF)] * (pieces - 1),
        compiler_params=small_params(),
        cost_estimate=EARLY,
        name=name,
    )(keep, got)


def tie(*values):
    return lax.optimization_barrier(values)


def ring_body(
    queries,
    cache_keys,
    cache_values,
    tree_keys,
    tree_values,
    cache_len,
    tree_parent,
    residual,
    low_feats,
    mid_feats,
    out_proj,
    last_node,
    draft_gain,
    draft_join,
):
    size = lax.axis_size("request")
    own_count = queries.shape[0]
    columns = residual.shape[2]
    width = draft_join.shape[2]
    all_req = last_node.shape[0]
    side_rows = residual.shape[0] * TREE
    block = own_count * TREE
    two = 2 * block

    forward = [(device_of(p, c), device_of(p + 1, c)) for p in range(CHIPS) for c in range(2)]
    backward = [(b, a) for a, b in forward]
    ahead = lambda v: lax.ppermute(v, "request", forward)
    back = lambda v: lax.ppermute(v, "request", backward)
    swap_core = lambda v: lax.ppermute(v, "request", [(r, r ^ 1) for r in range(size)])
    swap_x = lambda v: lax.ppermute(v, "request", [(r, r ^ 2) for r in range(size)])
    swap_z = lambda v, k: lax.ppermute(v, "request", [(r, r ^ (4 * k)) for r in range(size)])
    swap_side = lambda v: lax.ppermute(v, "tensor", [(0, 1), (1, 0)])
    f32 = lambda *shape: jax.ShapeDtypeStruct(shape, F32)
    bf16 = lambda *shape: jax.ShapeDtypeStruct(shape, BF)

    res = residual.reshape(-1, columns)
    h, picked, feats, res_rows = attention(
        queries,
        cache_keys,
        cache_values,
        tree_keys,
        tree_values,
        cache_len,
        tree_parent,
        last_node,
        picks=(low_feats.reshape(-1, columns), mid_feats.reshape(-1, columns), res),
    )
    feats_other = swap_side(feats)
    by_z = jnp.concatenate([picked, swap_z(picked, 1)], axis=0)
    h, by_z = tie(h, by_z)
    by_z = jnp.concatenate([by_z, swap_z(by_z, 2)], axis=0)
    f1, b1 = ahead(h), back(h)
    hs = swap_core(h)
    feats, feats_other, by_z = tie(feats, feats_other, by_z)
    by_x = jnp.concatenate([by_z, swap_x(by_z)], axis=0)
    store = lambda term, refs: refs[0].__setitem__(Ellipsis, term)
    (joined_low,) = join_layer(
        "join_low", 0, feats[:all_req], feats_other[:all_req], None, draft_join,
        [f32(all_req, width)], store,
    )

    f1, b1, hs, by_x, joined_low = tie(f1, b1, hs, by_x, joined_low)
    f2, b2 = ahead(f1), back(b1)
    picked_other = swap_core(by_x)
    f1s, b1s = swap_core(f1), swap_core(b1)

    def finish_a(total, more, results):
        results[0][...] = total[: 3 * two]
        results[1][...] = total[3 * two :] + more[0][...]

    part_a, part_picked = project(
        "project_a",
        [h, hs, f1, f1s, b1, b1s, by_x, picked_other],
        out_proj,
        [res_rows],
        finish_a,
        [f32(3 * two, columns), f32(all_req, columns)],
    )
    part_other = swap_side(part_picked)
    joined_low, part_a = tie(joined_low, part_a)
    (joined_feats,) = join_layer(
        "join_mid", 1, feats[all_req:], feats_other[all_req:], joined_low, draft_join,
        [f32(all_req, width)], store,
    )

    f2, b2, part_a, part_other, joined_feats = tie(f2, b2, part_a, part_other, joined_feats)
    f3, b3 = ahead(f2), back(b2)
    f2s, b2s = swap_core(f2), swap_core(b2)

    def split_2(total, keep, send):
        split_pairs([2], [total[:two]], [total[two:]], keep, send)

    keep_2, send_2, keep16, send16 = project_and_join(
        "project_2_join_hidden",
        [f2, f2s, b2, b2s],
        out_proj,
        split_2,
        part_picked,
        part_other,
        joined_feats,
        draft_join,
        2,
    )
    got16 = swap_core(send16)

    stay8, send8 = add_and_split("sum_core", keep16, got16, 2)
    f3, b3, stay8, send8, send_2 = tie(f3, b3, stay8, send8, send_2)
    got8 = swap_x(send8)
    got_2 = swap_side(send_2)
    f4, b4 = ahead(f3[:TREE]), back(b3[TREE:])
    f3s, b3s = swap_core(f3), swap_core(b3)

    def finish_3(total, more, results):
        before = more[0]
        split_pairs(
            [0, 1],
            [before[two : 2 * two], before[2 * two :]],
            [total[two:], total[:two]],
            *results,
        )

    keep_3, send_3 = project(
        "project_3", [f3, f3s, b3, b3s], out_proj, [part_a], finish_3,
        [f32(2 * two, columns), bf16(2 * two, columns)],
    )
    got_3 = swap_side(send_3)
    got8, keep_3 = tie(got8, keep_3)
    stay2, *sends = add_and_split("sum_x", stay8, got8, 4)

    f4, b4, got_2, *sends = tie(f4, b4, got_2, *sends)
    f4s, b4s = swap_core(f4), swap_core(b4)
    gots = [swap_z(v, k) for k, v in enumerate(sends, 1)]

    def finish_4(total, more, results):
        split_pairs([3], [more[0][:two]], [total[...]], *results)

    keep_4, send_4 = project(
        "project_4", [f4, b4, f4s, b4s], out_proj, [part_a], finish_4,
        [f32(two, columns), bf16(two, columns)],
    )
    got_4 = swap_side(send_4)
    keep_4, got_3, *gots = tie(keep_4, got_3, *gots)
    joined = stay2 + gots[0].astype(F32) + gots[1].astype(F32) + gots[2].astype(F32)
    squares = jnp.sum(joined * joined, axis=1, keepdims=True)
    other_squares = swap_side(squares)
    hidden = finish_hidden(
        res, [(keep_2, [2]), (keep_3, [0, 1]), (keep_4, [3])], [got_2, got_3, got_4]
    ).reshape(residual.shape)
    other_squares, hidden = tie(other_squares, hidden)
    row_scale = lax.rsqrt((squares + other_squares) / D + 1e-05)
    features = (joined * row_scale * draft_gain[None, :]).astype(BF)
    return (hidden, features)


def any_body(
    queries,
    cache_keys,
    cache_values,
    tree_keys,
    tree_values,
    cache_len,
    tree_parent,
    residual,
    low_feats,
    mid_feats,
    out_proj,
    last_node,
    draft_gain,
    draft_join,
):
    flat_rows, _ = attention(
        queries, cache_keys, cache_values, tree_keys, tree_values, cache_len, tree_parent, last_node
    )
    partial_value = jnp.dot(
        lax.all_gather(flat_rows, "request", axis=0, tiled=True),
        out_proj,
        preferred_element_type=F32,
    )
    summed = lax.psum_scatter(partial_value, "tensor", scatter_dimension=0, tiled=True)
    local_req = residual.shape[0]
    columns = residual.shape[2]
    hidden = (residual.reshape(-1, columns).astype(F32) + summed).astype(BF)
    hidden = hidden.reshape(residual.shape)
    first_req = lax.axis_index("tensor") * local_req
    chosen_all = last_node[:, None] == jnp.arange(TREE, dtype=jnp.int32)[None, :]
    own_chosen = lax.dynamic_slice_in_dim(chosen_all, first_req, local_req, 0)

    def choose(rows):
        return jnp.sum(jnp.where(own_chosen[:, :, None], rows.astype(F32), 0.0), axis=1).astype(BF)

    rows = jnp.stack((choose(low_feats), choose(mid_feats), choose(hidden)), axis=1)
    stacked = lax.all_gather(rows, "tensor", axis=0, tiled=True)
    joined_part = jnp.einsum("bsk,skn->bn", stacked, draft_join, preferred_element_type=F32)
    joined = lax.psum_scatter(joined_part, "request", scatter_dimension=0, tiled=True)
    squares = lax.psum(jnp.sum(joined * joined, axis=1), "tensor")
    row_scale = lax.rsqrt(squares / D + 1e-05)
    features = (joined * row_scale[:, None] * draft_gain[None, :]).astype(BF)
    return (hidden, features)


def solution(mesh):
    small = mesh.shape["tensor"] == 2 and mesh.shape["request"] == 2 * CHIPS
    return jax.shard_map(
        ring_body if small else any_body,
        mesh=mesh,
        in_specs=(
            P("request", None, "tensor"),
            P("request", None, "tensor"),
            P("request", None, "tensor"),
            P("request", None, "tensor"),
            P("request", None, "tensor"),
            P("request"),
            P("request", None),
            P("tensor", None, "request"),
            P("tensor", None, "request"),
            P("tensor", None, "request"),
            P("tensor", "request"),
            P(),
            P("tensor"),
            P(None, "request", "tensor"),
        ),
        out_specs=(P("tensor", None, "request"), P("request", "tensor")),
        check_vma=False,
    )
```

time: 301 us -> 93.9 us (0.31)
  waiting for transfers between devices: 201 us -> 18 us
  matrix products: 45.8 us -> 0 us
  Pallas kernels: 0 us -> 42.5 us
  starting transfers between devices: 0.12 us -> 29.4 us
  blocking collectives: 18.7 us -> 0 us
  between operations: 13.9 us -> 0.98 us
  local copies, waits for them, and re-layouts: 12 us -> 0.97 us
  other arithmetic: 8.41 us -> 1.83 us
    psum x1 -> x0, waiting for transfers between devices: 93.4 us -> none  [body(): joined_total = lax.psum(joined_part, 'request')]
    all_gather x1 -> x0, waiting for transfers between devices: 77.6 us -> none  [body(): lax.all_gather(flat_rows, 'request', axis=0, tiled=True)]
    dot_general x40 -> x0, matrix products: 45.8 us -> none  [the longest x1 20.8 us: body(): jnp.einsum('bsk,skn->bn', stacked, draft_join, preferred_element_type=jnp...]
    pallas_call x0 -> x10, Pallas kernels: none -> 42.5 us  [the longest x2 16.2 us: join_layer(): pl.pallas_call(kernel, grid=(steps,), in_specs=specs, out_specs=[pl.Block...]
    reduce_scatter x1 -> x0, waiting for transfers between devices: 30 us -> none  [body(): lax.psum_scatter(partial_value, 'tensor', scatter_dimension=0, tiled=True)]
    ppermute x0 -> x32, starting transfers between devices: none -> 29.4 us  [the longest x5 10.6 us: ring_body(): lax.ppermute(v, 'request', [(r, r ^ 4 * k) for r in range(size)])]
    ppermute x0 -> x32, waiting for transfers between devices: none -> 18 us  [the longest x2 5.7 us: ring_body(): lax.ppermute(v, 'request', [(r, r ^ 2) for r in range(size)])]
    all_gather x3 -> x0, blocking collectives: 13.7 us -> none  [the longest x1 4.59 us: body(): lax.all_gather(pick(hidden), 'tensor', axis=0, tiled=True)]
  transfers between devices with their start and end apart: 3 -> 32, of which waited for: 3 -> 10; matrix products, arithmetic and copies ran while one was open for 0% -> 1% of each run, Pallas kernels for 0% -> 38%
where the time goes in v2:
time: 93.9 us; the launch traced here: 93.7 us
  Pallas kernels  42.5 us (45%)
  starting transfers between devices  29.4 us (31%)
  waiting for transfers between devices  18 us (19%)
  other arithmetic  1.83 us (2%)
  between operations  0.98 us (1%)
  local copies, waits for them, and re-layouts  0.97 us (1%)
    pallas_call x2, Pallas kernels, join_layer(): pl.pallas_call(kernel, grid=(steps,), in_specs=specs, out_specs=[pl.Block...  16.2 us
    ppermute x5, starting transfers between devices, ring_body(): lax.ppermute(v, 'request', [(r, r ^ 4 * k) for r in range(size)])  10.6 us
    pallas_call x3, Pallas kernels, project(): pl.pallas_call(kernel, in_specs=[VMEM] * (n + 1 + m), out_specs=[VMEM] *...  9.31 us
    pallas_call x1, Pallas kernels, project_and_join(): pl.pallas_call(kernel, in_specs=[VMEM] * (n + 4) + [HBM], out_specs=[VMEM...  8.56 us
    pallas_call x1, Pallas kernels, attention(): pl.pallas_call(kernel, in_specs=in_specs, out_specs=[VMEM] * len(outs), o...  7.4 us
    ppermute x6, starting transfers between devices, ring_body(): swap_side = lambda v: lax.ppermute(v, 'tensor', [(0, 1), (1, 0)])  6.26 us
    ppermute x2, waiting for transfers between devices, ring_body(): lax.ppermute(v, 'request', [(r, r ^ 2) for r in range(size)])  5.7 us
    ppermute x4, starting transfers between devices, ring_body(): ahead = lambda v: lax.ppermute(v, 'request', forward)  4.71 us
  transfers between devices with their start and end apart: 32, of which 10 were waited for; matrix products, arithmetic and copies ran while one was open for 1% of the time, Pallas kernels for 38%

profile of v2, /device:TPU:0, one launch (start us, length us, event | category | flops | bytes accessed | tf_op | source)
XLA Modules:
  0.0 93.7 jit_solution(965481267013273878)
XLA Ops:
  0.6 7.4 %attention.1 = (bf16[32,8192]{1,0:T(8,128)(2,1)}, bf16[2,8192]{1,0:T(2,128)(2,1)}, bf16[64,1024]{1,0:T(8,128)(2,1)}, f32[32,1024]{1,0:T(8,128)}) custom-call(s32[2]{0:T(128)} %len_ref.1, s32[32]{0:T(128)} %last_ref.1, s32[2,16]{1,0:T(2,128)} %refs_0_.1, bf16[2,16,8192]{2,1,0:T(8,128)(2,1)} %refs_1_.1, bf16[2,256,512]{2,1,0:T(8,128)(2,1)} %refs_2_.3, ...), custom_call_target="tpu_custom_call" | custom-call | flops 1 | bytes 1 | tf_op jit(solution)/shard_map/attention/pallas_call | solution.py:172
  8.1 3.1 %collective-permute-start = (bf16[2,8192]{1,0:T(2,128)(2,1)}, bf16[2,8192]{1,0:T(2,128)(2,1)S(1)}, u32[]{:S(2)}, u32[]{:S(2)}) collective-permute-start(bf16[2,8192]{1,0:T(2,128)(2,1)} %get-tuple-element.60), channel_id=1, source_target_pairs={{0,4},{1,5},{2,6},{3,7},{4,0},{5,1},{6,2},{7,3},{8,12},{9,13},{10,... | collective-permute-start | bytes 98312 | tf_op jit(solution)/shard_map/ppermute | solution.py:418
  11.1 2.1 %collective-permute-done = bf16[2,8192]{1,0:T(2,128)(2,1)S(1)} collective-permute-done((bf16[2,8192]{1,0:T(2,128)(2,1)}, bf16[2,8192]{1,0:T(2,128)(2,1)S(1)}, u32[]{:S(2)}, u32[]{:S(2)}) %collective-permute-start) | collective-permute-done | bytes 32800 | tf_op jit(solution)/shard_map/ppermute | solution.py:418
  13.2 0.8 pad_maximum_fusion.2
  14.1 3.1 %collective-permute-start.5 = (bf16[4,8192]{1,0:T(4,128)(2,1)S(1)}, bf16[4,8192]{1,0:T(4,128)(2,1)S(1)}, u32[]{:S(2)}, u32[]{:S(2)}) collective-permute-start(bf16[4,8192]{1,0:T(4,128)(2,1)S(1)} %pad_maximum_fusion.2), channel_id=1, source_target_pairs={{0,8},{1,9},{2,10},{3,11},{4,12},{5,13},{6,14},{7,15},{8,0},{9,1},... | collective-permute-start | bytes 196616 | tf_op jit(solution)/shard_map/ppermute | solution.py:418
  17.2 1.5 %collective-permute-start.4 = (bf16[64,1024]{1,0:T(8,128)(2,1)}, bf16[64,1024]{1,0:T(8,128)(2,1)S(1)}, u32[]{:S(2)}, u32[]{:S(2)}) collective-permute-start(bf16[64,1024]{1,0:T(8,128)(2,1)} %get-tuple-element.65), channel_id=1, source_target_pairs={{0,16},{16,0},{1,17},{17,1},{2,18},{18,2},{3,19},{19,3},{4,20},{20... | collective-permute-start | bytes 393224 | tf_op jit(solution)/shard_map/ppermute | solution.py:419
  18.7 1.6 %collective-permute-start.1 = (bf16[32,8192]{1,0:T(8,128)(2,1)}, bf16[32,8192]{1,0:T(8,128)(2,1)S(1)}, u32[]{:S(2)}, u32[]{:S(2)}) collective-permute-start(bf16[32,8192]{1,0:T(8,128)(2,1)} %get-tuple-element.61.refs_0_), channel_id=1, source_target_pairs={{0,4},{1,5},{4,8},{5,9},{8,12},{9,13},{12,14},{13,15},{14,10},{15,... | collective-permute-start | bytes 1572872 | tf_op jit(solution)/shard_map/ppermute | solution.py:414
  20.8 1.6 %collective-permute-done.4 = bf16[64,1024]{1,0:T(8,128)(2,1)S(1)} collective-permute-done((bf16[64,1024]{1,0:T(8,128)(2,1)}, bf16[64,1024]{1,0:T(8,128)(2,1)S(1)}, u32[]{:S(2)}, u32[]{:S(2)}) %collective-permute-start.4) | collective-permute-done | bytes 131104 | tf_op jit(solution)/shard_map/ppermute | solution.py:419
  22.4 1.5 %collective-permute-start.6 = (bf16[8,8192]{1,0:T(8,128)(2,1)S(1)}, bf16[8,8192]{1,0:T(8,128)(2,1)S(1)}, u32[]{:S(2)}, u32[]{:S(2)}) collective-permute-start(bf16[8,8192]{1,0:T(8,128)(2,1)S(1)} %pad_maximum_fusion.1), channel_id=1, source_target_pairs={{0,2},{1,3},{2,0},{3,1},{4,6},{5,7},{6,4},{7,5},{8,10},{9,11},{10,... | collective-permute-start | bytes 393224 | tf_op jit(solution)/shard_map/ppermute | solution.py:417
  23.9 0.9 fusion
  24.8 8.5 %join_low.1.refs_4_ = f32[32,8192]{1,0:T(8,128)S(1)} custom-call(bf16[32,1024]{1,0:T(8,128)(2,1)S(1)} %get-tuple-element.120.refs_0_, bf16[32,1024]{1,0:T(8,128)(2,1)S(1)} %get-tuple-element.117.refs_1_, bf16[3,1024,8192]{2,1,0:T(8,128)(2,1)} %refs_8_.3, bf16[3,1024,8192]{2,1,0:T(8,128)(2,1)} %refs_8_.3), custom_call_target="tpu_custom_call" | custom-call | flops 1 | bytes 1 | tf_op jit(solution)/shard_map/join_low/pallas_call | solution.py:257
  34.3 1.2 %collective-permute-start.7 = (bf16[32,8192]{1,0:T(8,128)(2,1)S(1)}, bf16[32,8192]{1,0:T(8,128)(2,1)S(1)}, u32[]{:S(2)}, u32[]{:S(2)}) collective-permute-start(bf16[32,8192]{1,0:T(8,128)(2,1)S(1)} %collective-permute-done.1.refs_2_), channel_id=1, source_target_pairs={{0,4},{1,5},{4,8},{5,9},{8,12},{9,13},{12,14},{13,15},{14,10},{15,... | collective-permute-start | bytes 1572872 | tf_op jit(solution)/shard_map/ppermute | solution.py:414
  35.5 0.8 collective-permute-start.8
  36.3 1.5 %collective-permute-done.11.refs_7_ = bf16[16,8192]{1,0:T(8,128)(2,1)S(1)} collective-permute-done((bf16[16,8192]{1,0:T(8,128)(2,1)S(1)}, bf16[16,8192]{1,0:T(8,128)(2,1)S(1)}, u32[]{:S(2)}, u32[]{:S(2)}) %collective-permute-start.11) | collective-permute-done | bytes 262176 | tf_op jit(solution)/shard_map/ppermute | solution.py:416
  37.9 3.9 %project_a.1 = (f32[192,1024]{1,0:T(8,128)S(1)}, f32[32,1024]{1,0:T(8,128)S(1)}) custom-call(bf16[32,8192]{1,0:T(8,128)(2,1)S(1)} %copy-done.1, bf16[32,8192]{1,0:T(8,128)(2,1)S(1)} %collective-permute-done.3.refs_1_, bf16[32,8192]{1,0:T(8,128)(2,1)S(1)} %collective-permute-done.1.refs_2_, bf16[32,8192]{1,0:T(8,128)(2,1)S(1)} %collective-permute-done.9.refs_3_, ...), custom_call_target="tpu_custom_call" | custom-call | flops 1 | bytes 1 | tf_op jit(solution)/shard_map/project_a/pallas_call | solution.py:203
  41.9 1.2 %collective-permute-start.12 = (f32[32,1024]{1,0:T(8,128)S(1)}, f32[32,1024]{1,0:T(8,128)S(1)}, u32[]{:S(2)}, u32[]{:S(2)}) collective-permute-start(f32[32,1024]{1,0:T(8,128)S(1)} %get-tuple-element.75.refs_5_), channel_id=1, source_target_pairs={{0,16},{16,0},{1,17},{17,1},{2,18},{18,2},{3,19},{19,3},{4,20},{20... | collective-permute-start | bytes 393224 | tf_op jit(solution)/shard_map/ppermute | solution.py:419
  43.1 7.7 %join_mid.1.refs_7_ = f32[32,8192]{1,0:T(8,128)S(1)} custom-call(bf16[32,1024]{1,0:T(8,128)(2,1)S(1)} %get-tuple-element.121.refs_0_, bf16[32,1024]{1,0:T(8,128)(2,1)S(1)} %get-tuple-element.116.refs_1_, bf16[3,1024,8192]{2,1,0:T(8,128)(2,1)} %refs_8_.3, bf16[3,1024,8192]{2,1,0:T(8,128)(2,1)} %refs_8_.3, f32[32,8192]{1,0:T(8,128)S(1)} %join_low.1.refs_4_), custom_call_target="tpu_custom_call" | custom-call | flops 1 | bytes 1 | tf_op jit(solution)/shard_map/join_mid/pallas_call | solution.py:257
  51.4 1.6 %collective-permute-start.13 = (bf16[32,8192]{1,0:T(8,128)(2,1)S(1)}, bf16[32,8192]{1,0:T(8,128)(2,1)S(1)}, u32[]{:S(2)}, u32[]{:S(2)}) collective-permute-start(bf16[32,8192]{1,0:T(8,128)(2,1)S(1)} %collective-permute-done.7.refs_0_), channel_id=1, source_target_pairs={{0,4},{1,5},{4,8},{5,9},{8,12},{9,13},{12,14},{13,15},{14,10},{15,... | collective-permute-start | bytes 1572872 | tf_op jit(solution)/shard_map/ppermute | solution.py:414
  53.6 8.6 %project_2_join_hidden.1 = (f32[64,1024]{1,0:T(8,128)S(1)}, bf16[64,1024]{1,0:T(8,128)(2,1)S(1)}, f32[16,8192]{1,0:T(8,128)S(1)}, bf16[16,8192]{1,0:T(8,128)(2,1)S(1)}) custom-call(bf16[32,8192]{1,0:T(8,128)(2,1)S(1)} %collective-permute-done.7.refs_0_, bf16[32,8192]{1,0:T(8,128)(2,1)S(1)} %collective-permute-done.15.refs_1_, ...), custom_call_target="tpu_custom_call" | custom-call | flops 1 | bytes 1 | tf_op jit(solution)/shard_map/project_2_join_hidden/pallas_call | solution.py:304
  62.4 1.4 %collective-permute-done.17.g_ref = bf16[16,8192]{1,0:T(8,128)(2,1)S(1)} collective-permute-done((bf16[16,8192]{1,0:T(8,128)(2,1)S(1)}, bf16[16,8192]{1,0:T(8,128)(2,1)S(1)}, u32[]{:S(2)}, u32[]{:S(2)}) %collective-permute-start.17) | collective-permute-done | bytes 262176 | tf_op jit(solution)/shard_map/ppermute | solution.py:416
  63.8 1.5 %collective-permute-done.13.refs_0_ = bf16[32,8192]{1,0:T(8,128)(2,1)S(1)} collective-permute-done((bf16[32,8192]{1,0:T(8,128)(2,1)S(1)}, bf16[32,8192]{1,0:T(8,128)(2,1)S(1)}, u32[]{:S(2)}, u32[]{:S(2)}) %collective-permute-start.13) | collective-permute-done | bytes 524320 | tf_op jit(solution)/shard_map/ppermute | solution.py:414
  65.3 1.3 %collective-permute-done.14.refs_2_ = bf16[32,8192]{1,0:T(8,128)(2,1)S(1)} collective-permute-done((bf16[32,8192]{1,0:T(8,128)(2,1)S(1)}, bf16[32,8192]{1,0:T(8,128)(2,1)S(1)}, u32[]{:S(2)}, u32[]{:S(2)}) %collective-permute-start.14) | collective-permute-done | bytes 524320 | tf_op jit(solution)/shard_map/ppermute | solution.py:415
  67.5 1.7 %collective-permute-start.22 = (bf16[16,8192]{1,0:T(8,128)(2,1)S(1)}, bf16[16,8192]{1,0:T(8,128)(2,1)S(1)}, u32[]{:S(2)}, u32[]{:S(2)}) collective-permute-start(bf16[16,8192]{1,0:T(8,128)(2,1)S(1)} %slice.23), channel_id=1, source_target_pairs={{4,0},{5,1},{8,4},{9,5},{12,8},{13,9},{14,12},{15,13},{10,14},{11,... | collective-permute-start | bytes 786440 | tf_op jit(solution)/shard_map/ppermute | solution.py:415
  69.7 0.9 collective-permute-start.23
  70.6 2.3 %project_3.1 = (f32[128,1024]{1,0:T(8,128)S(1)}, bf16[128,1024]{1,0:T(8,128)(2,1)S(1)}) custom-call(bf16[32,8192]{1,0:T(8,128)(2,1)S(1)} %collective-permute-done.13.refs_0_, bf16[32,8192]{1,0:T(8,128)(2,1)S(1)} %collective-permute-done.19.refs_1_, bf16[32,8192]{1,0:T(8,128)(2,1)S(1)} %collective-permute-done.14.refs_2_, ...), custom_call_target="tpu_custom_call" | custom-call | flops 1 | bytes 1 | tf_op jit(solution)/shard_map/project_3/pallas_call | solution.py:203
  73.0 5.3 %collective-permute-done.18.g_ref = bf16[8,8192]{1,0:T(8,128)(2,1)S(1)} collective-permute-done((bf16[8,8192]{1,0:T(8,128)(2,1)S(1)}, bf16[8,8192]{1,0:T(8,128)(2,1)S(1)}, u32[]{:S(2)}, u32[]{:S(2)}) %collective-permute-start.18) | collective-permute-done | bytes 131104 | tf_op jit(solution)/shard_map/ppermute | solution.py:417
  79.5 2.5 %collective-permute-start.28 = (bf16[2,8192]{1,0:T(2,128)(2,1)S(1)}, bf16[2,8192]{1,0:T(2,128)(2,1)S(1)}, u32[]{:S(2)}, u32[]{:S(2)}) collective-permute-start(bf16[2,8192]{1,0:T(2,128)(2,1)S(1)} %get-tuple-element.103), channel_id=1, source_target_pairs={{0,8},{1,9},{2,10},{3,11},{4,12},{5,13},{6,14},{7,15},{8,0},{9,1},... | collective-permute-start | bytes 98312 | tf_op jit(solution)/shard_map/ppermute | solution.py:418
  82.0 1.9 %collective-permute-start.29 = (bf16[2,8192]{1,0:T(2,128)(2,1)S(1)}, bf16[2,8192]{1,0:T(2,128)(2,1)S(1)}, u32[]{:S(2)}, u32[]{:S(2)}) collective-permute-start(bf16[2,8192]{1,0:T(2,128)(2,1)S(1)} %get-tuple-element.104), channel_id=1, source_target_pairs={{0,12},{1,13},{2,14},{3,15},{4,8},{5,9},{6,10},{7,11},{8,4},{9,5},... | collective-permute-start | bytes 98312 | tf_op jit(solution)/shard_map/ppermute | solution.py:418
  83.8 3.0 %project_4.1 = (f32[64,1024]{1,0:T(8,128)S(1)}, bf16[64,1024]{1,0:T(8,128)(2,1)S(1)}) custom-call(bf16[16,8192]{1,0:T(8,128)(2,1)S(1)} %collective-permute-done.21.refs_0_, bf16[16,8192]{1,0:T(8,128)(2,1)S(1)} %collective-permute-done.22.refs_1_, bf16[16,8192]{1,0:T(8,128)(2,1)S(1)} %collective-permute-done.24.refs_2_, ...), custom_call_target="tpu_custom_call" | custom-call | flops 1 | bytes 1 | tf_op jit(solution)/shard_map/project_4/pallas_call | solution.py:203
  86.9 1.6 %collective-permute-start.31 = (bf16[64,1024]{1,0:T(8,128)(2,1)S(1)}, bf16[64,1024]{1,0:T(8,128)(2,1)S(1)}, u32[]{:S(2)}, u32[]{:S(2)}) collective-permute-start(bf16[64,1024]{1,0:T(8,128)(2,1)S(1)} %get-tuple-element.113), channel_id=1, source_target_pairs={{0,16},{16,0},{1,17},{17,1},{2,18},{18,2},{3,19},{19,3},{4,20},{20... | collective-permute-start | bytes 393224 | tf_op jit(solution)/shard_map/ppermute | solution.py:419
  89.2 2.7 %collective-permute-done.31.refs_5_ = bf16[64,1024]{1,0:T(8,128)(2,1)S(1)} collective-permute-done((bf16[64,1024]{1,0:T(8,128)(2,1)S(1)}, bf16[64,1024]{1,0:T(8,128)(2,1)S(1)}, u32[]{:S(2)}, u32[]{:S(2)}) %collective-permute-start.31) | collective-permute-done | bytes 131104 | tf_op jit(solution)/shard_map/ppermute | solution.py:419
  91.9 1.0 %finish_hidden.1 = bf16[256,1024]{1,0:T(8,128)(2,1)} custom-call(bf16[256,1024]{1,0:T(8,128)(2,1)S(1)} %bitcast.12, f32[64,1024]{1,0:T(8,128)S(1)} %get-tuple-element.108.refs_0_, f32[128,1024]{1,0:T(8,128)S(1)} %get-tuple-element.109.refs_1_, f32[64,1024]{1,0:T(8,128)S(1)} %get-tuple-element.110.refs_2_, ...), custom_call_target="tpu_custom_call" | custom-call | flops 1 | bytes 1 | tf_op jit(solution)/shard_map/finish_hidden/pallas_call | solution.py:350
  (68 shorter events, 6.9 us)
Async XLA Ops:
  8.1 5.2 %collective-permute-start = (bf16[2,8192]{1,0:T(2,128)(2,1)}, bf16[2,8192]{1,0:T(2,128)(2,1)S(1)}, u32[]{:S(2)}, u32[]{:S(2)}) collective-permute-start(bf16[2,8192]{1,0:T(2,128)(2,1)} %get-tuple-element.60), channel_id=1, source_target_pairs={{0,4},{1,5},{2,6},{3,7},{4,0},{5,1},{6,2},{7,3},{8,12},{9,13},{10,... | collective-permute-start | bytes 98312 | tf_op jit(solution)/shard_map/ppermute | solution.py:418
  14.1 6.7 %collective-permute-start.5 = (bf16[4,8192]{1,0:T(4,128)(2,1)S(1)}, bf16[4,8192]{1,0:T(4,128)(2,1)S(1)}, u32[]{:S(2)}, u32[]{:S(2)}) collective-permute-start(bf16[4,8192]{1,0:T(4,128)(2,1)S(1)} %pad_maximum_fusion.2), channel_id=1, source_target_pairs={{0,8},{1,9},{2,10},{3,11},{4,12},{5,13},{6,14},{7,15},{8,0},{9,1},... | collective-permute-start | bytes 196616 | tf_op jit(solution)/shard_map/ppermute | solution.py:418
  17.2 5.2 %collective-permute-start.4 = (bf16[64,1024]{1,0:T(8,128)(2,1)}, bf16[64,1024]{1,0:T(8,128)(2,1)S(1)}, u32[]{:S(2)}, u32[]{:S(2)}) collective-permute-start(bf16[64,1024]{1,0:T(8,128)(2,1)} %get-tuple-element.65), channel_id=1, source_target_pairs={{0,16},{16,0},{1,17},{17,1},{2,18},{18,2},{3,19},{19,3},{4,20},{20... | collective-permute-start | bytes 393224 | tf_op jit(solution)/shard_map/ppermute | solution.py:419
  18.7 15.0 %collective-permute-start.1 = (bf16[32,8192]{1,0:T(8,128)(2,1)}, bf16[32,8192]{1,0:T(8,128)(2,1)S(1)}, u32[]{:S(2)}, u32[]{:S(2)}) collective-permute-start(bf16[32,8192]{1,0:T(8,128)(2,1)} %get-tuple-element.61.refs_0_), channel_id=1, source_target_pairs={{0,4},{1,5},{4,8},{5,9},{8,12},{9,13},{12,14},{13,15},{14,10},{15,... | collective-permute-start | bytes 1572872 | tf_op jit(solution)/shard_map/ppermute | solution.py:414
  20.3 13.4 %collective-permute-start.2 = (bf16[32,8192]{1,0:T(8,128)(2,1)}, bf16[32,8192]{1,0:T(8,128)(2,1)S(1)}, u32[]{:S(2)}, u32[]{:S(2)}) collective-permute-start(bf16[32,8192]{1,0:T(8,128)(2,1)} %get-tuple-element.61.refs_0_), channel_id=1, source_target_pairs={{4,0},{5,1},{8,4},{9,5},{12,8},{13,9},{14,12},{15,13},{10,14},{11,... | collective-permute-start | bytes 1572872 | tf_op jit(solution)/shard_map/ppermute | solution.py:415
  20.7 13.0 %collective-permute-start.3 = (bf16[32,8192]{1,0:T(8,128)(2,1)}, bf16[32,8192]{1,0:T(8,128)(2,1)S(1)}, u32[]{:S(2)}, u32[]{:S(2)}) collective-permute-start(bf16[32,8192]{1,0:T(8,128)(2,1)} %get-tuple-element.61.refs_0_), channel_id=1, source_target_pairs={{0,1},{1,0},{2,3},{3,2},{4,5},{5,4},{6,7},{7,6},{8,9},{9,8},{10,11... | collective-permute-start | bytes 1572872 | tf_op jit(solution)/shard_map/ppermute | solution.py:416
  22.4 11.3 %collective-permute-start.6 = (bf16[8,8192]{1,0:T(8,128)(2,1)S(1)}, bf16[8,8192]{1,0:T(8,128)(2,1)S(1)}, u32[]{:S(2)}, u32[]{:S(2)}) collective-permute-start(bf16[8,8192]{1,0:T(8,128)(2,1)S(1)} %pad_maximum_fusion.1), channel_id=1, source_target_pairs={{0,2},{1,3},{2,0},{3,1},{4,6},{5,7},{6,4},{7,5},{8,10},{9,11},{10,... | collective-permute-start | bytes 393224 | tf_op jit(solution)/shard_map/ppermute | solution.py:417
  33.7 4.1 %collective-permute-start.10 = (bf16[32,8192]{1,0:T(8,128)(2,1)S(1)}, bf16[32,8192]{1,0:T(8,128)(2,1)S(1)}, u32[]{:S(2)}, u32[]{:S(2)}) collective-permute-start(bf16[32,8192]{1,0:T(8,128)(2,1)S(1)} %collective-permute-done.2.refs_4_), channel_id=1, source_target_pairs={{0,1},{1,0},{2,3},{3,2},{4,5},{5,4},{6,7},{7,6},{8,9},{9,8},{10,11... | collective-permute-start | bytes 1572872 | tf_op jit(solution)/shard_map/ppermute | solution.py:416
  33.8 4.1 %collective-permute-start.9 = (bf16[32,8192]{1,0:T(8,128)(2,1)S(1)}, bf16[32,8192]{1,0:T(8,128)(2,1)S(1)}, u32[]{:S(2)}, u32[]{:S(2)}) collective-permute-start(bf16[32,8192]{1,0:T(8,128)(2,1)S(1)} %collective-permute-done.1.refs_2_), channel_id=1, source_target_pairs={{0,1},{1,0},{2,3},{3,2},{4,5},{5,4},{6,7},{7,6},{8,9},{9,8},{10,11... | collective-permute-start | bytes 1572872 | tf_op jit(solution)/shard_map/ppermute | solution.py:416
  34.3 16.5 %collective-permute-start.7 = (bf16[32,8192]{1,0:T(8,128)(2,1)S(1)}, bf16[32,8192]{1,0:T(8,128)(2,1)S(1)}, u32[]{:S(2)}, u32[]{:S(2)}) collective-permute-start(bf16[32,8192]{1,0:T(8,128)(2,1)S(1)} %collective-permute-done.1.refs_2_), channel_id=1, source_target_pairs={{0,4},{1,5},{4,8},{5,9},{8,12},{9,13},{12,14},{13,15},{14,10},{15,... | collective-permute-start | bytes 1572872 | tf_op jit(solution)/shard_map/ppermute | solution.py:414
  35.5 15.3 %collective-permute-start.8 = (bf16[32,8192]{1,0:T(8,128)(2,1)S(1)}, bf16[32,8192]{1,0:T(8,128)(2,1)S(1)}, u32[]{:S(2)}, u32[]{:S(2)}) collective-permute-start(bf16[32,8192]{1,0:T(8,128)(2,1)S(1)} %collective-permute-done.2.refs_4_), channel_id=1, source_target_pairs={{4,0},{5,1},{8,4},{9,5},{12,8},{13,9},{14,12},{15,13},{10,14},{11,... | collective-permute-start | bytes 1572872 | tf_op jit(solution)/shard_map/ppermute | solution.py:415
  36.3 1.5 %collective-permute-start.11 = (bf16[16,8192]{1,0:T(8,128)(2,1)S(1)}, bf16[16,8192]{1,0:T(8,128)(2,1)S(1)}, u32[]{:S(2)}, u32[]{:S(2)}) collective-permute-start(bf16[16,8192]{1,0:T(8,128)(2,1)S(1)} %pad_maximum_fusion.refs_6_), channel_id=1, source_target_pairs={{0,1},{1,0},{2,3},{3,2},{4,5},{5,4},{6,7},{7,6},{8,9},{9,8},{10,11... | collective-permute-start | bytes 786440 | tf_op jit(solution)/shard_map/ppermute | solution.py:416
  41.9 9.0 %collective-permute-start.12 = (f32[32,1024]{1,0:T(8,128)S(1)}, f32[32,1024]{1,0:T(8,128)S(1)}, u32[]{:S(2)}, u32[]{:S(2)}) collective-permute-start(f32[32,1024]{1,0:T(8,128)S(1)} %get-tuple-element.75.refs_5_), channel_id=1, source_target_pairs={{0,16},{16,0},{1,17},{17,1},{2,18},{18,2},{3,19},{19,3},{4,20},{20... | collective-permute-start | bytes 393224 | tf_op jit(solution)/shard_map/ppermute | solution.py:419
  50.9 2.6 %collective-permute-start.15 = (bf16[32,8192]{1,0:T(8,128)(2,1)S(1)}, bf16[32,8192]{1,0:T(8,128)(2,1)S(1)}, u32[]{:S(2)}, u32[]{:S(2)}) collective-permute-start(bf16[32,8192]{1,0:T(8,128)(2,1)S(1)} %collective-permute-done.7.refs_0_), channel_id=1, source_target_pairs={{0,1},{1,0},{2,3},{3,2},{4,5},{5,4},{6,7},{7,6},{8,9},{9,8},{10,11... | collective-permute-start | bytes 1572872 | tf_op jit(solution)/shard_map/ppermute | solution.py:416
  50.9 2.6 %collective-permute-start.16 = (bf16[32,8192]{1,0:T(8,128)(2,1)S(1)}, bf16[32,8192]{1,0:T(8,128)(2,1)S(1)}, u32[]{:S(2)}, u32[]{:S(2)}) collective-permute-start(bf16[32,8192]{1,0:T(8,128)(2,1)S(1)} %collective-permute-done.8.refs_2_), channel_id=1, source_target_pairs={{0,1},{1,0},{2,3},{3,2},{4,5},{5,4},{6,7},{7,6},{8,9},{9,8},{10,11... | collective-permute-start | bytes 1572872 | tf_op jit(solution)/shard_map/ppermute | solution.py:416
  51.4 13.9 %collective-permute-start.13 = (bf16[32,8192]{1,0:T(8,128)(2,1)S(1)}, bf16[32,8192]{1,0:T(8,128)(2,1)S(1)}, u32[]{:S(2)}, u32[]{:S(2)}) collective-permute-start(bf16[32,8192]{1,0:T(8,128)(2,1)S(1)} %collective-permute-done.7.refs_0_), channel_id=1, source_target_pairs={{0,4},{1,5},{4,8},{5,9},{8,12},{9,13},{12,14},{13,15},{14,10},{15,... | collective-permute-start | bytes 1572872 | tf_op jit(solution)/shard_map/ppermute | solution.py:414
  53.0 13.6 %collective-permute-start.14 = (bf16[32,8192]{1,0:T(8,128)(2,1)S(1)}, bf16[32,8192]{1,0:T(8,128)(2,1)S(1)}, u32[]{:S(2)}, u32[]{:S(2)}) collective-permute-start(bf16[32,8192]{1,0:T(8,128)(2,1)S(1)} %collective-permute-done.8.refs_2_), channel_id=1, source_target_pairs={{4,0},{5,1},{8,4},{9,5},{12,8},{13,9},{14,12},{15,13},{10,14},{11,... | collective-permute-start | bytes 1572872 | tf_op jit(solution)/shard_map/ppermute | solution.py:415
  62.2 1.6 %collective-permute-start.17 = (bf16[16,8192]{1,0:T(8,128)(2,1)S(1)}, bf16[16,8192]{1,0:T(8,128)(2,1)S(1)}, u32[]{:S(2)}, u32[]{:S(2)}) collective-permute-start(bf16[16,8192]{1,0:T(8,128)(2,1)S(1)} %get-tuple-element.82), channel_id=1, source_target_pairs={{0,1},{1,0},{2,3},{3,2},{4,5},{5,4},{6,7},{7,6},{8,9},{9,8},{10,11... | collective-permute-start | bytes 786440 | tf_op jit(solution)/shard_map/ppermute | solution.py:416
  66.6 3.1 %collective-permute-start.19 = (bf16[32,8192]{1,0:T(8,128)(2,1)S(1)}, bf16[32,8192]{1,0:T(8,128)(2,1)S(1)}, u32[]{:S(2)}, u32[]{:S(2)}) collective-permute-start(bf16[32,8192]{1,0:T(8,128)(2,1)S(1)} %collective-permute-done.13.refs_0_), channel_id=1, source_target_pairs={{0,1},{1,0},{2,3},{3,2},{4,5},{5,4},{6,7},{7,6},{8,9},{9,8},{10,11... | collective-permute-start | bytes 1572872 | tf_op jit(solution)/shard_map/ppermute | solution.py:416
  66.6 4.0 %collective-permute-start.20 = (bf16[32,8192]{1,0:T(8,128)(2,1)S(1)}, bf16[32,8192]{1,0:T(8,128)(2,1)S(1)}, u32[]{:S(2)}, u32[]{:S(2)}) collective-permute-start(bf16[32,8192]{1,0:T(8,128)(2,1)S(1)} %collective-permute-done.14.refs_2_), channel_id=1, source_target_pairs={{0,1},{1,0},{2,3},{3,2},{4,5},{5,4},{6,7},{7,6},{8,9},{9,8},{10,11... | collective-permute-start | bytes 1572872 | tf_op jit(solution)/shard_map/ppermute | solution.py:416
  67.2 11.1 %collective-permute-start.21 = (bf16[16,8192]{1,0:T(8,128)(2,1)S(1)}, bf16[16,8192]{1,0:T(8,128)(2,1)S(1)}, u32[]{:S(2)}, u32[]{:S(2)}) collective-permute-start(bf16[16,8192]{1,0:T(8,128)(2,1)S(1)} %slice.22), channel_id=1, source_target_pairs={{0,4},{1,5},{4,8},{5,9},{8,12},{9,13},{12,14},{13,15},{14,10},{15,... | collective-permute-start | bytes 786440 | tf_op jit(solution)/shard_map/ppermute | solution.py:414
  67.5 10.8 %collective-permute-start.22 = (bf16[16,8192]{1,0:T(8,128)(2,1)S(1)}, bf16[16,8192]{1,0:T(8,128)(2,1)S(1)}, u32[]{:S(2)}, u32[]{:S(2)}) collective-permute-start(bf16[16,8192]{1,0:T(8,128)(2,1)S(1)} %slice.23), channel_id=1, source_target_pairs={{4,0},{5,1},{8,4},{9,5},{12,8},{13,9},{14,12},{15,13},{10,14},{11,... | collective-permute-start | bytes 786440 | tf_op jit(solution)/shard_map/ppermute | solution.py:415
  69.3 9.0 %collective-permute-start.18 = (bf16[8,8192]{1,0:T(8,128)(2,1)S(1)}, bf16[8,8192]{1,0:T(8,128)(2,1)S(1)}, u32[]{:S(2)}, u32[]{:S(2)}) collective-permute-start(bf16[8,8192]{1,0:T(8,128)(2,1)S(1)} %get-tuple-element.87), channel_id=1, source_target_pairs={{0,2},{1,3},{2,0},{3,1},{4,6},{5,7},{6,4},{7,5},{8,10},{9,11},{10,... | collective-permute-start | bytes 393224 | tf_op jit(solution)/shard_map/ppermute | solution.py:417
  69.7 8.6 %collective-permute-start.23 = (bf16[64,1024]{1,0:T(8,128)(2,1)S(1)}, bf16[64,1024]{1,0:T(8,128)(2,1)S(1)}, u32[]{:S(2)}, u32[]{:S(2)}) collective-permute-start(bf16[64,1024]{1,0:T(8,128)(2,1)S(1)} %get-tuple-element.94), channel_id=1, source_target_pairs={{0,16},{16,0},{1,17},{17,1},{2,18},{18,2},{3,19},{19,3},{4,20},{20... | collective-permute-start | bytes 393224 | tf_op jit(solution)/shard_map/ppermute | solution.py:419
  78.4 3.6 %collective-permute-start.24 = (bf16[16,8192]{1,0:T(8,128)(2,1)S(1)}, bf16[16,8192]{1,0:T(8,128)(2,1)S(1)}, u32[]{:S(2)}, u32[]{:S(2)}) collective-permute-start(bf16[16,8192]{1,0:T(8,128)(2,1)S(1)} %collective-permute-done.21.refs_0_), channel_id=1, source_target_pairs={{0,1},{1,0},{2,3},{3,2},{4,5},{5,4},{6,7},{7,6},{8,9},{9,8},{10,11... | collective-permute-start | bytes 786440 | tf_op jit(solution)/shard_map/ppermute | solution.py:416
  78.4 5.4 %collective-permute-start.25 = (bf16[16,8192]{1,0:T(8,128)(2,1)S(1)}, bf16[16,8192]{1,0:T(8,128)(2,1)S(1)}, u32[]{:S(2)}, u32[]{:S(2)}) collective-permute-start(bf16[16,8192]{1,0:T(8,128)(2,1)S(1)} %collective-permute-done.22.refs_1_), channel_id=1, source_target_pairs={{0,1},{1,0},{2,3},{3,2},{4,5},{5,4},{6,7},{7,6},{8,9},{9,8},{10,11... | collective-permute-start | bytes 786440 | tf_op jit(solution)/shard_map/ppermute | solution.py:416
  78.9 9.5 %collective-permute-start.26 = (bf16[128,1024]{1,0:T(8,128)(2,1)S(1)}, bf16[128,1024]{1,0:T(8,128)(2,1)S(1)}, u32[]{:S(2)}, u32[]{:S(2)}) collective-permute-start(bf16[128,1024]{1,0:T(8,128)(2,1)S(1)} %get-tuple-element.101), channel_id=1, source_target_pairs={{0,16},{16,0},{1,17},{17,1},{2,18},{18,2},{3,19},{19,3},{4,20},{20... | collective-permute-start | bytes 786440 | tf_op jit(solution)/shard_map/ppermute | solution.py:419
  79.5 9.0 %collective-permute-start.27 = (bf16[2,8192]{1,0:T(2,128)(2,1)S(1)}, bf16[2,8192]{1,0:T(2,128)(2,1)S(1)}, u32[]{:S(2)}, u32[]{:S(2)}) collective-permute-start(bf16[2,8192]{1,0:T(2,128)(2,1)S(1)} %get-tuple-element.102), channel_id=1, source_target_pairs={{0,4},{1,5},{2,6},{3,7},{4,0},{5,1},{6,2},{7,3},{8,12},{9,13},{10,... | collective-permute-start | bytes 98312 | tf_op jit(solution)/shard_map/ppermute | solution.py:418
  79.5 9.0 %collective-permute-start.28 = (bf16[2,8192]{1,0:T(2,128)(2,1)S(1)}, bf16[2,8192]{1,0:T(2,128)(2,1)S(1)}, u32[]{:S(2)}, u32[]{:S(2)}) collective-permute-start(bf16[2,8192]{1,0:T(2,128)(2,1)S(1)} %get-tuple-element.103), channel_id=1, source_target_pairs={{0,8},{1,9},{2,10},{3,11},{4,12},{5,13},{6,14},{7,15},{8,0},{9,1},... | collective-permute-start | bytes 98312 | tf_op jit(solution)/shard_map/ppermute | solution.py:418
  82.0 6.5 %collective-permute-start.29 = (bf16[2,8192]{1,0:T(2,128)(2,1)S(1)}, bf16[2,8192]{1,0:T(2,128)(2,1)S(1)}, u32[]{:S(2)}, u32[]{:S(2)}) collective-permute-start(bf16[2,8192]{1,0:T(2,128)(2,1)S(1)} %get-tuple-element.104), channel_id=1, source_target_pairs={{0,12},{1,13},{2,14},{3,15},{4,8},{5,9},{6,10},{7,11},{8,4},{9,5},... | collective-permute-start | bytes 98312 | tf_op jit(solution)/shard_map/ppermute | solution.py:418
  86.9 5.0 %collective-permute-start.31 = (bf16[64,1024]{1,0:T(8,128)(2,1)S(1)}, bf16[64,1024]{1,0:T(8,128)(2,1)S(1)}, u32[]{:S(2)}, u32[]{:S(2)}) collective-permute-start(bf16[64,1024]{1,0:T(8,128)(2,1)S(1)} %get-tuple-element.113), channel_id=1, source_target_pairs={{0,16},{16,0},{1,17},{17,1},{2,18},{18,2},{3,19},{19,3},{4,20},{20... | collective-permute-start | bytes 393224 | tf_op jit(solution)/shard_map/ppermute | solution.py:419
  88.7 4.2 %collective-permute-start.30 = (f32[2,1]{0,1:T(1,128)S(1)}, f32[2,1]{0,1:T(1,128)S(1)}, u32[]{:S(2)}, u32[]{:S(2)}) collective-permute-start(f32[2,1]{0,1:T(1,128)S(1)} %bitcast.17), channel_id=1, source_target_pairs={{0,16},{16,0},{1,17},{17,1},{2,18},{18,2},{3,19},{19,3},{4,20},{20... | collective-permute-start | bytes 32 | tf_op jit(solution)/shard_map/ppermute | solution.py:419
  (8 other events, 186.2 us)

commit v3 on v2

--- a/solution.py
+++ b/solution.py
@@ -85,8 +85,8 @@
         copies[0].wait()
         up = lax.broadcasted_iota(jnp.int32, (TREE, TREE), 0)
         node = lax.broadcasted_iota(jnp.int32, (TREE, TREE), 1)
-        spread = lax.broadcasted_iota(jnp.int32, (GROUP * TREE, TREE), 0) % TREE
-        spread = spread == lax.broadcasted_iota(jnp.int32, (GROUP * TREE, TREE), 1)
+        spread = lax.broadcasted_iota(jnp.int32, (TREE, GROUP * TREE), 1) % TREE
+        spread = spread == lax.broadcasted_iota(jnp.int32, (TREE, GROUP * TREE), 0)
         spread = jnp.where(spread, 1.0, 0.0).astype(BF)
         dims = (((1,), (1,)), ((), ()))
         seen = []
@@ -95,11 +95,11 @@
             for _ in range(4):
                 paths = jnp.dot(reach, reach, preferred_element_type=F32)
                 reach = jnp.minimum(paths, 1.0).astype(BF)
-            seen.append(lax.dot_general(spread, reach, dims, preferred_element_type=F32) > 0.5)
+            seen.append(jnp.dot(reach, spread, preferred_element_type=F32) > 0.5)
         for c in copies[1:6]:
             c.wait()
         for b in range(count):
-            live = lax.broadcasted_iota(jnp.int32, (1, cache), 1) < len_ref[b]
+            live = lax.broadcasted_iota(jnp.int32, (cache, 1), 0) < len_ref[b]
             chosen = lax.broadcasted_iota(jnp.int32, (TREE, 1), 0) == last_ref[first + b]
             for g in range(groups):
                 head = slice(g * HEAD, (g + 1) * HEAD)
@@ -108,23 +108,28 @@
                     [q_ref[b, :, base + h * HEAD : base + (h + 1) * HEAD] for h in range(GROUP)],
                     axis=0,
                 )
-                s_cache = lax.dot_general(q, ck_ref[b, :, head], dims, preferred_element_type=F32)
-                s_tree = lax.dot_general(q, tk_ref[b, :, head], dims, preferred_element_type=F32)
+                s_cache = lax.dot_general(ck_ref[b, :, head], q, dims, preferred_element_type=F32)
+                s_tree = lax.dot_general(tk_ref[b, :, head], q, dims, preferred_element_type=F32)
                 s_cache = jnp.where(live, s_cache * FACTOR, -1e30)
                 s_tree = jnp.where(seen[b], s_tree * FACTOR, -1e30)
                 top = jnp.maximum(
-                    jnp.max(s_cache, axis=1, keepdims=True), jnp.max(s_tree, axis=1, keepdims=True)
+                    jnp.max(s_cache, axis=0, keepdims=True), jnp.max(s_tree, axis=0, keepdims=True)
                 )
                 e_cache = jnp.exp(s_cache - top)
                 e_tree = jnp.exp(s_tree - top)
-                total = jnp.sum(e_cache, axis=1, keepdims=True) + jnp.sum(
-                    e_tree, axis=1, keepdims=True
+                total = jnp.sum(e_cache, axis=0, keepdims=True) + jnp.sum(
+                    e_tree, axis=0, keepdims=True
                 )
                 inverse = 1.0 / total
                 w_cache = (e_cache * inverse).astype(BF)
                 w_tree = (e_tree * inverse).astype(BF)
-                mixed = jnp.dot(w_cache, cv_ref[b, :, head], preferred_element_type=F32)
-                mixed = mixed + jnp.dot(w_tree, tv_ref[b, :, head], preferred_element_type=F32)
+                over = (((0,), (0,)), ((), ()))
+                mixed = lax.dot_general(
+                    w_cache, cv_ref[b, :, head], over, preferred_element_type=F32
+                )
+                mixed = mixed + lax.dot_general(
+                    w_tree, tv_ref[b, :, head], over, preferred_element_type=F32
+                )
                 for h in range(GROUP):
                     block = mixed[h * TREE : (h + 1) * TREE]
                     where = slice(base + h * HEAD, base + (h + 1) * HEAD)
@@ -519,10 +524,10 @@
     gots = [swap_z(v, k) for k, v in enumerate(sends, 1)]
 
     def finish_4(total, more, results):
-        split_pairs([3], [more[0][:two]], [total[...]], *results)
+        split_pairs([3], [more[0][:two]], [total[:two]], *results)
 
     keep_4, send_4 = project(
-        "project_4", [f4, b4, f4s, b4s], out_proj, [part_a], finish_4,
+        "project_4", [f4, b4, f4s, b4s, f4, b4, f4s, b4s], out_proj, [part_a], finish_4,
         [f32(two, columns), bf16(two, columns)],
     )
     got_4 = swap_side(send_4)

time: 93.9 us -> 92.6 us (0.986)
  Pallas kernels: 42.5 us -> 41.3 us
  transfers between devices with their start and end apart: 32 -> 32, of which waited for: 10 -> 10; matrix products, arithmetic and copies ran while one was open for 1% -> 1% of each run, Pallas kernels for 38% -> 37%
where the time goes in v3:
time: 92.6 us; the launch traced here: 92.4 us
  Pallas kernels  41.3 us (45%)
  starting transfers between devices  30 us (32%)
  waiting for transfers between devices  17.4 us (19%)
  other arithmetic  1.83 us (2%)
  between operations  0.98 us (1%)
  local copies, waits for them, and re-layouts  0.97 us (1%)
    pallas_call x2, Pallas kernels, join_layer(): pl.pallas_call(kernel, grid=(steps,), in_specs=specs, out_specs=[pl.Block...  16.2 us
    ppermute x5, starting transfers between devices, ring_body(): lax.ppermute(v, 'request', [(r, r ^ 4 * k) for r in range(size)])  10.6 us
    pallas_call x3, Pallas kernels, project(): pl.pallas_call(kernel, in_specs=[VMEM] * (n + 1 + m), out_specs=[VMEM] *...  8.64 us
    pallas_call x1, Pallas kernels, project_and_join(): pl.pallas_call(kernel, in_specs=[VMEM] * (n + 4) + [HBM], out_specs=[VMEM...  8.56 us
    ppermute x6, starting transfers between devices, ring_body(): swap_side = lambda v: lax.ppermute(v, 'tensor', [(0, 1), (1, 0)])  6.88 us
    pallas_call x1, Pallas kernels, attention(): pl.pallas_call(kernel, in_specs=in_specs, out_specs=[VMEM] * len(outs), o...  6.79 us
    ppermute x2, waiting for transfers between devices, ring_body(): lax.ppermute(v, 'request', [(r, r ^ 2) for r in range(size)])  5.69 us
    ppermute x4, starting transfers between devices, ring_body(): ahead = lambda v: lax.ppermute(v, 'request', forward)  4.72 us
  transfers between devices with their start and end apart: 32, of which 10 were waited for; matrix products, arithmetic and copies ran while one was open for 1% of the time, Pallas kernels for 37%

profile of v3, /device:TPU:0, one launch (start us, length us, event | category | flops | bytes accessed | tf_op | source)
XLA Modules:
  0.0 92.4 jit_solution(9480411468973443936)
XLA Ops:
  0.6 6.8 %attention.1 = (bf16[32,8192]{1,0:T(8,128)(2,1)}, bf16[2,8192]{1,0:T(2,128)(2,1)}, bf16[64,1024]{1,0:T(8,128)(2,1)}, f32[32,1024]{1,0:T(8,128)}) custom-call(s32[2]{0:T(128)} %len_ref.1, s32[32]{0:T(128)} %last_ref.1, s32[2,16]{1,0:T(2,128)} %refs_0_.1, bf16[2,16,8192]{2,1,0:T(8,128)(2,1)} %refs_1_.1, bf16[2,256,512]{2,1,0:T(8,128)(2,1)} %refs_2_.3, ...), custom_call_target="tpu_custom_call" | custom-call | flops 1 | bytes 1 | tf_op jit(solution)/shard_map/attention/pallas_call | solution.py:177
  7.4 3.1 %collective-permute-start = (bf16[2,8192]{1,0:T(2,128)(2,1)}, bf16[2,8192]{1,0:T(2,128)(2,1)S(1)}, u32[]{:S(2)}, u32[]{:S(2)}) collective-permute-start(bf16[2,8192]{1,0:T(2,128)(2,1)} %get-tuple-element.60), channel_id=1, source_target_pairs={{0,4},{1,5},{2,6},{3,7},{4,0},{5,1},{6,2},{7,3},{8,12},{9,13},{10,... | collective-permute-start | bytes 98312 | tf_op jit(solution)/shard_map/ppermute | solution.py:423
  10.5 2.1 %collective-permute-done = bf16[2,8192]{1,0:T(2,128)(2,1)S(1)} collective-permute-done((bf16[2,8192]{1,0:T(2,128)(2,1)}, bf16[2,8192]{1,0:T(2,128)(2,1)S(1)}, u32[]{:S(2)}, u32[]{:S(2)}) %collective-permute-start) | collective-permute-done | bytes 32800 | tf_op jit(solution)/shard_map/ppermute | solution.py:423
  12.6 0.8 pad_maximum_fusion.2
  13.5 3.1 %collective-permute-start.5 = (bf16[4,8192]{1,0:T(4,128)(2,1)S(1)}, bf16[4,8192]{1,0:T(4,128)(2,1)S(1)}, u32[]{:S(2)}, u32[]{:S(2)}) collective-permute-start(bf16[4,8192]{1,0:T(4,128)(2,1)S(1)} %pad_maximum_fusion.2), channel_id=1, source_target_pairs={{0,8},{1,9},{2,10},{3,11},{4,12},{5,13},{6,14},{7,15},{8,0},{9,1},... | collective-permute-start | bytes 196616 | tf_op jit(solution)/shard_map/ppermute | solution.py:423
  16.6 1.5 %collective-permute-start.4 = (bf16[64,1024]{1,0:T(8,128)(2,1)}, bf16[64,1024]{1,0:T(8,128)(2,1)S(1)}, u32[]{:S(2)}, u32[]{:S(2)}) collective-permute-start(bf16[64,1024]{1,0:T(8,128)(2,1)} %get-tuple-element.65), channel_id=1, source_target_pairs={{0,16},{16,0},{1,17},{17,1},{2,18},{18,2},{3,19},{19,3},{4,20},{20... | collective-permute-start | bytes 393224 | tf_op jit(solution)/shard_map/ppermute | solution.py:424
  18.1 1.6 %collective-permute-start.1 = (bf16[32,8192]{1,0:T(8,128)(2,1)}, bf16[32,8192]{1,0:T(8,128)(2,1)S(1)}, u32[]{:S(2)}, u32[]{:S(2)}) collective-permute-start(bf16[32,8192]{1,0:T(8,128)(2,1)} %get-tuple-element.61.refs_0_), channel_id=1, source_target_pairs={{0,4},{1,5},{4,8},{5,9},{8,12},{9,13},{12,14},{13,15},{14,10},{15,... | collective-permute-start | bytes 1572872 | tf_op jit(solution)/shard_map/ppermute | solution.py:419
  20.2 1.6 %collective-permute-done.4 = bf16[64,1024]{1,0:T(8,128)(2,1)S(1)} collective-permute-done((bf16[64,1024]{1,0:T(8,128)(2,1)}, bf16[64,1024]{1,0:T(8,128)(2,1)S(1)}, u32[]{:S(2)}, u32[]{:S(2)}) %collective-permute-start.4) | collective-permute-done | bytes 131104 | tf_op jit(solution)/shard_map/ppermute | solution.py:424
  21.8 1.5 %collective-permute-start.6 = (bf16[8,8192]{1,0:T(8,128)(2,1)S(1)}, bf16[8,8192]{1,0:T(8,128)(2,1)S(1)}, u32[]{:S(2)}, u32[]{:S(2)}) collective-permute-start(bf16[8,8192]{1,0:T(8,128)(2,1)S(1)} %pad_maximum_fusion.1), channel_id=1, source_target_pairs={{0,2},{1,3},{2,0},{3,1},{4,6},{5,7},{6,4},{7,5},{8,10},{9,11},{10,... | collective-permute-start | bytes 393224 | tf_op jit(solution)/shard_map/ppermute | solution.py:422
  23.2 0.9 fusion
  24.2 8.5 %join_low.1.refs_4_ = f32[32,8192]{1,0:T(8,128)S(1)} custom-call(bf16[32,1024]{1,0:T(8,128)(2,1)S(1)} %get-tuple-element.120.refs_0_, bf16[32,1024]{1,0:T(8,128)(2,1)S(1)} %get-tuple-element.117.refs_1_, bf16[3,1024,8192]{2,1,0:T(8,128)(2,1)} %refs_8_.4, bf16[3,1024,8192]{2,1,0:T(8,128)(2,1)} %refs_8_.4), custom_call_target="tpu_custom_call" | custom-call | flops 1 | bytes 1 | tf_op jit(solution)/shard_map/join_low/pallas_call | solution.py:262
  33.7 1.2 %collective-permute-start.7 = (bf16[32,8192]{1,0:T(8,128)(2,1)S(1)}, bf16[32,8192]{1,0:T(8,128)(2,1)S(1)}, u32[]{:S(2)}, u32[]{:S(2)}) collective-permute-start(bf16[32,8192]{1,0:T(8,128)(2,1)S(1)} %collective-permute-done.1.refs_2_), channel_id=1, source_target_pairs={{0,4},{1,5},{4,8},{5,9},{8,12},{9,13},{12,14},{13,15},{14,10},{15,... | collective-permute-start | bytes 1572872 | tf_op jit(solution)/shard_map/ppermute | solution.py:419
  35.7 1.5 %collective-permute-done.11.refs_7_ = bf16[16,8192]{1,0:T(8,128)(2,1)S(1)} collective-permute-done((bf16[16,8192]{1,0:T(8,128)(2,1)S(1)}, bf16[16,8192]{1,0:T(8,128)(2,1)S(1)}, u32[]{:S(2)}, u32[]{:S(2)}) %collective-permute-start.11) | collective-permute-done | bytes 262176 | tf_op jit(solution)/shard_map/ppermute | solution.py:421
  37.3 3.9 %project_a.1 = (f32[192,1024]{1,0:T(8,128)S(1)}, f32[32,1024]{1,0:T(8,128)S(1)}) custom-call(bf16[32,8192]{1,0:T(8,128)(2,1)S(1)} %copy-done.1, bf16[32,8192]{1,0:T(8,128)(2,1)S(1)} %collective-permute-done.3.refs_1_, bf16[32,8192]{1,0:T(8,128)(2,1)S(1)} %collective-permute-done.1.refs_2_, bf16[32,8192]{1,0:T(8,128)(2,1)S(1)} %collective-permute-done.9.refs_3_, ...), custom_call_target="tpu_custom_call" | custom-call | flops 1 | bytes 1 | tf_op jit(solution)/shard_map/project_a/pallas_call | solution.py:208
  41.3 1.2 %collective-permute-start.12 = (f32[32,1024]{1,0:T(8,128)S(1)}, f32[32,1024]{1,0:T(8,128)S(1)}, u32[]{:S(2)}, u32[]{:S(2)}) collective-permute-start(f32[32,1024]{1,0:T(8,128)S(1)} %get-tuple-element.75.refs_5_), channel_id=1, source_target_pairs={{0,16},{16,0},{1,17},{17,1},{2,18},{18,2},{3,19},{19,3},{4,20},{20... | collective-permute-start | bytes 393224 | tf_op jit(solution)/shard_map/ppermute | solution.py:424
  42.5 7.7 %join_mid.1.refs_7_ = f32[32,8192]{1,0:T(8,128)S(1)} custom-call(bf16[32,1024]{1,0:T(8,128)(2,1)S(1)} %get-tuple-element.121.refs_0_, bf16[32,1024]{1,0:T(8,128)(2,1)S(1)} %get-tuple-element.116.refs_1_, bf16[3,1024,8192]{2,1,0:T(8,128)(2,1)} %refs_8_.4, bf16[3,1024,8192]{2,1,0:T(8,128)(2,1)} %refs_8_.4, f32[32,8192]{1,0:T(8,128)S(1)} %join_low.1.refs_4_), custom_call_target="tpu_custom_call" | custom-call | flops 1 | bytes 1 | tf_op jit(solution)/shard_map/join_mid/pallas_call | solution.py:262
  50.8 1.6 %collective-permute-start.13 = (bf16[32,8192]{1,0:T(8,128)(2,1)S(1)}, bf16[32,8192]{1,0:T(8,128)(2,1)S(1)}, u32[]{:S(2)}, u32[]{:S(2)}) collective-permute-start(bf16[32,8192]{1,0:T(8,128)(2,1)S(1)} %collective-permute-done.7.refs_0_), channel_id=1, source_target_pairs={{0,4},{1,5},{4,8},{5,9},{8,12},{9,13},{12,14},{13,15},{14,10},{15,... | collective-permute-start | bytes 1572872 | tf_op jit(solution)/shard_map/ppermute | solution.py:419
  53.0 8.6 %project_2_join_hidden.1 = (f32[64,1024]{1,0:T(8,128)S(1)}, bf16[64,1024]{1,0:T(8,128)(2,1)S(1)}, f32[16,8192]{1,0:T(8,128)S(1)}, bf16[16,8192]{1,0:T(8,128)(2,1)S(1)}) custom-call(bf16[32,8192]{1,0:T(8,128)(2,1)S(1)} %collective-permute-done.7.refs_0_, bf16[32,8192]{1,0:T(8,128)(2,1)S(1)} %collective-permute-done.15.refs_1_, ...), custom_call_target="tpu_custom_call" | custom-call | flops 1 | bytes 1 | tf_op jit(solution)/shard_map/project_2_join_hidden/pallas_call | solution.py:309
  61.8 1.4 %collective-permute-done.17.g_ref = bf16[16,8192]{1,0:T(8,128)(2,1)S(1)} collective-permute-done((bf16[16,8192]{1,0:T(8,128)(2,1)S(1)}, bf16[16,8192]{1,0:T(8,128)(2,1)S(1)}, u32[]{:S(2)}, u32[]{:S(2)}) %collective-permute-start.17) | collective-permute-done | bytes 262176 | tf_op jit(solution)/shard_map/ppermute | solution.py:421
  63.2 1.5 %collective-permute-done.13.refs_0_ = bf16[32,8192]{1,0:T(8,128)(2,1)S(1)} collective-permute-done((bf16[32,8192]{1,0:T(8,128)(2,1)S(1)}, bf16[32,8192]{1,0:T(8,128)(2,1)S(1)}, u32[]{:S(2)}, u32[]{:S(2)}) %collective-permute-start.13) | collective-permute-done | bytes 524320 | tf_op jit(solution)/shard_map/ppermute | solution.py:419
  64.7 1.3 %collective-permute-done.14.refs_2_ = bf16[32,8192]{1,0:T(8,128)(2,1)S(1)} collective-permute-done((bf16[32,8192]{1,0:T(8,128)(2,1)S(1)}, bf16[32,8192]{1,0:T(8,128)(2,1)S(1)}, u32[]{:S(2)}, u32[]{:S(2)}) %collective-permute-start.14) | collective-permute-done | bytes 524320 | tf_op jit(solution)/shard_map/ppermute | solution.py:420
  66.9 1.7 %collective-permute-start.22 = (bf16[16,8192]{1,0:T(8,128)(2,1)S(1)}, bf16[16,8192]{1,0:T(8,128)(2,1)S(1)}, u32[]{:S(2)}, u32[]{:S(2)}) collective-permute-start(bf16[16,8192]{1,0:T(8,128)(2,1)S(1)} %slice.23), channel_id=1, source_target_pairs={{4,0},{5,1},{8,4},{9,5},{12,8},{13,9},{14,12},{15,13},{10,14},{11,... | collective-permute-start | bytes 786440 | tf_op jit(solution)/shard_map/ppermute | solution.py:420
  69.1 0.9 collective-permute-start.23
  70.0 2.3 %project_3.1 = (f32[128,1024]{1,0:T(8,128)S(1)}, bf16[128,1024]{1,0:T(8,128)(2,1)S(1)}) custom-call(bf16[32,8192]{1,0:T(8,128)(2,1)S(1)} %collective-permute-done.13.refs_0_, bf16[32,8192]{1,0:T(8,128)(2,1)S(1)} %collective-permute-done.19.refs_1_, bf16[32,8192]{1,0:T(8,128)(2,1)S(1)} %collective-permute-done.14.refs_2_, ...), custom_call_target="tpu_custom_call" | custom-call | flops 1 | bytes 1 | tf_op jit(solution)/shard_map/project_3/pallas_call | solution.py:208
  72.3 5.3 %collective-permute-done.18.g_ref = bf16[8,8192]{1,0:T(8,128)(2,1)S(1)} collective-permute-done((bf16[8,8192]{1,0:T(8,128)(2,1)S(1)}, bf16[8,8192]{1,0:T(8,128)(2,1)S(1)}, u32[]{:S(2)}, u32[]{:S(2)}) %collective-permute-start.18) | collective-permute-done | bytes 131104 | tf_op jit(solution)/shard_map/ppermute | solution.py:422
  78.8 2.5 %collective-permute-start.28 = (bf16[2,8192]{1,0:T(2,128)(2,1)S(1)}, bf16[2,8192]{1,0:T(2,128)(2,1)S(1)}, u32[]{:S(2)}, u32[]{:S(2)}) collective-permute-start(bf16[2,8192]{1,0:T(2,128)(2,1)S(1)} %get-tuple-element.103), channel_id=1, source_target_pairs={{0,8},{1,9},{2,10},{3,11},{4,12},{5,13},{6,14},{7,15},{8,0},{9,1},... | collective-permute-start | bytes 98312 | tf_op jit(solution)/shard_map/ppermute | solution.py:423
  81.4 1.9 %collective-permute-start.29 = (bf16[2,8192]{1,0:T(2,128)(2,1)S(1)}, bf16[2,8192]{1,0:T(2,128)(2,1)S(1)}, u32[]{:S(2)}, u32[]{:S(2)}) collective-permute-start(bf16[2,8192]{1,0:T(2,128)(2,1)S(1)} %get-tuple-element.104), channel_id=1, source_target_pairs={{0,12},{1,13},{2,14},{3,15},{4,8},{5,9},{6,10},{7,11},{8,4},{9,5},... | collective-permute-start | bytes 98312 | tf_op jit(solution)/shard_map/ppermute | solution.py:423
  83.2 2.4 %project_4.1 = (f32[64,1024]{1,0:T(8,128)S(1)}, bf16[64,1024]{1,0:T(8,128)(2,1)S(1)}) custom-call(bf16[16,8192]{1,0:T(8,128)(2,1)S(1)} %collective-permute-done.21.refs_0_.refs_4_, bf16[16,8192]{1,0:T(8,128)(2,1)S(1)} %collective-permute-done.22.refs_1_.refs_5_, bf16[16,8192]{1,0:T(8,128)(2,1)S(1)} %collective-permute-done.24.refs_2_.refs_6_, ...), custom_call_target="tpu_custom_call" | custom-call | flops 1 | bytes 1 | tf_op jit(solution)/shard_map/project_4/pallas_call | solution.py:208
  85.6 1.6 %collective-permute-start.31 = (bf16[64,1024]{1,0:T(8,128)(2,1)S(1)}, bf16[64,1024]{1,0:T(8,128)(2,1)S(1)}, u32[]{:S(2)}, u32[]{:S(2)}) collective-permute-start(bf16[64,1024]{1,0:T(8,128)(2,1)S(1)} %get-tuple-element.113), channel_id=1, source_target_pairs={{0,16},{16,0},{1,17},{17,1},{2,18},{18,2},{3,19},{19,3},{4,20},{20... | collective-permute-start | bytes 393224 | tf_op jit(solution)/shard_map/ppermute | solution.py:424
  87.4 1.2 %collective-permute-start.30 = (f32[2,1]{0,1:T(1,128)S(1)}, f32[2,1]{0,1:T(1,128)S(1)}, u32[]{:S(2)}, u32[]{:S(2)}) collective-permute-start(f32[2,1]{0,1:T(1,128)S(1)} %bitcast.17), channel_id=1, source_target_pairs={{0,16},{16,0},{1,17},{17,1},{2,18},{18,2},{3,19},{19,3},{4,20},{20... | collective-permute-start | bytes 32 | tf_op jit(solution)/shard_map/ppermute | solution.py:424
  88.6 2.1 %collective-permute-done.31.refs_5_ = bf16[64,1024]{1,0:T(8,128)(2,1)S(1)} collective-permute-done((bf16[64,1024]{1,0:T(8,128)(2,1)S(1)}, bf16[64,1024]{1,0:T(8,128)(2,1)S(1)}, u32[]{:S(2)}, u32[]{:S(2)}) %collective-permute-start.31) | collective-permute-done | bytes 131104 | tf_op jit(solution)/shard_map/ppermute | solution.py:424
  90.6 1.0 %finish_hidden.1 = bf16[256,1024]{1,0:T(8,128)(2,1)} custom-call(bf16[256,1024]{1,0:T(8,128)(2,1)S(1)} %bitcast.12, f32[64,1024]{1,0:T(8,128)S(1)} %get-tuple-element.108.refs_0_, f32[128,1024]{1,0:T(8,128)S(1)} %get-tuple-element.109.refs_1_, f32[64,1024]{1,0:T(8,128)S(1)} %get-tuple-element.110.refs_2_, ...), custom_call_target="tpu_custom_call" | custom-call | flops 1 | bytes 1 | tf_op jit(solution)/shard_map/finish_hidden/pallas_call | solution.py:355
  (68 shorter events, 7.1 us)
Async XLA Ops:
  7.4 5.2 %collective-permute-start = (bf16[2,8192]{1,0:T(2,128)(2,1)}, bf16[2,8192]{1,0:T(2,128)(2,1)S(1)}, u32[]{:S(2)}, u32[]{:S(2)}) collective-permute-start(bf16[2,8192]{1,0:T(2,128)(2,1)} %get-tuple-element.60), channel_id=1, source_target_pairs={{0,4},{1,5},{2,6},{3,7},{4,0},{5,1},{6,2},{7,3},{8,12},{9,13},{10,... | collective-permute-start | bytes 98312 | tf_op jit(solution)/shard_map/ppermute | solution.py:423
  13.5 6.7 %collective-permute-start.5 = (bf16[4,8192]{1,0:T(4,128)(2,1)S(1)}, bf16[4,8192]{1,0:T(4,128)(2,1)S(1)}, u32[]{:S(2)}, u32[]{:S(2)}) collective-permute-start(bf16[4,8192]{1,0:T(4,128)(2,1)S(1)} %pad_maximum_fusion.2), channel_id=1, source_target_pairs={{0,8},{1,9},{2,10},{3,11},{4,12},{5,13},{6,14},{7,15},{8,0},{9,1},... | collective-permute-start | bytes 196616 | tf_op jit(solution)/shard_map/ppermute | solution.py:423
  16.6 5.2 %collective-permute-start.4 = (bf16[64,1024]{1,0:T(8,128)(2,1)}, bf16[64,1024]{1,0:T(8,128)(2,1)S(1)}, u32[]{:S(2)}, u32[]{:S(2)}) collective-permute-start(bf16[64,1024]{1,0:T(8,128)(2,1)} %get-tuple-element.65), channel_id=1, source_target_pairs={{0,16},{16,0},{1,17},{17,1},{2,18},{18,2},{3,19},{19,3},{4,20},{20... | collective-permute-start | bytes 393224 | tf_op jit(solution)/shard_map/ppermute | solution.py:424
  18.1 15.0 %collective-permute-start.1 = (bf16[32,8192]{1,0:T(8,128)(2,1)}, bf16[32,8192]{1,0:T(8,128)(2,1)S(1)}, u32[]{:S(2)}, u32[]{:S(2)}) collective-permute-start(bf16[32,8192]{1,0:T(8,128)(2,1)} %get-tuple-element.61.refs_0_), channel_id=1, source_target_pairs={{0,4},{1,5},{4,8},{5,9},{8,12},{9,13},{12,14},{13,15},{14,10},{15,... | collective-permute-start | bytes 1572872 | tf_op jit(solution)/shard_map/ppermute | solution.py:419
  19.7 13.4 %collective-permute-start.2 = (bf16[32,8192]{1,0:T(8,128)(2,1)}, bf16[32,8192]{1,0:T(8,128)(2,1)S(1)}, u32[]{:S(2)}, u32[]{:S(2)}) collective-permute-start(bf16[32,8192]{1,0:T(8,128)(2,1)} %get-tuple-element.61.refs_0_), channel_id=1, source_target_pairs={{4,0},{5,1},{8,4},{9,5},{12,8},{13,9},{14,12},{15,13},{10,14},{11,... | collective-permute-start | bytes 1572872 | tf_op jit(solution)/shard_map/ppermute | solution.py:420
  20.1 13.0 %collective-permute-start.3 = (bf16[32,8192]{1,0:T(8,128)(2,1)}, bf16[32,8192]{1,0:T(8,128)(2,1)S(1)}, u32[]{:S(2)}, u32[]{:S(2)}) collective-permute-start(bf16[32,8192]{1,0:T(8,128)(2,1)} %get-tuple-element.61.refs_0_), channel_id=1, source_target_pairs={{0,1},{1,0},{2,3},{3,2},{4,5},{5,4},{6,7},{7,6},{8,9},{9,8},{10,11... | collective-permute-start | bytes 1572872 | tf_op jit(solution)/shard_map/ppermute | solution.py:421
  21.8 11.3 %collective-permute-start.6 = (bf16[8,8192]{1,0:T(8,128)(2,1)S(1)}, bf16[8,8192]{1,0:T(8,128)(2,1)S(1)}, u32[]{:S(2)}, u32[]{:S(2)}) collective-permute-start(bf16[8,8192]{1,0:T(8,128)(2,1)S(1)} %pad_maximum_fusion.1), channel_id=1, source_target_pairs={{0,2},{1,3},{2,0},{3,1},{4,6},{5,7},{6,4},{7,5},{8,10},{9,11},{10,... | collective-permute-start | bytes 393224 | tf_op jit(solution)/shard_map/ppermute | solution.py:422
  33.1 4.1 %collective-permute-start.10 = (bf16[32,8192]{1,0:T(8,128)(2,1)S(1)}, bf16[32,8192]{1,0:T(8,128)(2,1)S(1)}, u32[]{:S(2)}, u32[]{:S(2)}) collective-permute-start(bf16[32,8192]{1,0:T(8,128)(2,1)S(1)} %collective-permute-done.2.refs_4_), channel_id=1, source_target_pairs={{0,1},{1,0},{2,3},{3,2},{4,5},{5,4},{6,7},{7,6},{8,9},{9,8},{10,11... | collective-permute-start | bytes 1572872 | tf_op jit(solution)/shard_map/ppermute | solution.py:421
  33.2 4.1 %collective-permute-start.9 = (bf16[32,8192]{1,0:T(8,128)(2,1)S(1)}, bf16[32,8192]{1,0:T(8,128)(2,1)S(1)}, u32[]{:S(2)}, u32[]{:S(2)}) collective-permute-start(bf16[32,8192]{1,0:T(8,128)(2,1)S(1)} %collective-permute-done.1.refs_2_), channel_id=1, source_target_pairs={{0,1},{1,0},{2,3},{3,2},{4,5},{5,4},{6,7},{7,6},{8,9},{9,8},{10,11... | collective-permute-start | bytes 1572872 | tf_op jit(solution)/shard_map/ppermute | solution.py:421
  33.7 16.5 %collective-permute-start.7 = (bf16[32,8192]{1,0:T(8,128)(2,1)S(1)}, bf16[32,8192]{1,0:T(8,128)(2,1)S(1)}, u32[]{:S(2)}, u32[]{:S(2)}) collective-permute-start(bf16[32,8192]{1,0:T(8,128)(2,1)S(1)} %collective-permute-done.1.refs_2_), channel_id=1, source_target_pairs={{0,4},{1,5},{4,8},{5,9},{8,12},{9,13},{12,14},{13,15},{14,10},{15,... | collective-permute-start | bytes 1572872 | tf_op jit(solution)/shard_map/ppermute | solution.py:419
  34.9 15.3 %collective-permute-start.8 = (bf16[32,8192]{1,0:T(8,128)(2,1)S(1)}, bf16[32,8192]{1,0:T(8,128)(2,1)S(1)}, u32[]{:S(2)}, u32[]{:S(2)}) collective-permute-start(bf16[32,8192]{1,0:T(8,128)(2,1)S(1)} %collective-permute-done.2.refs_4_), channel_id=1, source_target_pairs={{4,0},{5,1},{8,4},{9,5},{12,8},{13,9},{14,12},{15,13},{10,14},{11,... | collective-permute-start | bytes 1572872 | tf_op jit(solution)/shard_map/ppermute | solution.py:420
  35.7 1.5 %collective-permute-start.11 = (bf16[16,8192]{1,0:T(8,128)(2,1)S(1)}, bf16[16,8192]{1,0:T(8,128)(2,1)S(1)}, u32[]{:S(2)}, u32[]{:S(2)}) collective-permute-start(bf16[16,8192]{1,0:T(8,128)(2,1)S(1)} %pad_maximum_fusion.refs_6_), channel_id=1, source_target_pairs={{0,1},{1,0},{2,3},{3,2},{4,5},{5,4},{6,7},{7,6},{8,9},{9,8},{10,11... | collective-permute-start | bytes 786440 | tf_op jit(solution)/shard_map/ppermute | solution.py:421
  41.3 9.0 %collective-permute-start.12 = (f32[32,1024]{1,0:T(8,128)S(1)}, f32[32,1024]{1,0:T(8,128)S(1)}, u32[]{:S(2)}, u32[]{:S(2)}) collective-permute-start(f32[32,1024]{1,0:T(8,128)S(1)} %get-tuple-element.75.refs_5_), channel_id=1, source_target_pairs={{0,16},{16,0},{1,17},{17,1},{2,18},{18,2},{3,19},{19,3},{4,20},{20... | collective-permute-start | bytes 393224 | tf_op jit(solution)/shard_map/ppermute | solution.py:424
  50.3 2.6 %collective-permute-start.15 = (bf16[32,8192]{1,0:T(8,128)(2,1)S(1)}, bf16[32,8192]{1,0:T(8,128)(2,1)S(1)}, u32[]{:S(2)}, u32[]{:S(2)}) collective-permute-start(bf16[32,8192]{1,0:T(8,128)(2,1)S(1)} %collective-permute-done.7.refs_0_), channel_id=1, source_target_pairs={{0,1},{1,0},{2,3},{3,2},{4,5},{5,4},{6,7},{7,6},{8,9},{9,8},{10,11... | collective-permute-start | bytes 1572872 | tf_op jit(solution)/shard_map/ppermute | solution.py:421
  50.3 2.6 %collective-permute-start.16 = (bf16[32,8192]{1,0:T(8,128)(2,1)S(1)}, bf16[32,8192]{1,0:T(8,128)(2,1)S(1)}, u32[]{:S(2)}, u32[]{:S(2)}) collective-permute-start(bf16[32,8192]{1,0:T(8,128)(2,1)S(1)} %collective-permute-done.8.refs_2_), channel_id=1, source_target_pairs={{0,1},{1,0},{2,3},{3,2},{4,5},{5,4},{6,7},{7,6},{8,9},{9,8},{10,11... | collective-permute-start | bytes 1572872 | tf_op jit(solution)/shard_map/ppermute | solution.py:421
  50.8 13.9 %collective-permute-start.13 = (bf16[32,8192]{1,0:T(8,128)(2,1)S(1)}, bf16[32,8192]{1,0:T(8,128)(2,1)S(1)}, u32[]{:S(2)}, u32[]{:S(2)}) collective-permute-start(bf16[32,8192]{1,0:T(8,128)(2,1)S(1)} %collective-permute-done.7.refs_0_), channel_id=1, source_target_pairs={{0,4},{1,5},{4,8},{5,9},{8,12},{9,13},{12,14},{13,15},{14,10},{15,... | collective-permute-start | bytes 1572872 | tf_op jit(solution)/shard_map/ppermute | solution.py:419
  52.4 13.6 %collective-permute-start.14 = (bf16[32,8192]{1,0:T(8,128)(2,1)S(1)}, bf16[32,8192]{1,0:T(8,128)(2,1)S(1)}, u32[]{:S(2)}, u32[]{:S(2)}) collective-permute-start(bf16[32,8192]{1,0:T(8,128)(2,1)S(1)} %collective-permute-done.8.refs_2_), channel_id=1, source_target_pairs={{4,0},{5,1},{8,4},{9,5},{12,8},{13,9},{14,12},{15,13},{10,14},{11,... | collective-permute-start | bytes 1572872 | tf_op jit(solution)/shard_map/ppermute | solution.py:420
  61.6 1.6 %collective-permute-start.17 = (bf16[16,8192]{1,0:T(8,128)(2,1)S(1)}, bf16[16,8192]{1,0:T(8,128)(2,1)S(1)}, u32[]{:S(2)}, u32[]{:S(2)}) collective-permute-start(bf16[16,8192]{1,0:T(8,128)(2,1)S(1)} %get-tuple-element.82), channel_id=1, source_target_pairs={{0,1},{1,0},{2,3},{3,2},{4,5},{5,4},{6,7},{7,6},{8,9},{9,8},{10,11... | collective-permute-start | bytes 786440 | tf_op jit(solution)/shard_map/ppermute | solution.py:421
  66.0 3.1 %collective-permute-start.19 = (bf16[32,8192]{1,0:T(8,128)(2,1)S(1)}, bf16[32,8192]{1,0:T(8,128)(2,1)S(1)}, u32[]{:S(2)}, u32[]{:S(2)}) collective-permute-start(bf16[32,8192]{1,0:T(8,128)(2,1)S(1)} %collective-permute-done.13.refs_0_), channel_id=1, source_target_pairs={{0,1},{1,0},{2,3},{3,2},{4,5},{5,4},{6,7},{7,6},{8,9},{9,8},{10,11... | collective-permute-start | bytes 1572872 | tf_op jit(solution)/shard_map/ppermute | solution.py:421
  66.0 4.0 %collective-permute-start.20 = (bf16[32,8192]{1,0:T(8,128)(2,1)S(1)}, bf16[32,8192]{1,0:T(8,128)(2,1)S(1)}, u32[]{:S(2)}, u32[]{:S(2)}) collective-permute-start(bf16[32,8192]{1,0:T(8,128)(2,1)S(1)} %collective-permute-done.14.refs_2_), channel_id=1, source_target_pairs={{0,1},{1,0},{2,3},{3,2},{4,5},{5,4},{6,7},{7,6},{8,9},{9,8},{10,11... | collective-permute-start | bytes 1572872 | tf_op jit(solution)/shard_map/ppermute | solution.py:421
  66.6 11.1 %collective-permute-start.21 = (bf16[16,8192]{1,0:T(8,128)(2,1)S(1)}, bf16[16,8192]{1,0:T(8,128)(2,1)S(1)}, u32[]{:S(2)}, u32[]{:S(2)}) collective-permute-start(bf16[16,8192]{1,0:T(8,128)(2,1)S(1)} %slice.22), channel_id=1, source_target_pairs={{0,4},{1,5},{4,8},{5,9},{8,12},{9,13},{12,14},{13,15},{14,10},{15,... | collective-permute-start | bytes 786440 | tf_op jit(solution)/shard_map/ppermute | solution.py:419
  66.9 10.8 %collective-permute-start.22 = (bf16[16,8192]{1,0:T(8,128)(2,1)S(1)}, bf16[16,8192]{1,0:T(8,128)(2,1)S(1)}, u32[]{:S(2)}, u32[]{:S(2)}) collective-permute-start(bf16[16,8192]{1,0:T(8,128)(2,1)S(1)} %slice.23), channel_id=1, source_target_pairs={{4,0},{5,1},{8,4},{9,5},{12,8},{13,9},{14,12},{15,13},{10,14},{11,... | collective-permute-start | bytes 786440 | tf_op jit(solution)/shard_map/ppermute | solution.py:420
  68.7 9.0 %collective-permute-start.18 = (bf16[8,8192]{1,0:T(8,128)(2,1)S(1)}, bf16[8,8192]{1,0:T(8,128)(2,1)S(1)}, u32[]{:S(2)}, u32[]{:S(2)}) collective-permute-start(bf16[8,8192]{1,0:T(8,128)(2,1)S(1)} %get-tuple-element.87), channel_id=1, source_target_pairs={{0,2},{1,3},{2,0},{3,1},{4,6},{5,7},{6,4},{7,5},{8,10},{9,11},{10,... | collective-permute-start | bytes 393224 | tf_op jit(solution)/shard_map/ppermute | solution.py:422
  69.1 8.6 %collective-permute-start.23 = (bf16[64,1024]{1,0:T(8,128)(2,1)S(1)}, bf16[64,1024]{1,0:T(8,128)(2,1)S(1)}, u32[]{:S(2)}, u32[]{:S(2)}) collective-permute-start(bf16[64,1024]{1,0:T(8,128)(2,1)S(1)} %get-tuple-element.94), channel_id=1, source_target_pairs={{0,16},{16,0},{1,17},{17,1},{2,18},{18,2},{3,19},{19,3},{4,20},{20... | collective-permute-start | bytes 393224 | tf_op jit(solution)/shard_map/ppermute | solution.py:424
  77.8 3.6 %collective-permute-start.24 = (bf16[16,8192]{1,0:T(8,128)(2,1)S(1)}, bf16[16,8192]{1,0:T(8,128)(2,1)S(1)}, u32[]{:S(2)}, u32[]{:S(2)}) collective-permute-start(bf16[16,8192]{1,0:T(8,128)(2,1)S(1)} %collective-permute-done.21.refs_0_.refs_4_), channel_id=1, source_target_pairs={{0,1},{1,0},{2,3},{3,2},{4,5},{5,4},{6,7},{7,6},{8,9},{9,8},{10,11... | collective-permute-start | bytes 786440 | tf_op jit(solution)/shard_map/ppermute | solution.py:421
  77.8 5.4 %collective-permute-start.25 = (bf16[16,8192]{1,0:T(8,128)(2,1)S(1)}, bf16[16,8192]{1,0:T(8,128)(2,1)S(1)}, u32[]{:S(2)}, u32[]{:S(2)}) collective-permute-start(bf16[16,8192]{1,0:T(8,128)(2,1)S(1)} %collective-permute-done.22.refs_1_.refs_5_), channel_id=1, source_target_pairs={{0,1},{1,0},{2,3},{3,2},{4,5},{5,4},{6,7},{7,6},{8,9},{9,8},{10,11... | collective-permute-start | bytes 786440 | tf_op jit(solution)/shard_map/ppermute | solution.py:421
  78.3 8.9 %collective-permute-start.26 = (bf16[128,1024]{1,0:T(8,128)(2,1)S(1)}, bf16[128,1024]{1,0:T(8,128)(2,1)S(1)}, u32[]{:S(2)}, u32[]{:S(2)}) collective-permute-start(bf16[128,1024]{1,0:T(8,128)(2,1)S(1)} %get-tuple-element.101), channel_id=1, source_target_pairs={{0,16},{16,0},{1,17},{17,1},{2,18},{18,2},{3,19},{19,3},{4,20},{20... | collective-permute-start | bytes 786440 | tf_op jit(solution)/shard_map/ppermute | solution.py:424
  78.8 8.3 %collective-permute-start.27 = (bf16[2,8192]{1,0:T(2,128)(2,1)S(1)}, bf16[2,8192]{1,0:T(2,128)(2,1)S(1)}, u32[]{:S(2)}, u32[]{:S(2)}) collective-permute-start(bf16[2,8192]{1,0:T(2,128)(2,1)S(1)} %get-tuple-element.102), channel_id=1, source_target_pairs={{0,4},{1,5},{2,6},{3,7},{4,0},{5,1},{6,2},{7,3},{8,12},{9,13},{10,... | collective-permute-start | bytes 98312 | tf_op jit(solution)/shard_map/ppermute | solution.py:423
  78.8 8.3 %collective-permute-start.28 = (bf16[2,8192]{1,0:T(2,128)(2,1)S(1)}, bf16[2,8192]{1,0:T(2,128)(2,1)S(1)}, u32[]{:S(2)}, u32[]{:S(2)}) collective-permute-start(bf16[2,8192]{1,0:T(2,128)(2,1)S(1)} %get-tuple-element.103), channel_id=1, source_target_pairs={{0,8},{1,9},{2,10},{3,11},{4,12},{5,13},{6,14},{7,15},{8,0},{9,1},... | collective-permute-start | bytes 98312 | tf_op jit(solution)/shard_map/ppermute | solution.py:423
  81.4 5.8 %collective-permute-start.29 = (bf16[2,8192]{1,0:T(2,128)(2,1)S(1)}, bf16[2,8192]{1,0:T(2,128)(2,1)S(1)}, u32[]{:S(2)}, u32[]{:S(2)}) collective-permute-start(bf16[2,8192]{1,0:T(2,128)(2,1)S(1)} %get-tuple-element.104), channel_id=1, source_target_pairs={{0,12},{1,13},{2,14},{3,15},{4,8},{5,9},{6,10},{7,11},{8,4},{9,5},... | collective-permute-start | bytes 98312 | tf_op jit(solution)/shard_map/ppermute | solution.py:423
  85.6 5.0 %collective-permute-start.31 = (bf16[64,1024]{1,0:T(8,128)(2,1)S(1)}, bf16[64,1024]{1,0:T(8,128)(2,1)S(1)}, u32[]{:S(2)}, u32[]{:S(2)}) collective-permute-start(bf16[64,1024]{1,0:T(8,128)(2,1)S(1)} %get-tuple-element.113), channel_id=1, source_target_pairs={{0,16},{16,0},{1,17},{17,1},{2,18},{18,2},{3,19},{19,3},{4,20},{20... | collective-permute-start | bytes 393224 | tf_op jit(solution)/shard_map/ppermute | solution.py:424
  87.4 4.2 %collective-permute-start.30 = (f32[2,1]{0,1:T(1,128)S(1)}, f32[2,1]{0,1:T(1,128)S(1)}, u32[]{:S(2)}, u32[]{:S(2)}) collective-permute-start(f32[2,1]{0,1:T(1,128)S(1)} %bitcast.17), channel_id=1, source_target_pairs={{0,16},{16,0},{1,17},{17,1},{2,18},{18,2},{3,19},{19,3},{4,20},{20... | collective-permute-start | bytes 32 | tf_op jit(solution)/shard_map/ppermute | solution.py:424
  (8 other events, 184.1 us)

commit v4 on v3

--- a/solution.py
+++ b/solution.py
@@ -330,10 +330,7 @@
 def finish_hidden(residual, kept, got):
     rows = 2 * TREE
     n = len(kept)
-    pair_of = []
-    for i, k in enumerate(kept):
-        pair_of.append(k[1])
-    arrays = [k[0] for k in kept] + list(got)
+    arrays = [k[0] for k in kept] + [g[0] for g in got]
 
     def kernel(res, *refs):
         out = refs[-1]
@@ -341,16 +338,18 @@
         side = lax.axis_index("tensor")
         for i in range(n):
             keep, more = refs[i], refs[n + i]
-            for j, pair in enumerate(pair_of[i]):
+            for j, pair in enumerate(kept[i][1]):
                 first, mine = first_is_mine(pair, position, side)
                 chip = jnp.where(mine, first, (first + 4) & 7)
                 chip = jnp.where(chip < 4, chip * 2, (7 - chip) * 2 + 1)
                 for c in range(2):
                     place = (chip * 2 + (core ^ c) - side * 8) * rows
-                    place = pl.multiple_of(place, rows)
-                    here = slice((2 * j + c) * rows, (2 * j + c + 1) * rows)
-                    total = keep[here] + more[here].astype(F32)
-                    out[pl.ds(place, rows)] = (res[pl.ds(place, rows)].astype(F32) + total).astype(BF)
+                    place = pl.ds(pl.multiple_of(place, rows), rows)
+                    at = (2 * j + c) * rows
+                    total = keep[at : at + rows]
+                    at = at + got[i][1]
+                    total = total + more[at : at + rows].astype(F32)
+                    out[place] = (res[place].astype(F32) + total).astype(BF)
 
     return pl.pallas_call(
         kernel,
@@ -498,28 +497,30 @@
     stay8, send8 = add_and_split("sum_core", keep16, got16, 2)
     f3, b3, stay8, send8, send_2 = tie(f3, b3, stay8, send8, send_2)
     got8 = swap_x(send8)
-    got_2 = swap_side(send_2)
     f4, b4 = ahead(f3[:TREE]), back(b3[TREE:])
     f3s, b3s = swap_core(f3), swap_core(b3)
 
     def finish_3(total, more, results):
-        before = more[0]
+        before, earlier = more
+        keep, send = results
         split_pairs(
             [0, 1],
             [before[two : 2 * two], before[2 * two :]],
             [total[two:], total[:two]],
-            *results,
+            keep,
+            send.at[: 2 * two],
         )
+        send[2 * two :] = earlier[...]
 
     keep_3, send_3 = project(
-        "project_3", [f3, f3s, b3, b3s], out_proj, [part_a], finish_3,
-        [f32(2 * two, columns), bf16(2 * two, columns)],
+        "project_3", [f3, f3s, b3, b3s], out_proj, [part_a, send_2], finish_3,
+        [f32(2 * two, columns), bf16(3 * two, columns)],
     )
     got_3 = swap_side(send_3)
     got8, keep_3 = tie(got8, keep_3)
     stay2, *sends = add_and_split("sum_x", stay8, got8, 4)
 
-    f4, b4, got_2, *sends = tie(f4, b4, got_2, *sends)
+    f4, b4, *sends = tie(f4, b4, *sends)
     f4s, b4s = swap_core(f4), swap_core(b4)
     gots = [swap_z(v, k) for k, v in enumerate(sends, 1)]
 
@@ -536,7 +537,9 @@
     squares = jnp.sum(joined * joined, axis=1, keepdims=True)
     other_squares = swap_side(squares)
     hidden = finish_hidden(
-        res, [(keep_2, [2]), (keep_3, [0, 1]), (keep_4, [3])], [got_2, got_3, got_4]
+        res,
+        [(keep_2, [2]), (keep_3, [0, 1]), (keep_4, [3])],
+        [(got_3, 2 * two), (got_3, 0), (got_4, 0)],
     ).reshape(residual.shape)
     other_squares, hidden = tie(other_squares, hidden)
     row_scale = lax.rsqrt((squares + other_squares) / D + 1e-05)

time: 92.6 us -> 92.1 us (level)
  starting transfers between devices: 30 us -> 28.3 us
  waiting for transfers between devices: 17.4 us -> 18.5 us
    ppermute x6 -> x5, starting transfers between devices: 6.88 us -> 5.22 us  [ring_body(): swap_side = lambda v: lax.ppermute(v, 'tensor', [(0, 1), (1, 0)])]
    ppermute x6 -> x5, waiting for transfers between devices: 3.63 us -> 4.23 us  [ring_body(): swap_side = lambda v: lax.ppermute(v, 'tensor', [(0, 1), (1, 0)])]
  transfers between devices with their start and end apart: 32 -> 31, of which waited for: 10 -> 11; matrix products, arithmetic and copies ran while one was open for 1% -> 1% of each run, Pallas kernels for 37% -> 38%
where the time goes in v4:
time: 92.1 us; the launch traced here: 91.9 us
  Pallas kernels  41.3 us (45%)
  starting transfers between devices  28.3 us (31%)
  waiting for transfers between devices  18.5 us (20%)
  other arithmetic  1.83 us (2%)
  local copies, waits for them, and re-layouts  0.97 us (1%)
  between operations  0.96 us (1%)
    pallas_call x2, Pallas kernels, join_layer(): pl.pallas_call(kernel, grid=(steps,), in_specs=specs, out_specs=[pl.Block...  16.2 us
    ppermute x5, starting transfers between devices, ring_body(): lax.ppermute(v, 'request', [(r, r ^ 4 * k) for r in range(size)])  10.6 us
    pallas_call x3, Pallas kernels, project(): pl.pallas_call(kernel, in_specs=[VMEM] * (n + 1 + m), out_specs=[VMEM] *...  8.65 us
    pallas_call x1, Pallas kernels, project_and_join(): pl.pallas_call(kernel, in_specs=[VMEM] * (n + 4) + [HBM], out_specs=[VMEM...  8.56 us
    pallas_call x1, Pallas kernels, attention(): pl.pallas_call(kernel, in_specs=in_specs, out_specs=[VMEM] * len(outs), o...  6.8 us
    ppermute x2, waiting for transfers between devices, ring_body(): lax.ppermute(v, 'request', [(r, r ^ 2) for r in range(size)])  5.62 us
    ppermute x5, starting transfers between devices, ring_body(): swap_side = lambda v: lax.ppermute(v, 'tensor', [(0, 1), (1, 0)])  5.22 us
    ppermute x4, starting transfers between devices, ring_body(): ahead = lambda v: lax.ppermute(v, 'request', forward)  4.72 us
  transfers between devices with their start and end apart: 31, of which 11 were waited for; matrix products, arithmetic and copies ran while one was open for 1% of the time, Pallas kernels for 38%

profile of v4, /device:TPU:0, one launch (start us, length us, event | category | flops | bytes accessed | tf_op | source)
XLA Modules:
  0.0 91.9 jit_solution(4380122580828170923)
XLA Ops:
  0.6 6.8 %attention.1 = (bf16[32,8192]{1,0:T(8,128)(2,1)}, bf16[2,8192]{1,0:T(2,128)(2,1)}, bf16[64,1024]{1,0:T(8,128)(2,1)}, f32[32,1024]{1,0:T(8,128)}) custom-call(s32[2]{0:T(128)} %len_ref.1, s32[32]{0:T(128)} %last_ref.1, s32[2,16]{1,0:T(2,128)} %refs_0_.1, bf16[2,16,8192]{2,1,0:T(8,128)(2,1)} %refs_1_.1, bf16[2,256,512]{2,1,0:T(8,128)(2,1)} %refs_2_.3, ...), custom_call_target="tpu_custom_call" | custom-call | flops 1 | bytes 1 | tf_op jit(solution)/shard_map/attention/pallas_call | solution.py:177
  7.5 3.1 %collective-permute-start = (bf16[2,8192]{1,0:T(2,128)(2,1)}, bf16[2,8192]{1,0:T(2,128)(2,1)S(1)}, u32[]{:S(2)}, u32[]{:S(2)}) collective-permute-start(bf16[2,8192]{1,0:T(2,128)(2,1)} %get-tuple-element.59), channel_id=1, source_target_pairs={{0,4},{1,5},{2,6},{3,7},{4,0},{5,1},{6,2},{7,3},{8,12},{9,13},{10,... | collective-permute-start | bytes 98312 | tf_op jit(solution)/shard_map/ppermute | solution.py:422
  10.5 2.1 %collective-permute-done = bf16[2,8192]{1,0:T(2,128)(2,1)S(1)} collective-permute-done((bf16[2,8192]{1,0:T(2,128)(2,1)}, bf16[2,8192]{1,0:T(2,128)(2,1)S(1)}, u32[]{:S(2)}, u32[]{:S(2)}) %collective-permute-start) | collective-permute-done | bytes 32800 | tf_op jit(solution)/shard_map/ppermute | solution.py:422
  12.6 0.8 pad_maximum_fusion.2
  13.5 3.1 %collective-permute-start.5 = (bf16[4,8192]{1,0:T(4,128)(2,1)S(1)}, bf16[4,8192]{1,0:T(4,128)(2,1)S(1)}, u32[]{:S(2)}, u32[]{:S(2)}) collective-permute-start(bf16[4,8192]{1,0:T(4,128)(2,1)S(1)} %pad_maximum_fusion.2), channel_id=1, source_target_pairs={{0,8},{1,9},{2,10},{3,11},{4,12},{5,13},{6,14},{7,15},{8,0},{9,1},... | collective-permute-start | bytes 196616 | tf_op jit(solution)/shard_map/ppermute | solution.py:422
  16.6 1.5 %collective-permute-start.4 = (bf16[64,1024]{1,0:T(8,128)(2,1)}, bf16[64,1024]{1,0:T(8,128)(2,1)S(1)}, u32[]{:S(2)}, u32[]{:S(2)}) collective-permute-start(bf16[64,1024]{1,0:T(8,128)(2,1)} %get-tuple-element.64), channel_id=1, source_target_pairs={{0,16},{16,0},{1,17},{17,1},{2,18},{18,2},{3,19},{19,3},{4,20},{20... | collective-permute-start | bytes 393224 | tf_op jit(solution)/shard_map/ppermute | solution.py:423
  18.1 1.6 %collective-permute-start.1 = (bf16[32,8192]{1,0:T(8,128)(2,1)}, bf16[32,8192]{1,0:T(8,128)(2,1)S(1)}, u32[]{:S(2)}, u32[]{:S(2)}) collective-permute-start(bf16[32,8192]{1,0:T(8,128)(2,1)} %get-tuple-element.60.refs_0_), channel_id=1, source_target_pairs={{0,4},{1,5},{4,8},{5,9},{8,12},{9,13},{12,14},{13,15},{14,10},{15,... | collective-permute-start | bytes 1572872 | tf_op jit(solution)/shard_map/ppermute | solution.py:418
  20.2 1.6 %collective-permute-done.4 = bf16[64,1024]{1,0:T(8,128)(2,1)S(1)} collective-permute-done((bf16[64,1024]{1,0:T(8,128)(2,1)}, bf16[64,1024]{1,0:T(8,128)(2,1)S(1)}, u32[]{:S(2)}, u32[]{:S(2)}) %collective-permute-start.4) | collective-permute-done | bytes 131104 | tf_op jit(solution)/shard_map/ppermute | solution.py:423
  21.8 1.5 %collective-permute-start.6 = (bf16[8,8192]{1,0:T(8,128)(2,1)S(1)}, bf16[8,8192]{1,0:T(8,128)(2,1)S(1)}, u32[]{:S(2)}, u32[]{:S(2)}) collective-permute-start(bf16[8,8192]{1,0:T(8,128)(2,1)S(1)} %pad_maximum_fusion.1), channel_id=1, source_target_pairs={{0,2},{1,3},{2,0},{3,1},{4,6},{5,7},{6,4},{7,5},{8,10},{9,11},{10,... | collective-permute-start | bytes 393224 | tf_op jit(solution)/shard_map/ppermute | solution.py:421
  23.3 0.9 fusion
  24.2 8.5 %join_low.1.refs_4_ = f32[32,8192]{1,0:T(8,128)S(1)} custom-call(bf16[32,1024]{1,0:T(8,128)(2,1)S(1)} %get-tuple-element.118.refs_0_, bf16[32,1024]{1,0:T(8,128)(2,1)S(1)} %get-tuple-element.115.refs_1_, bf16[3,1024,8192]{2,1,0:T(8,128)(2,1)} %refs_8_.4, bf16[3,1024,8192]{2,1,0:T(8,128)(2,1)} %refs_8_.4), custom_call_target="tpu_custom_call" | custom-call | flops 1 | bytes 1 | tf_op jit(solution)/shard_map/join_low/pallas_call | solution.py:262
  33.7 1.2 %collective-permute-start.7 = (bf16[32,8192]{1,0:T(8,128)(2,1)S(1)}, bf16[32,8192]{1,0:T(8,128)(2,1)S(1)}, u32[]{:S(2)}, u32[]{:S(2)}) collective-permute-start(bf16[32,8192]{1,0:T(8,128)(2,1)S(1)} %collective-permute-done.1.refs_2_), channel_id=1, source_target_pairs={{0,4},{1,5},{4,8},{5,9},{8,12},{9,13},{12,14},{13,15},{14,10},{15,... | collective-permute-start | bytes 1572872 | tf_op jit(solution)/shard_map/ppermute | solution.py:418
  34.9 0.8 collective-permute-start.8
  35.7 1.5 %collective-permute-done.11.refs_7_ = bf16[16,8192]{1,0:T(8,128)(2,1)S(1)} collective-permute-done((bf16[16,8192]{1,0:T(8,128)(2,1)S(1)}, bf16[16,8192]{1,0:T(8,128)(2,1)S(1)}, u32[]{:S(2)}, u32[]{:S(2)}) %collective-permute-start.11) | collective-permute-done | bytes 262176 | tf_op jit(solution)/shard_map/ppermute | solution.py:420
  37.3 3.9 %project_a.1 = (f32[192,1024]{1,0:T(8,128)S(1)}, f32[32,1024]{1,0:T(8,128)S(1)}) custom-call(bf16[32,8192]{1,0:T(8,128)(2,1)S(1)} %copy-done.1, bf16[32,8192]{1,0:T(8,128)(2,1)S(1)} %collective-permute-done.3.refs_1_, bf16[32,8192]{1,0:T(8,128)(2,1)S(1)} %collective-permute-done.1.refs_2_, bf16[32,8192]{1,0:T(8,128)(2,1)S(1)} %collective-permute-done.9.refs_3_, ...), custom_call_target="tpu_custom_call" | custom-call | flops 1 | bytes 1 | tf_op jit(solution)/shard_map/project_a/pallas_call | solution.py:208
  41.3 1.2 %collective-permute-start.12 = (f32[32,1024]{1,0:T(8,128)S(1)}, f32[32,1024]{1,0:T(8,128)S(1)}, u32[]{:S(2)}, u32[]{:S(2)}) collective-permute-start(f32[32,1024]{1,0:T(8,128)S(1)} %get-tuple-element.74.refs_5_), channel_id=1, source_target_pairs={{0,16},{16,0},{1,17},{17,1},{2,18},{18,2},{3,19},{19,3},{4,20},{20... | collective-permute-start | bytes 393224 | tf_op jit(solution)/shard_map/ppermute | solution.py:423
  42.5 7.7 %join_mid.1.refs_7_ = f32[32,8192]{1,0:T(8,128)S(1)} custom-call(bf16[32,1024]{1,0:T(8,128)(2,1)S(1)} %get-tuple-element.119.refs_0_, bf16[32,1024]{1,0:T(8,128)(2,1)S(1)} %get-tuple-element.114.refs_1_, bf16[3,1024,8192]{2,1,0:T(8,128)(2,1)} %refs_8_.4, bf16[3,1024,8192]{2,1,0:T(8,128)(2,1)} %refs_8_.4, f32[32,8192]{1,0:T(8,128)S(1)} %join_low.1.refs_4_), custom_call_target="tpu_custom_call" | custom-call | flops 1 | bytes 1 | tf_op jit(solution)/shard_map/join_mid/pallas_call | solution.py:262
  50.8 1.6 %collective-permute-start.13 = (bf16[32,8192]{1,0:T(8,128)(2,1)S(1)}, bf16[32,8192]{1,0:T(8,128)(2,1)S(1)}, u32[]{:S(2)}, u32[]{:S(2)}) collective-permute-start(bf16[32,8192]{1,0:T(8,128)(2,1)S(1)} %collective-permute-done.7.refs_0_), channel_id=1, source_target_pairs={{0,4},{1,5},{4,8},{5,9},{8,12},{9,13},{12,14},{13,15},{14,10},{15,... | collective-permute-start | bytes 1572872 | tf_op jit(solution)/shard_map/ppermute | solution.py:418
  53.0 8.6 %project_2_join_hidden.1 = (f32[64,1024]{1,0:T(8,128)S(1)}, bf16[64,1024]{1,0:T(8,128)(2,1)S(1)}, f32[16,8192]{1,0:T(8,128)S(1)}, bf16[16,8192]{1,0:T(8,128)(2,1)S(1)}) custom-call(bf16[32,8192]{1,0:T(8,128)(2,1)S(1)} %collective-permute-done.7.refs_0_, bf16[32,8192]{1,0:T(8,128)(2,1)S(1)} %collective-permute-done.15.refs_1_, ...), custom_call_target="tpu_custom_call" | custom-call | flops 1 | bytes 1 | tf_op jit(solution)/shard_map/project_2_join_hidden/pallas_call | solution.py:309
  61.8 1.4 %collective-permute-done.17.g_ref = bf16[16,8192]{1,0:T(8,128)(2,1)S(1)} collective-permute-done((bf16[16,8192]{1,0:T(8,128)(2,1)S(1)}, bf16[16,8192]{1,0:T(8,128)(2,1)S(1)}, u32[]{:S(2)}, u32[]{:S(2)}) %collective-permute-start.17) | collective-permute-done | bytes 262176 | tf_op jit(solution)/shard_map/ppermute | solution.py:420
  63.2 1.5 %collective-permute-done.13.refs_0_ = bf16[32,8192]{1,0:T(8,128)(2,1)S(1)} collective-permute-done((bf16[32,8192]{1,0:T(8,128)(2,1)S(1)}, bf16[32,8192]{1,0:T(8,128)(2,1)S(1)}, u32[]{:S(2)}, u32[]{:S(2)}) %collective-permute-start.13) | collective-permute-done | bytes 524320 | tf_op jit(solution)/shard_map/ppermute | solution.py:418
  64.7 1.3 %collective-permute-done.14.refs_2_ = bf16[32,8192]{1,0:T(8,128)(2,1)S(1)} collective-permute-done((bf16[32,8192]{1,0:T(8,128)(2,1)S(1)}, bf16[32,8192]{1,0:T(8,128)(2,1)S(1)}, u32[]{:S(2)}, u32[]{:S(2)}) %collective-permute-start.14) | collective-permute-done | bytes 524320 | tf_op jit(solution)/shard_map/ppermute | solution.py:419
  66.9 1.7 %collective-permute-start.22 = (bf16[16,8192]{1,0:T(8,128)(2,1)S(1)}, bf16[16,8192]{1,0:T(8,128)(2,1)S(1)}, u32[]{:S(2)}, u32[]{:S(2)}) collective-permute-start(bf16[16,8192]{1,0:T(8,128)(2,1)S(1)} %slice.23), channel_id=1, source_target_pairs={{4,0},{5,1},{8,4},{9,5},{12,8},{13,9},{14,12},{15,13},{10,14},{11,... | collective-permute-start | bytes 786440 | tf_op jit(solution)/shard_map/ppermute | solution.py:419
  69.1 2.3 %project_3.1 = (f32[128,1024]{1,0:T(8,128)S(1)}, bf16[192,1024]{1,0:T(8,128)(2,1)S(1)}) custom-call(bf16[32,8192]{1,0:T(8,128)(2,1)S(1)} %collective-permute-done.13.refs_0_, bf16[32,8192]{1,0:T(8,128)(2,1)S(1)} %collective-permute-done.19.refs_1_, bf16[32,8192]{1,0:T(8,128)(2,1)S(1)} %collective-permute-done.14.refs_2_, ...), custom_call_target="tpu_custom_call" | custom-call | flops 1 | bytes 1 | tf_op jit(solution)/shard_map/project_3/pallas_call | solution.py:208
  71.5 0.9 %collective-permute-start.25 = (bf16[192,1024]{1,0:T(8,128)(2,1)S(1)}, bf16[192,1024]{1,0:T(8,128)(2,1)S(1)}, u32[]{:S(2)}, u32[]{:S(2)}) collective-permute-start(bf16[192,1024]{1,0:T(8,128)(2,1)S(1)} %get-tuple-element.100), channel_id=1, source_target_pairs={{0,16},{16,0},{1,17},{17,1},{2,18},{18,2},{3,19},{19,3},{4,20},{20... | collective-permute-start | bytes 1179656 | tf_op jit(solution)/shard_map/ppermute | solution.py:423
  72.4 5.3 %collective-permute-done.18.g_ref = bf16[8,8192]{1,0:T(8,128)(2,1)S(1)} collective-permute-done((bf16[8,8192]{1,0:T(8,128)(2,1)S(1)}, bf16[8,8192]{1,0:T(8,128)(2,1)S(1)}, u32[]{:S(2)}, u32[]{:S(2)}) %collective-permute-start.18) | collective-permute-done | bytes 131104 | tf_op jit(solution)/shard_map/ppermute | solution.py:421
  78.3 2.2 %collective-permute-start.27 = (bf16[2,8192]{1,0:T(2,128)(2,1)S(1)}, bf16[2,8192]{1,0:T(2,128)(2,1)S(1)}, u32[]{:S(2)}, u32[]{:S(2)}) collective-permute-start(bf16[2,8192]{1,0:T(2,128)(2,1)S(1)} %get-tuple-element.102), channel_id=1, source_target_pairs={{0,8},{1,9},{2,10},{3,11},{4,12},{5,13},{6,14},{7,15},{8,0},{9,1},... | collective-permute-start | bytes 98312 | tf_op jit(solution)/shard_map/ppermute | solution.py:422
  80.6 2.1 %collective-permute-start.28 = (bf16[2,8192]{1,0:T(2,128)(2,1)S(1)}, bf16[2,8192]{1,0:T(2,128)(2,1)S(1)}, u32[]{:S(2)}, u32[]{:S(2)}) collective-permute-start(bf16[2,8192]{1,0:T(2,128)(2,1)S(1)} %get-tuple-element.103), channel_id=1, source_target_pairs={{0,12},{1,13},{2,14},{3,15},{4,8},{5,9},{6,10},{7,11},{8,4},{9,5},... | collective-permute-start | bytes 98312 | tf_op jit(solution)/shard_map/ppermute | solution.py:422
  82.7 2.4 %project_4.1 = (f32[64,1024]{1,0:T(8,128)S(1)}, bf16[64,1024]{1,0:T(8,128)(2,1)S(1)}) custom-call(bf16[16,8192]{1,0:T(8,128)(2,1)S(1)} %collective-permute-done.21.refs_0_.refs_4_, bf16[16,8192]{1,0:T(8,128)(2,1)S(1)} %collective-permute-done.22.refs_1_.refs_5_, bf16[16,8192]{1,0:T(8,128)(2,1)S(1)} %collective-permute-done.23.refs_2_.refs_6_, ...), custom_call_target="tpu_custom_call" | custom-call | flops 1 | bytes 1 | tf_op jit(solution)/shard_map/project_4/pallas_call | solution.py:208
  86.5 1.0 %collective-permute-start.29 = (f32[2,1]{0,1:T(1,128)S(1)}, f32[2,1]{0,1:T(1,128)S(1)}, u32[]{:S(2)}, u32[]{:S(2)}) collective-permute-start(f32[2,1]{0,1:T(1,128)S(1)} %bitcast.17), channel_id=1, source_target_pairs={{0,16},{16,0},{1,17},{17,1},{2,18},{18,2},{3,19},{19,3},{4,20},{20... | collective-permute-start | bytes 32 | tf_op jit(solution)/shard_map/ppermute | solution.py:423
  87.5 2.7 %collective-permute-done.30.refs_5_ = bf16[64,1024]{1,0:T(8,128)(2,1)S(1)} collective-permute-done((bf16[64,1024]{1,0:T(8,128)(2,1)S(1)}, bf16[64,1024]{1,0:T(8,128)(2,1)S(1)}, u32[]{:S(2)}, u32[]{:S(2)}) %collective-permute-start.30) | collective-permute-done | bytes 131104 | tf_op jit(solution)/shard_map/ppermute | solution.py:423
  90.1 1.0 %finish_hidden.1 = bf16[256,1024]{1,0:T(8,128)(2,1)} custom-call(bf16[256,1024]{1,0:T(8,128)(2,1)S(1)} %bitcast.12, f32[64,1024]{1,0:T(8,128)S(1)} %get-tuple-element.107.refs_0_, f32[128,1024]{1,0:T(8,128)S(1)} %get-tuple-element.108.refs_1_, f32[64,1024]{1,0:T(8,128)S(1)} %get-tuple-element.109.refs_2_, ...), custom_call_target="tpu_custom_call" | custom-call | flops 1 | bytes 1 | tf_op jit(solution)/shard_map/finish_hidden/pallas_call | solution.py:354
  (66 shorter events, 7.0 us)
Async XLA Ops:
  7.5 5.2 %collective-permute-start = (bf16[2,8192]{1,0:T(2,128)(2,1)}, bf16[2,8192]{1,0:T(2,128)(2,1)S(1)}, u32[]{:S(2)}, u32[]{:S(2)}) collective-permute-start(bf16[2,8192]{1,0:T(2,128)(2,1)} %get-tuple-element.59), channel_id=1, source_target_pairs={{0,4},{1,5},{2,6},{3,7},{4,0},{5,1},{6,2},{7,3},{8,12},{9,13},{10,... | collective-permute-start | bytes 98312 | tf_op jit(solution)/shard_map/ppermute | solution.py:422
  13.5 6.7 %collective-permute-start.5 = (bf16[4,8192]{1,0:T(4,128)(2,1)S(1)}, bf16[4,8192]{1,0:T(4,128)(2,1)S(1)}, u32[]{:S(2)}, u32[]{:S(2)}) collective-permute-start(bf16[4,8192]{1,0:T(4,128)(2,1)S(1)} %pad_maximum_fusion.2), channel_id=1, source_target_pairs={{0,8},{1,9},{2,10},{3,11},{4,12},{5,13},{6,14},{7,15},{8,0},{9,1},... | collective-permute-start | bytes 196616 | tf_op jit(solution)/shard_map/ppermute | solution.py:422
  16.6 5.2 %collective-permute-start.4 = (bf16[64,1024]{1,0:T(8,128)(2,1)}, bf16[64,1024]{1,0:T(8,128)(2,1)S(1)}, u32[]{:S(2)}, u32[]{:S(2)}) collective-permute-start(bf16[64,1024]{1,0:T(8,128)(2,1)} %get-tuple-element.64), channel_id=1, source_target_pairs={{0,16},{16,0},{1,17},{17,1},{2,18},{18,2},{3,19},{19,3},{4,20},{20... | collective-permute-start | bytes 393224 | tf_op jit(solution)/shard_map/ppermute | solution.py:423
  18.1 15.0 %collective-permute-start.1 = (bf16[32,8192]{1,0:T(8,128)(2,1)}, bf16[32,8192]{1,0:T(8,128)(2,1)S(1)}, u32[]{:S(2)}, u32[]{:S(2)}) collective-permute-start(bf16[32,8192]{1,0:T(8,128)(2,1)} %get-tuple-element.60.refs_0_), channel_id=1, source_target_pairs={{0,4},{1,5},{4,8},{5,9},{8,12},{9,13},{12,14},{13,15},{14,10},{15,... | collective-permute-start | bytes 1572872 | tf_op jit(solution)/shard_map/ppermute | solution.py:418
  19.7 13.4 %collective-permute-start.2 = (bf16[32,8192]{1,0:T(8,128)(2,1)}, bf16[32,8192]{1,0:T(8,128)(2,1)S(1)}, u32[]{:S(2)}, u32[]{:S(2)}) collective-permute-start(bf16[32,8192]{1,0:T(8,128)(2,1)} %get-tuple-element.60.refs_0_), channel_id=1, source_target_pairs={{4,0},{5,1},{8,4},{9,5},{12,8},{13,9},{14,12},{15,13},{10,14},{11,... | collective-permute-start | bytes 1572872 | tf_op jit(solution)/shard_map/ppermute | solution.py:419
  20.1 13.0 %collective-permute-start.3 = (bf16[32,8192]{1,0:T(8,128)(2,1)}, bf16[32,8192]{1,0:T(8,128)(2,1)S(1)}, u32[]{:S(2)}, u32[]{:S(2)}) collective-permute-start(bf16[32,8192]{1,0:T(8,128)(2,1)} %get-tuple-element.60.refs_0_), channel_id=1, source_target_pairs={{0,1},{1,0},{2,3},{3,2},{4,5},{5,4},{6,7},{7,6},{8,9},{9,8},{10,11... | collective-permute-start | bytes 1572872 | tf_op jit(solution)/shard_map/ppermute | solution.py:420
  21.8 11.3 %collective-permute-start.6 = (bf16[8,8192]{1,0:T(8,128)(2,1)S(1)}, bf16[8,8192]{1,0:T(8,128)(2,1)S(1)}, u32[]{:S(2)}, u32[]{:S(2)}) collective-permute-start(bf16[8,8192]{1,0:T(8,128)(2,1)S(1)} %pad_maximum_fusion.1), channel_id=1, source_target_pairs={{0,2},{1,3},{2,0},{3,1},{4,6},{5,7},{6,4},{7,5},{8,10},{9,11},{10,... | collective-permute-start | bytes 393224 | tf_op jit(solution)/shard_map/ppermute | solution.py:421
  33.1 4.1 %collective-permute-start.10 = (bf16[32,8192]{1,0:T(8,128)(2,1)S(1)}, bf16[32,8192]{1,0:T(8,128)(2,1)S(1)}, u32[]{:S(2)}, u32[]{:S(2)}) collective-permute-start(bf16[32,8192]{1,0:T(8,128)(2,1)S(1)} %collective-permute-done.2.refs_4_), channel_id=1, source_target_pairs={{0,1},{1,0},{2,3},{3,2},{4,5},{5,4},{6,7},{7,6},{8,9},{9,8},{10,11... | collective-permute-start | bytes 1572872 | tf_op jit(solution)/shard_map/ppermute | solution.py:420
  33.2 4.1 %collective-permute-start.9 = (bf16[32,8192]{1,0:T(8,128)(2,1)S(1)}, bf16[32,8192]{1,0:T(8,128)(2,1)S(1)}, u32[]{:S(2)}, u32[]{:S(2)}) collective-permute-start(bf16[32,8192]{1,0:T(8,128)(2,1)S(1)} %collective-permute-done.1.refs_2_), channel_id=1, source_target_pairs={{0,1},{1,0},{2,3},{3,2},{4,5},{5,4},{6,7},{7,6},{8,9},{9,8},{10,11... | collective-permute-start | bytes 1572872 | tf_op jit(solution)/shard_map/ppermute | solution.py:420
  33.7 16.5 %collective-permute-start.7 = (bf16[32,8192]{1,0:T(8,128)(2,1)S(1)}, bf16[32,8192]{1,0:T(8,128)(2,1)S(1)}, u32[]{:S(2)}, u32[]{:S(2)}) collective-permute-start(bf16[32,8192]{1,0:T(8,128)(2,1)S(1)} %collective-permute-done.1.refs_2_), channel_id=1, source_target_pairs={{0,4},{1,5},{4,8},{5,9},{8,12},{9,13},{12,14},{13,15},{14,10},{15,... | collective-permute-start | bytes 1572872 | tf_op jit(solution)/shard_map/ppermute | solution.py:418
  34.9 15.3 %collective-permute-start.8 = (bf16[32,8192]{1,0:T(8,128)(2,1)S(1)}, bf16[32,8192]{1,0:T(8,128)(2,1)S(1)}, u32[]{:S(2)}, u32[]{:S(2)}) collective-permute-start(bf16[32,8192]{1,0:T(8,128)(2,1)S(1)} %collective-permute-done.2.refs_4_), channel_id=1, source_target_pairs={{4,0},{5,1},{8,4},{9,5},{12,8},{13,9},{14,12},{15,13},{10,14},{11,... | collective-permute-start | bytes 1572872 | tf_op jit(solution)/shard_map/ppermute | solution.py:419
  35.7 1.5 %collective-permute-start.11 = (bf16[16,8192]{1,0:T(8,128)(2,1)S(1)}, bf16[16,8192]{1,0:T(8,128)(2,1)S(1)}, u32[]{:S(2)}, u32[]{:S(2)}) collective-permute-start(bf16[16,8192]{1,0:T(8,128)(2,1)S(1)} %pad_maximum_fusion.refs_6_), channel_id=1, source_target_pairs={{0,1},{1,0},{2,3},{3,2},{4,5},{5,4},{6,7},{7,6},{8,9},{9,8},{10,11... | collective-permute-start | bytes 786440 | tf_op jit(solution)/shard_map/ppermute | solution.py:420
  41.3 9.0 %collective-permute-start.12 = (f32[32,1024]{1,0:T(8,128)S(1)}, f32[32,1024]{1,0:T(8,128)S(1)}, u32[]{:S(2)}, u32[]{:S(2)}) collective-permute-start(f32[32,1024]{1,0:T(8,128)S(1)} %get-tuple-element.74.refs_5_), channel_id=1, source_target_pairs={{0,16},{16,0},{1,17},{17,1},{2,18},{18,2},{3,19},{19,3},{4,20},{20... | collective-permute-start | bytes 393224 | tf_op jit(solution)/shard_map/ppermute | solution.py:423
  50.2 40.9 %copy-start.3 = (f32[8192]{0:T(1024)S(1)}, f32[8192]{0:T(1024)}, u32[]{:S(2)}) copy-start(f32[8192]{0:T(1024)} %param.26) | copy-start | bytes 98308
  50.3 2.6 %collective-permute-start.15 = (bf16[32,8192]{1,0:T(8,128)(2,1)S(1)}, bf16[32,8192]{1,0:T(8,128)(2,1)S(1)}, u32[]{:S(2)}, u32[]{:S(2)}) collective-permute-start(bf16[32,8192]{1,0:T(8,128)(2,1)S(1)} %collective-permute-done.7.refs_0_), channel_id=1, source_target_pairs={{0,1},{1,0},{2,3},{3,2},{4,5},{5,4},{6,7},{7,6},{8,9},{9,8},{10,11... | collective-permute-start | bytes 1572872 | tf_op jit(solution)/shard_map/ppermute | solution.py:420
  50.3 2.6 %collective-permute-start.16 = (bf16[32,8192]{1,0:T(8,128)(2,1)S(1)}, bf16[32,8192]{1,0:T(8,128)(2,1)S(1)}, u32[]{:S(2)}, u32[]{:S(2)}) collective-permute-start(bf16[32,8192]{1,0:T(8,128)(2,1)S(1)} %collective-permute-done.8.refs_2_), channel_id=1, source_target_pairs={{0,1},{1,0},{2,3},{3,2},{4,5},{5,4},{6,7},{7,6},{8,9},{9,8},{10,11... | collective-permute-start | bytes 1572872 | tf_op jit(solution)/shard_map/ppermute | solution.py:420
  50.8 13.9 %collective-permute-start.13 = (bf16[32,8192]{1,0:T(8,128)(2,1)S(1)}, bf16[32,8192]{1,0:T(8,128)(2,1)S(1)}, u32[]{:S(2)}, u32[]{:S(2)}) collective-permute-start(bf16[32,8192]{1,0:T(8,128)(2,1)S(1)} %collective-permute-done.7.refs_0_), channel_id=1, source_target_pairs={{0,4},{1,5},{4,8},{5,9},{8,12},{9,13},{12,14},{13,15},{14,10},{15,... | collective-permute-start | bytes 1572872 | tf_op jit(solution)/shard_map/ppermute | solution.py:418
  52.4 13.6 %collective-permute-start.14 = (bf16[32,8192]{1,0:T(8,128)(2,1)S(1)}, bf16[32,8192]{1,0:T(8,128)(2,1)S(1)}, u32[]{:S(2)}, u32[]{:S(2)}) collective-permute-start(bf16[32,8192]{1,0:T(8,128)(2,1)S(1)} %collective-permute-done.8.refs_2_), channel_id=1, source_target_pairs={{4,0},{5,1},{8,4},{9,5},{12,8},{13,9},{14,12},{15,13},{10,14},{11,... | collective-permute-start | bytes 1572872 | tf_op jit(solution)/shard_map/ppermute | solution.py:419
  61.6 1.6 %collective-permute-start.17 = (bf16[16,8192]{1,0:T(8,128)(2,1)S(1)}, bf16[16,8192]{1,0:T(8,128)(2,1)S(1)}, u32[]{:S(2)}, u32[]{:S(2)}) collective-permute-start(bf16[16,8192]{1,0:T(8,128)(2,1)S(1)} %get-tuple-element.81), channel_id=1, source_target_pairs={{0,1},{1,0},{2,3},{3,2},{4,5},{5,4},{6,7},{7,6},{8,9},{9,8},{10,11... | collective-permute-start | bytes 786440 | tf_op jit(solution)/shard_map/ppermute | solution.py:420
  66.0 3.1 %collective-permute-start.19 = (bf16[32,8192]{1,0:T(8,128)(2,1)S(1)}, bf16[32,8192]{1,0:T(8,128)(2,1)S(1)}, u32[]{:S(2)}, u32[]{:S(2)}) collective-permute-start(bf16[32,8192]{1,0:T(8,128)(2,1)S(1)} %collective-permute-done.13.refs_0_), channel_id=1, source_target_pairs={{0,1},{1,0},{2,3},{3,2},{4,5},{5,4},{6,7},{7,6},{8,9},{9,8},{10,11... | collective-permute-start | bytes 1572872 | tf_op jit(solution)/shard_map/ppermute | solution.py:420
  66.0 3.1 %collective-permute-start.20 = (bf16[32,8192]{1,0:T(8,128)(2,1)S(1)}, bf16[32,8192]{1,0:T(8,128)(2,1)S(1)}, u32[]{:S(2)}, u32[]{:S(2)}) collective-permute-start(bf16[32,8192]{1,0:T(8,128)(2,1)S(1)} %collective-permute-done.14.refs_2_), channel_id=1, source_target_pairs={{0,1},{1,0},{2,3},{3,2},{4,5},{5,4},{6,7},{7,6},{8,9},{9,8},{10,11... | collective-permute-start | bytes 1572872 | tf_op jit(solution)/shard_map/ppermute | solution.py:420
  66.6 11.1 %collective-permute-start.21 = (bf16[16,8192]{1,0:T(8,128)(2,1)S(1)}, bf16[16,8192]{1,0:T(8,128)(2,1)S(1)}, u32[]{:S(2)}, u32[]{:S(2)}) collective-permute-start(bf16[16,8192]{1,0:T(8,128)(2,1)S(1)} %slice.22), channel_id=1, source_target_pairs={{0,4},{1,5},{4,8},{5,9},{8,12},{9,13},{12,14},{13,15},{14,10},{15,... | collective-permute-start | bytes 786440 | tf_op jit(solution)/shard_map/ppermute | solution.py:418
  66.9 10.8 %collective-permute-start.22 = (bf16[16,8192]{1,0:T(8,128)(2,1)S(1)}, bf16[16,8192]{1,0:T(8,128)(2,1)S(1)}, u32[]{:S(2)}, u32[]{:S(2)}) collective-permute-start(bf16[16,8192]{1,0:T(8,128)(2,1)S(1)} %slice.23), channel_id=1, source_target_pairs={{4,0},{5,1},{8,4},{9,5},{12,8},{13,9},{14,12},{15,13},{10,14},{11,... | collective-permute-start | bytes 786440 | tf_op jit(solution)/shard_map/ppermute | solution.py:419
  68.7 9.0 %collective-permute-start.18 = (bf16[8,8192]{1,0:T(8,128)(2,1)S(1)}, bf16[8,8192]{1,0:T(8,128)(2,1)S(1)}, u32[]{:S(2)}, u32[]{:S(2)}) collective-permute-start(bf16[8,8192]{1,0:T(8,128)(2,1)S(1)} %get-tuple-element.86), channel_id=1, source_target_pairs={{0,2},{1,3},{2,0},{3,1},{4,6},{5,7},{6,4},{7,5},{8,10},{9,11},{10,... | collective-permute-start | bytes 393224 | tf_op jit(solution)/shard_map/ppermute | solution.py:421
  71.5 14.8 %collective-permute-start.25 = (bf16[192,1024]{1,0:T(8,128)(2,1)S(1)}, bf16[192,1024]{1,0:T(8,128)(2,1)S(1)}, u32[]{:S(2)}, u32[]{:S(2)}) collective-permute-start(bf16[192,1024]{1,0:T(8,128)(2,1)S(1)} %get-tuple-element.100), channel_id=1, source_target_pairs={{0,16},{16,0},{1,17},{17,1},{2,18},{18,2},{3,19},{19,3},{4,20},{20... | collective-permute-start | bytes 1179656 | tf_op jit(solution)/shard_map/ppermute | solution.py:423
  77.8 2.8 %collective-permute-start.23 = (bf16[16,8192]{1,0:T(8,128)(2,1)S(1)}, bf16[16,8192]{1,0:T(8,128)(2,1)S(1)}, u32[]{:S(2)}, u32[]{:S(2)}) collective-permute-start(bf16[16,8192]{1,0:T(8,128)(2,1)S(1)} %collective-permute-done.21.refs_0_.refs_4_), channel_id=1, source_target_pairs={{0,1},{1,0},{2,3},{3,2},{4,5},{5,4},{6,7},{7,6},{8,9},{9,8},{10,11... | collective-permute-start | bytes 786440 | tf_op jit(solution)/shard_map/ppermute | solution.py:420
  77.8 4.9 %collective-permute-start.24 = (bf16[16,8192]{1,0:T(8,128)(2,1)S(1)}, bf16[16,8192]{1,0:T(8,128)(2,1)S(1)}, u32[]{:S(2)}, u32[]{:S(2)}) collective-permute-start(bf16[16,8192]{1,0:T(8,128)(2,1)S(1)} %collective-permute-done.22.refs_1_.refs_5_), channel_id=1, source_target_pairs={{0,1},{1,0},{2,3},{3,2},{4,5},{5,4},{6,7},{7,6},{8,9},{9,8},{10,11... | collective-permute-start | bytes 786440 | tf_op jit(solution)/shard_map/ppermute | solution.py:420
  78.3 7.3 %collective-permute-start.26 = (bf16[2,8192]{1,0:T(2,128)(2,1)S(1)}, bf16[2,8192]{1,0:T(2,128)(2,1)S(1)}, u32[]{:S(2)}, u32[]{:S(2)}) collective-permute-start(bf16[2,8192]{1,0:T(2,128)(2,1)S(1)} %get-tuple-element.101), channel_id=1, source_target_pairs={{0,4},{1,5},{2,6},{3,7},{4,0},{5,1},{6,2},{7,3},{8,12},{9,13},{10,... | collective-permute-start | bytes 98312 | tf_op jit(solution)/shard_map/ppermute | solution.py:422
  78.3 7.3 %collective-permute-start.27 = (bf16[2,8192]{1,0:T(2,128)(2,1)S(1)}, bf16[2,8192]{1,0:T(2,128)(2,1)S(1)}, u32[]{:S(2)}, u32[]{:S(2)}) collective-permute-start(bf16[2,8192]{1,0:T(2,128)(2,1)S(1)} %get-tuple-element.102), channel_id=1, source_target_pairs={{0,8},{1,9},{2,10},{3,11},{4,12},{5,13},{6,14},{7,15},{8,0},{9,1},... | collective-permute-start | bytes 98312 | tf_op jit(solution)/shard_map/ppermute | solution.py:422
  80.6 5.7 %collective-permute-start.28 = (bf16[2,8192]{1,0:T(2,128)(2,1)S(1)}, bf16[2,8192]{1,0:T(2,128)(2,1)S(1)}, u32[]{:S(2)}, u32[]{:S(2)}) collective-permute-start(bf16[2,8192]{1,0:T(2,128)(2,1)S(1)} %get-tuple-element.103), channel_id=1, source_target_pairs={{0,12},{1,13},{2,14},{3,15},{4,8},{5,9},{6,10},{7,11},{8,4},{9,5},... | collective-permute-start | bytes 98312 | tf_op jit(solution)/shard_map/ppermute | solution.py:422
  85.1 5.0 %collective-permute-start.30 = (bf16[64,1024]{1,0:T(8,128)(2,1)S(1)}, bf16[64,1024]{1,0:T(8,128)(2,1)S(1)}, u32[]{:S(2)}, u32[]{:S(2)}) collective-permute-start(bf16[64,1024]{1,0:T(8,128)(2,1)S(1)} %get-tuple-element.111), channel_id=1, source_target_pairs={{0,16},{16,0},{1,17},{17,1},{2,18},{18,2},{3,19},{19,3},{4,20},{20... | collective-permute-start | bytes 393224 | tf_op jit(solution)/shard_map/ppermute | solution.py:423
  86.5 4.6 %collective-permute-start.29 = (f32[2,1]{0,1:T(1,128)S(1)}, f32[2,1]{0,1:T(1,128)S(1)}, u32[]{:S(2)}, u32[]{:S(2)}) collective-permute-start(f32[2,1]{0,1:T(1,128)S(1)} %bitcast.17), channel_id=1, source_target_pairs={{0,16},{16,0},{1,17},{17,1},{2,18},{18,2},{3,19},{19,3},{4,20},{20... | collective-permute-start | bytes 32 | tf_op jit(solution)/shard_map/ppermute | solution.py:423
  (7 other events, 142.2 us)
